TPU v7x, 256 devices: a whole 4x4x8 slice. The times are simulated.
256 devices in a mesh: dom: 2 (over core), gx: 16 (over x, y), gy: 8 (over z).
Axes of the slice: x: 4, y: 4, z: 8, core: 2. Of those that a mesh axis runs over, the one named last changes fastest.
Arguments:
- fields: float32 [2, 4, 8, 2048, 1024], P('dom', None, None, 'gx', 'gy'), may hold values from -6 to 6
- turbine_mask: int32 [8, 2048, 1024], P(None, 'gx', 'gy'), may hold values 0 or 1
- inflow_source: int32 [1024], P('gy'), may hold values from 0 to 1023
- inflow_weight: int32 [1024], P('gy'), may hold values from 0 to 16
Outputs:
- fields_next: float32 [2, 4, 8, 2048, 1024], P('dom', None, None, 'gx', 'gy')
- inflow: float32 [32, 1024], P(('dom', 'gx'), 'gy')
All inputs are finite; a program needn't handle non-finite values. No bound on the sum of `turbine_mask` on one device may be relied on, other than what follows from the above.
Results may differ from a plain program's by a relative error of at most 0.00016.
Values sent between devices are 32-bit elements; how exact they have to be, the bound alone decides.
No kernel may reach another device: no remote copies, remote signals or barrier semaphores. Data moves between devices by JAX's collectives and lax.ppermute only.
A program may use at most 192 MiB of HBM per device.

v0:
```python
import jax
import jax.numpy as jnp
from jax import lax
from jax.sharding import PartitionSpec as P

NX = 2048
NY = 1024
LEVELS = 4
CYCLES = 2
COARSE = 2


time_step = 0.2
mean_wind = 1.0
viscosity = 0.05
vertical_mix = 0.1
thrust = 1.0
damping = 0.8
highest = lax.Precision.HIGHEST
row_block = 512


def partner_2(array, axis, apart):
    return lax.ppermute(array, axis, [(i, i ^ 1 << apart) for i in range(lax.axis_size(axis))])


def in_order(blocks, dim):
    lengths = list(blocks.shape[1:])
    lengths[dim] *= blocks.shape[0]
    return jnp.moveaxis(blocks, 0, dim).reshape(lengths)


def from_everyone(array, axis):
    copies = jnp.broadcast_to(array, (lax.axis_size(axis), *array.shape))
    return lax.all_to_all(copies, axis, split_axis=0, concat_axis=0, tiled=True)


def gathered_copies(array, axis, dim):
    return in_order(from_everyone(array, axis), dim)


def from_root(array, axis, root):
    return lax.dynamic_index_in_dim(lax.all_gather(array, axis), root, 0, keepdims=False)


def extended(array, sides, width):
    edges = {}
    for axis, dim in sides:
        size, length = (lax.axis_size(axis), array.shape[dim])
        up = [(i, (i + 1) % size) for i in range(size)]
        last = lax.slice_in_dim(array, length - width, length, axis=dim)
        first = lax.slice_in_dim(array, 0, width, axis=dim)
        edges[dim] = (
            lax.ppermute(last, axis, up),
            lax.ppermute(first, axis, [(b, a) for a, b in up]),
        )
    done = []
    for _, dim in sides:
        low, high = edges[dim]
        around = [(width, width) if d in done else (0, 0) for d in range(array.ndim)]
        array = jnp.concatenate([jnp.pad(low, around), array, jnp.pad(high, around)], axis=dim)
        done.append(dim)
    return array


def natural_order(position):
    return position


def derivative_rows(first_row, block_rows, length, order):
    row_index = order(first_row + lax.broadcasted_iota(jnp.int32, (block_rows, length), 0))
    col_index = order(lax.broadcasted_iota(jnp.int32, (block_rows, length), 1))
    offset = row_index - col_index
    half_angle = jnp.pi / length * offset.astype(jnp.float32)
    parity = jnp.where(offset % 2 == 0, 1.0, -1.0)
    spacing = 2.0 * jnp.pi / length
    sine_value = jnp.where(offset == 0, 1.0, jnp.sin(half_angle))
    slope_rows = jnp.where(
        offset == 0, 0.0, 0.5 * spacing * parity * jnp.cos(half_angle) / sine_value
    )
    bend_rows = jnp.where(
        offset == 0,
        -jnp.pi**2 / 3.0 - spacing * spacing / 6.0,
        -0.5 * spacing * spacing * parity / (sine_value * sine_value),
    )
    return jnp.stack([slope_rows, bend_rows])


def apply_table(operand, length, form, out_shape, out_axis, order):
    block_rows = min(row_block, length)

    def add_block(block_index, gathered):
        first_row = block_index * block_rows
        table_rows = derivative_rows(first_row, block_rows, length, order)
        product = jnp.einsum(form, table_rows, operand, precision=highest)
        return lax.dynamic_update_slice_in_dim(gathered, product, first_row, out_axis)

    return lax.fori_loop(0, length // block_rows, add_block, jnp.zeros(out_shape, jnp.float32))


def line_terms(operand, order):
    shape_out = (operand.shape[0], 2, NX, operand.shape[2])
    return apply_table(operand, NX, "sax,rxk->rsak", shape_out, 2, order)


def span_terms(operand):
    shape_out = (operand.shape[0], operand.shape[1], 2, NY)
    return apply_table(operand, NY, "say,rky->rksa", shape_out, 3, natural_order)


def line_parts(current, back_x, back_y):
    slope_x = back_x[:, 0].reshape(current.shape)
    bend_x = back_x[:, 1].reshape(current.shape)
    slope_y = back_y[:, :, 0].reshape(current.shape)
    bend_y = back_y[:, :, 1].reshape(current.shape)
    part_x = -(mean_wind + current[0]) * slope_x + viscosity * bend_x
    part_y = -current[1] * slope_y + viscosity * bend_y
    return (part_x, part_y)


def vertical(values):
    upper_cells = jnp.concatenate([values[..., 1:, :, :], values[..., -1:, :, :]], axis=-3)
    lower_cells = jnp.concatenate([values[..., :1, :, :], values[..., :-1, :, :]], axis=-3)
    return (upper_cells, lower_cells)


def face_cells(padded, west_edge, east_edge, first_x, last_x):
    west_cells = padded[..., :-2, 1:-1]
    east_cells = padded[..., 2:, 1:-1]
    west_cells = west_cells.at[..., 0, :].set(jnp.where(first_x, west_edge, west_cells[..., 0, :]))
    east_cells = east_cells.at[..., -1, :].set(jnp.where(last_x, east_edge, east_cells[..., -1, :]))
    return (east_cells, west_cells, padded[..., 1:-1, 2:], padded[..., 1:-1, :-2])


def mend_rims(padded, lower_half):
    inner_last = padded.shape[1] - 2
    payload = jnp.where(
        lower_half,
        jnp.stack([padded[:, inner_last], padded[:, inner_last + 1]]),
        jnp.stack([padded[:, 0], padded[:, 1]]),
    )
    partner = partner_2(payload, "dom", 0)
    padded = padded.at[:, 0].set(partner[0])
    return padded.at[:, inner_last + 1].set(partner[1])


def operate(pressure, grid_level, cells):
    east_cells, west_cells, north_cells, south_cells = cells
    upper_cells, lower_cells = vertical(pressure)
    factor = 0.25**grid_level
    return (
        factor * (2.0 * pressure - east_cells - west_cells)
        + factor * (2.0 * pressure - north_cells - south_cells)
        + (2.0 * pressure - upper_cells - lower_cells)
    )


def restrict(residual):
    depth, rows_count, cols_count = residual.shape
    return residual.reshape(depth, rows_count // 2, 2, cols_count // 2, 2).mean(axis=(2, 4))


def prolong(correction):
    return jnp.repeat(jnp.repeat(correction, 2, axis=1), 2, axis=2)


def interpolate(inlet_plane, source_rows, weight_rows):
    length = inlet_plane.shape[2]
    row_index = lax.broadcasted_iota(jnp.int32, (length, source_rows.shape[0]), 0)
    share_first = weight_rows.astype(jnp.float32)[None, :] / 16.0
    follow = (source_rows + 1) % length
    blend_table = jnp.where(row_index == source_rows[None, :], share_first, 0.0) + jnp.where(
        row_index == follow[None, :], 1.0 - share_first, 0.0
    )
    stacked = inlet_plane.reshape(inlet_plane.shape[0] * inlet_plane.shape[1], length)
    blended = jnp.dot(stacked, blend_table, precision=highest, preferred_element_type=jnp.float32)
    return blended.reshape(inlet_plane.shape[0], inlet_plane.shape[1], source_rows.shape[0])


def on_device(fields, turbine_mask, inflow_source, inflow_weight):
    own = fields[0]
    level_count = own.shape[1]
    width_x = own.shape[2]
    width_y = own.shape[3]
    domain_index = lax.axis_index("dom")
    is_precursor = domain_index == 0
    grid_index = lax.axis_index("gx")
    grid_count = lax.axis_size("gx")
    owner_index = NX // 2 // width_x
    column = own[:, :, NX // 2 % width_x, :]
    whole_plane = gathered_copies(column, "gy", 2)
    inlet_plane = from_root(whole_plane, ("dom", "gx"), owner_index)
    inflow = interpolate(inlet_plane, inflow_source, inflow_weight)
    folded_pair = lax.all_to_all(fields, "dom", split_axis=3, concat_axis=0, tiled=True)
    precursor = folded_pair[0]
    farm = folded_pair[1]
    half_width = width_x // 2
    mask_cells = lax.dynamic_slice_in_dim(turbine_mask, domain_index * half_width, half_width, 1)
    first_x = (grid_index == 0) & is_precursor
    last_x = (grid_index == grid_count - 1) & (domain_index == 1)

    def joint_order(position):
        piece_index = position // half_width
        return (
            piece_index % grid_count * width_x
            + piece_index // grid_count * half_width
            + position % half_width
        )

    stacked = precursor.reshape(4 * level_count, half_width, width_y)
    spread_x = line_terms(
        lax.all_to_all(stacked, ("dom", "gx"), split_axis=0, concat_axis=1, tiled=True), joint_order
    )
    back_x = lax.all_to_all(spread_x, ("dom", "gx"), split_axis=2, concat_axis=0, tiled=True)
    spread_y = span_terms(lax.all_to_all(stacked, "gy", split_axis=0, concat_axis=2, tiled=True))
    back_y = lax.all_to_all(spread_y, "gy", split_axis=3, concat_axis=0, tiled=True)
    part_x, part_y = line_parts(precursor, back_x, back_y)
    upper_prec, lower_prec = vertical(precursor)
    part_z = -precursor[2] * (upper_prec - lower_prec) * 0.5 + vertical_mix * (
        upper_prec + lower_prec - 2.0 * precursor
    )
    precursor_next = precursor + time_step * (part_x + part_y + part_z)

    def grid_faces(values):
        padded_grid = extended(values, (("gx", 1), ("gy", 2)), 1)
        padded_grid = mend_rims(padded_grid, is_precursor)
        return padded_grid

    farm_width = farm.shape[2]
    upper_cells, lower_cells = vertical(farm)
    padded = grid_faces(farm.reshape(4 * level_count, farm_width, width_y)).reshape(
        4, level_count, farm_width + 2, width_y + 2
    )
    east_cells, west_cells, north_cells, south_cells = face_cells(
        padded, inflow, farm[..., -1, :], first_x, last_x
    )
    moving = (
        -(mean_wind + farm[0]) * (east_cells - west_cells) * 0.5
        - farm[1] * (north_cells - south_cells) * 0.5
        - farm[2] * (upper_cells - lower_cells) * 0.5
    )
    mixing = viscosity * (
        east_cells + west_cells + north_cells + south_cells - 4.0 * farm
    ) + vertical_mix * (upper_cells + lower_cells - 2.0 * farm)
    flags = jnp.array([1.0, 1.0, 1.0, 0.0], jnp.float32).reshape(4, 1, 1, 1)
    drag = thrust * mask_cells.astype(jnp.float32) * jnp.abs(farm[0])
    star = farm + time_step * (moving + mixing - drag * farm * flags)
    horizontal = star[:2]
    star_padded = grid_faces(horizontal.reshape(2 * level_count, farm_width, width_y)).reshape(
        2, level_count, farm_width + 2, width_y + 2
    )
    star_east, star_west, star_north, star_south = face_cells(
        star_padded, inflow[:2], horizontal[..., -1, :], first_x, last_x
    )
    upward = star[2]
    zero_level = jnp.zeros_like(upward[:1])
    upward_above = jnp.concatenate([upward[1:], zero_level], axis=0)
    upward_below = jnp.concatenate([zero_level, upward[:-1]], axis=0)
    source = -(
        (star_east[0] - star_west[0]) * 0.5
        + (star_north[1] - star_south[1]) * 0.5
        + (upward_above - upward_below) * 0.5
    )

    def level_cells(pressure):
        padded_level = grid_faces(pressure)
        return face_cells(
            padded_level, pressure[..., 0, :], jnp.zeros_like(pressure[..., 0, :]), first_x, last_x
        )

    def jacobi_sweep(pressure, target, grid_level, from_zero):
        diagonal = 4.0 * 0.25**grid_level + 2.0
        if from_zero:
            return damping * target / diagonal
        return (
            pressure
            + damping * (target - operate(pressure, grid_level, level_cells(pressure))) / diagonal
        )

    def vcycle(grid_level, pressure, target, from_zero):
        if grid_level == LEVELS - 1:
            for sweep_index in range(COARSE):
                pressure = jacobi_sweep(
                    pressure, target, grid_level, from_zero and sweep_index == 0
                )
            return pressure
        pressure = jacobi_sweep(pressure, target, grid_level, from_zero)
        residual = target - operate(pressure, grid_level, level_cells(pressure))
        coarse_target = restrict(residual)
        correction = vcycle(grid_level + 1, jnp.zeros_like(coarse_target), coarse_target, True)
        pressure = pressure + prolong(correction)
        return jacobi_sweep(pressure, target, grid_level, False)

    pressure = jnp.zeros_like(source)
    for cycle_index in range(CYCLES):
        pressure = vcycle(0, pressure, source, cycle_index == 0)
    final_padded = grid_faces(pressure)
    east_pressure, west_pressure, north_pressure, south_pressure = face_cells(
        final_padded, pressure[..., 0, :], jnp.zeros_like(pressure[..., 0, :]), first_x, last_x
    )
    upper_pressure, lower_pressure = vertical(pressure)
    gradient = jnp.stack(
        [
            (east_pressure - west_pressure) * 0.5,
            (north_pressure - south_pressure) * 0.5,
            (upper_pressure - lower_pressure) * 0.5,
            jnp.zeros_like(pressure),
        ]
    )
    farm_next = star - gradient
    combined = lax.all_to_all(
        jnp.stack([precursor_next, farm_next]), "dom", split_axis=0, concat_axis=3, tiled=True
    )
    group_count = lax.axis_size("dom") * grid_count
    own_rows = 4 * level_count // group_count
    group_index = domain_index * grid_count + grid_index
    inflow_rows = lax.dynamic_slice_in_dim(
        inflow.reshape(4 * level_count, width_y), group_index * own_rows, own_rows, 0
    )
    return (combined, inflow_rows)


def solution(mesh):
    placed = (P("dom", None, None, "gx", "gy"), P(None, "gx", "gy"), P("gy"), P("gy"))
    return jax.shard_map(
        on_device,
        mesh=mesh,
        in_specs=placed,
        out_specs=(P("dom", None, None, "gx", "gy"), P(("dom", "gx"), "gy")),
        check_vma=False,
    )
```

profile of v0, /device:TPU:1, one launch (start us, length us, event | category | flops | bytes accessed | tf_op | source)
XLA Modules:
  0.0 601.7 jit_solution(15078208861300713219)
XLA Ops:
  7.2 4.1 copy.1004
  11.3 7.0 %all-to-all-start = ((f32[1,4,8,128,128]{4,2,1,0,3:T(8,128)}), f32[1,4,8,128,128]{4,2,1,0,3:T(8,128)S(1)}, u32[]{:S(2)}, u32[]{:S(2)}) async-start(f32[1,4,8,128,128]{4,2,1,0,3:T(8,128)} %copy.1004), calls=%async_computation | async-start | bytes 4194304 | tf_op jit(solution)/shard_map/all_to_all | solution.py:194
  21.4 6.4 %all-to-all-start.5 = ((f32[8,4,8,128]{3,2,1,0:T(8,128)}), f32[8,4,8,128]{3,2,1,0:T(8,128)S(1)}, u32[]{:S(2)}, u32[]{:S(2)}) async-start(f32[8,4,8,128]{3,2,1,0:T(8,128)} %broadcast_in_dim.125), calls=%async_computation.5 | async-start | bytes 262144 | tf_op jit(solution)/shard_map/all_to_all | solution.py:35
  35.8 9.2 %all-to-all-start.1 = ((f32[32,64,128]{2,1,0:T(8,128)}), f32[32,64,128]{2,1,0:T(8,128)S(1)}, u32[]{:S(2)}, u32[]{:S(2)}) async-start(f32[32,64,128]{2,1,0:T(8,128)} %bitcast.14), calls=%async_computation.1 | async-start | bytes 2097152 | tf_op jit(solution)/shard_map/all_to_all | solution.py:212
  45.9 15.7 %all-to-all-done.1 = f32[32,64,128]{2,1,0:T(8,128)S(1)} async-done(((f32[32,64,128]{2,1,0:T(8,128)}), f32[32,64,128]{2,1,0:T(8,128)S(1)}, u32[]{:S(2)}, u32[]{:S(2)}) %all-to-all-start.1) | async-done | bytes 1048608 | tf_op jit(solution)/shard_map/all_to_all | solution.py:212
  61.6 4.2 all-to-all-start.3
  67.5 108.6 %while.103 = (s32[]{:T(128)}, f32[1,2,2048,128]{3,1,0,2:T(2,128)}, f32[1,2048,128]{2,1,0:T(8,128)S(1)}, s32[]{:T(128)}, s32[]{:T(128)}, /*index=5*/s32[]{:T(128)}, s32[]{:T(128)}) while((s32[]{:T(128)}, f32[1,2,2048,128]{3,1,0,2:T(2,128)}, f32[1,2048,128]{2,1,0:T(8,128)S(1)}, s32[]{:T(128)}, s32[]{:T(128)}, /*index=5*/s32[]{:T(128)}, ...), condition=%wide.region_1.2_spmd, body=%wide.region_0.1_spmd.sunk | while | flops 3303058944 | bytes 19490956 | solution.py:98
  67.7 19.0 %fusion.318 = (f32[1,512,2048]{2,1,0:T(8,128)S(1)}, f32[1,512,2048]{2,1,0:T(8,128)S(1)}) fusion(s32[2048]{0:T(1024)S(1)} %get-tuple-element.1461, s32[2048]{0:T(1024)S(1)} %get-tuple-element.1462, pred[2048]{0:T(1024)(128)(4,1)S(1)} %get-tuple-element.1463, s32[2048]{0:T(1024)S(1)} %get-tuple-element.1464, s32[2048]{0:T(1024)S(1)} %get-tuple-element.1465, ...), kind=kLoop, calls=%fused_computation.27.clone.1 | loop fusion | flops 79691776 | bytes 8434688 | tf_op jit(solution)/shard_map/while/body/eval_jaxpr/jit(_where)/select_n | solution.py:78
  86.7 6.7 %fusion.319 = f32[1,2,512,128]{3,2,1,0:T(8,128)S(1)} fusion(f32[1,512,2048]{2,1,0:T(8,128)S(1)} %get-tuple-element.1473, f32[1,512,2048]{2,1,0:T(8,128)S(1)} %get-tuple-element.1474, f32[1,2048,128]{2,1,0:T(8,128)S(1)} %get-tuple-element.1517), kind=kOutput, calls=%fused_computation.52.clone.1 | convolution fusion | flops 3223322624 | bytes 9961472 | tf_op jit(solution)/shard_map/while/body/eval_jaxpr/sax,rxk->rsak/dot_general | solution.py:95
  94.7 19.0 %fusion.318 = (f32[1,512,2048]{2,1,0:T(8,128)S(1)}, f32[1,512,2048]{2,1,0:T(8,128)S(1)}) fusion(s32[2048]{0:T(1024)S(1)} %get-tuple-element.1461, s32[2048]{0:T(1024)S(1)} %get-tuple-element.1462, pred[2048]{0:T(1024)(128)(4,1)S(1)} %get-tuple-element.1463, s32[2048]{0:T(1024)S(1)} %get-tuple-element.1464, s32[2048]{0:T(1024)S(1)} %get-tuple-element.1465, ...), kind=kLoop, calls=%fused_computation.27.clone.1 | loop fusion | flops 79691776 | bytes 8434688 | tf_op jit(solution)/shard_map/while/body/eval_jaxpr/jit(_where)/select_n | solution.py:78
  113.7 6.7 %fusion.319 = f32[1,2,512,128]{3,2,1,0:T(8,128)S(1)} fusion(f32[1,512,2048]{2,1,0:T(8,128)S(1)} %get-tuple-element.1473, f32[1,512,2048]{2,1,0:T(8,128)S(1)} %get-tuple-element.1474, f32[1,2048,128]{2,1,0:T(8,128)S(1)} %get-tuple-element.1517), kind=kOutput, calls=%fused_computation.52.clone.1 | convolution fusion | flops 3223322624 | bytes 9961472 | tf_op jit(solution)/shard_map/while/body/eval_jaxpr/sax,rxk->rsak/dot_general | solution.py:95
  121.8 19.0 %fusion.318 = (f32[1,512,2048]{2,1,0:T(8,128)S(1)}, f32[1,512,2048]{2,1,0:T(8,128)S(1)}) fusion(s32[2048]{0:T(1024)S(1)} %get-tuple-element.1461, s32[2048]{0:T(1024)S(1)} %get-tuple-element.1462, pred[2048]{0:T(1024)(128)(4,1)S(1)} %get-tuple-element.1463, s32[2048]{0:T(1024)S(1)} %get-tuple-element.1464, s32[2048]{0:T(1024)S(1)} %get-tuple-element.1465, ...), kind=kLoop, calls=%fused_computation.27.clone.1 | loop fusion | flops 79691776 | bytes 8434688 | tf_op jit(solution)/shard_map/while/body/eval_jaxpr/jit(_where)/select_n | solution.py:78
  140.8 6.7 %fusion.319 = f32[1,2,512,128]{3,2,1,0:T(8,128)S(1)} fusion(f32[1,512,2048]{2,1,0:T(8,128)S(1)} %get-tuple-element.1473, f32[1,512,2048]{2,1,0:T(8,128)S(1)} %get-tuple-element.1474, f32[1,2048,128]{2,1,0:T(8,128)S(1)} %get-tuple-element.1517), kind=kOutput, calls=%fused_computation.52.clone.1 | convolution fusion | flops 3223322624 | bytes 9961472 | tf_op jit(solution)/shard_map/while/body/eval_jaxpr/sax,rxk->rsak/dot_general | solution.py:95
  148.7 19.0 %fusion.318 = (f32[1,512,2048]{2,1,0:T(8,128)S(1)}, f32[1,512,2048]{2,1,0:T(8,128)S(1)}) fusion(s32[2048]{0:T(1024)S(1)} %get-tuple-element.1461, s32[2048]{0:T(1024)S(1)} %get-tuple-element.1462, pred[2048]{0:T(1024)(128)(4,1)S(1)} %get-tuple-element.1463, s32[2048]{0:T(1024)S(1)} %get-tuple-element.1464, s32[2048]{0:T(1024)S(1)} %get-tuple-element.1465, ...), kind=kLoop, calls=%fused_computation.27.clone.1 | loop fusion | flops 79691776 | bytes 8434688 | tf_op jit(solution)/shard_map/while/body/eval_jaxpr/jit(_where)/select_n | solution.py:78
  167.8 6.7 %fusion.319 = f32[1,2,512,128]{3,2,1,0:T(8,128)S(1)} fusion(f32[1,512,2048]{2,1,0:T(8,128)S(1)} %get-tuple-element.1473, f32[1,512,2048]{2,1,0:T(8,128)S(1)} %get-tuple-element.1474, f32[1,2048,128]{2,1,0:T(8,128)S(1)} %get-tuple-element.1517), kind=kOutput, calls=%fused_computation.52.clone.1 | convolution fusion | flops 3223322624 | bytes 9961472 | tf_op jit(solution)/shard_map/while/body/eval_jaxpr/sax,rxk->rsak/dot_general | solution.py:95
  176.1 5.6 all-to-all-start.2
  184.7 28.4 %while.104 = (s32[]{:T(128)}, f32[4,64,2,1024]{3,1,0,2:T(8,128)}, f32[4,64,1024]{2,1,0:T(8,128)S(1)}, s32[]{:T(128)}, s32[]{:T(128)}, /*index=5*/s32[]{:T(128)}, s32[]{:T(128)}) while((s32[]{:T(128)}, f32[4,64,2,1024]{3,1,0,2:T(8,128)}, f32[4,64,1024]{2,1,0:T(8,128)S(1)}, s32[]{:T(128)}, s32[]{:T(128)}, /*index=5*/s32[]{:T(128)}, ...), condition=%wide.region_3.4_spmd, body=%wide.region_2.3_spmd.sunk | while | flops 3235906048 | bytes 10489987 | solution.py:98
  184.7 9.3 %fusion.321 = (f32[1,512,1024]{2,1,0:T(8,128)S(1)}, f32[1,512,1024]{2,1,0:T(8,128)S(1)}) fusion(s32[512]{0:T(512)S(1)} %iota_add_fusion.3), kind=kLoop, calls=%fused_computation.88.clone.1 | loop fusion | flops 13631488 | bytes 4196352 | tf_op jit(solution)/shard_map/while/body/eval_jaxpr/jit(_where)/select_n | solution.py:78
  193.9 4.9 fusion.322
  198.8 9.3 %fusion.321 = (f32[1,512,1024]{2,1,0:T(8,128)S(1)}, f32[1,512,1024]{2,1,0:T(8,128)S(1)}) fusion(s32[512]{0:T(512)S(1)} %iota_add_fusion.3), kind=kLoop, calls=%fused_computation.88.clone.1 | loop fusion | flops 13631488 | bytes 4196352 | tf_op jit(solution)/shard_map/while/body/eval_jaxpr/jit(_where)/select_n | solution.py:78
  208.1 4.9 fusion.322
  213.1 4.8 copy.1010
  217.9 7.8 %reshape.3353 = f32[8,1,65536]{2,1,0:T(1,128)} reshape(f32[1024,2,4,64]{3,2,1,0:T(4,128)} %bitcast.445) | data formatting | bytes 4194304
  225.8 6.8 %all-to-all-start.4 = ((f32[8,1,65536]{2,1,0:T(1,128)}), f32[8,1,65536]{2,1,0:T(1,128)}, u32[]{:S(2)}, u32[]{:S(2)}) async-start(f32[8,1,65536]{2,1,0:T(1,128)} %reshape.3353), calls=%async_computation.4 | async-start | bytes 4194304 | tf_op jit(solution)/shard_map/all_to_all | solution.py:216
  256.7 17.6 %collective-permute-done = f32[32,64,1]{1,0,2:T(8,128)} collective-permute-done((f32[32,64,1]{1,0,2:T(8,128)}, f32[32,64,1]{1,0,2:T(8,128)}, u32[]{:S(2)}, u32[]{:S(2)}) %collective-permute-start) | collective-permute-done | bytes 8224 | tf_op jit(solution)/shard_map/ppermute | solution.py:54
  300.3 8.5 %reduce.144 = f32[8,65536]{1,0:T(8,128)} reduce(f32[8,1,65536]{2,1,0:T(1,128)} %all-to-all-done.4, f32[]{:T(128)} %broadcast.3502), dimensions={1}, to_apply=%all_to_all.88.reduce_sub_computation | reduce | bytes 4194308 | tf_op jit(solution)/shard_map/all_to_all | solution.py:216
  308.8 6.4 %reshape.3354 = f32[1024,2,4,64]{3,2,1,0:T(4,128)} reshape(f32[8,65536]{1,0:T(8,128)} %reduce.144) | data formatting | bytes 4194304
  315.2 4.8 copy.1117
  330.1 4.8 multiply_add_fusion
  335.3 4.5 collective-permute-start.8
  346.7 5.0 collective-permute-done.5
  371.9 5.6 reduce_sum.54
  391.9 5.1 collective-permute-start.22
  405.0 4.8 collective-permute-start.27
  417.8 4.8 collective-permute-start.32
  435.2 4.8 collective-permute-start.37
  448.2 5.1 collective-permute-start.42
  461.1 5.1 collective-permute-start.47
  474.5 5.1 collective-permute-start.52
  487.1 5.6 reduce_sum.57
  496.2 5.1 collective-permute-start.57
  507.1 5.2 collective-permute-start.62
  519.8 4.8 collective-permute-start.67
  532.5 4.8 collective-permute-start.72
  548.5 4.8 collective-permute-start.77
  561.2 5.1 collective-permute-start.82
  574.5 5.1 collective-permute-start.87
  587.8 5.4 all_to_all.104
  (628 shorter events, 243.7 us)
Async XLA Ops:
  11.3 9.5 %all-to-all-start = ((f32[1,4,8,128,128]{4,2,1,0,3:T(8,128)}), f32[1,4,8,128,128]{4,2,1,0,3:T(8,128)S(1)}, u32[]{:S(2)}, u32[]{:S(2)}) async-start(f32[1,4,8,128,128]{4,2,1,0,3:T(8,128)} %copy.1004), calls=%async_computation | async-start | bytes 4194304 | tf_op jit(solution)/shard_map/all_to_all | solution.py:194
  21.4 14.3 %all-to-all-start.5 = ((f32[8,4,8,128]{3,2,1,0:T(8,128)}), f32[8,4,8,128]{3,2,1,0:T(8,128)S(1)}, u32[]{:S(2)}, u32[]{:S(2)}) async-start(f32[8,4,8,128]{3,2,1,0:T(8,128)} %broadcast_in_dim.125), calls=%async_computation.5 | async-start | bytes 262144 | tf_op jit(solution)/shard_map/all_to_all | solution.py:35
  35.8 25.8 %all-to-all-start.1 = ((f32[32,64,128]{2,1,0:T(8,128)}), f32[32,64,128]{2,1,0:T(8,128)S(1)}, u32[]{:S(2)}, u32[]{:S(2)}) async-start(f32[32,64,128]{2,1,0:T(8,128)} %bitcast.14), calls=%async_computation.1 | async-start | bytes 2097152 | tf_op jit(solution)/shard_map/all_to_all | solution.py:212
  45.0 278.1 %all-gather.2.cloned.1.call-start = ((), (), s32[]{:S(2)}) async-start(), calls=%async_computation.7 | async-start | bytes 4325376 | tf_op jit(solution)/shard_map/all_gather | solution.py:43
  61.6 114.5 %all-to-all-start.3 = ((f32[32,64,128]{2,1,0:T(8,128)}), f32[32,64,128]{2,1,0:T(8,128)}, u32[]{:S(2)}, u32[]{:S(2)}) async-start(f32[32,64,128]{2,1,0:T(8,128)} %bitcast.14), calls=%async_computation.3 | async-start | bytes 2097152 | tf_op jit(solution)/shard_map/all_to_all | solution.py:215
  176.1 49.7 %all-to-all-start.2 = ((f32[1,2,2048,128]{3,1,0,2:T(2,128)}), f32[1,2,2048,128]{3,1,0,2:T(2,128)}, u32[]{:S(2)}, u32[]{:S(2)}) async-start(f32[1,2,2048,128]{3,1,0,2:T(2,128)} %get-tuple-element.1079), calls=%async_computation.2 | async-start | bytes 4194304 | tf_op jit(solution)/shard_map/all_to_all | solution.py:214
  225.8 74.0 %all-to-all-start.4 = ((f32[8,1,65536]{2,1,0:T(1,128)}), f32[8,1,65536]{2,1,0:T(1,128)}, u32[]{:S(2)}, u32[]{:S(2)}) async-start(f32[8,1,65536]{2,1,0:T(1,128)} %reshape.3353), calls=%async_computation.4 | async-start | bytes 4194304 | tf_op jit(solution)/shard_map/all_to_all | solution.py:216
  236.6 37.7 %collective-permute-start = (f32[32,64,1]{1,0,2:T(8,128)}, f32[32,64,1]{1,0,2:T(8,128)}, u32[]{:S(2)}, u32[]{:S(2)}) collective-permute-start(f32[32,64,1]{1,0,2:T(8,128)} %copy.1123), channel_id=1, source_target_pairs={{0,1},{1,2},{2,3},{3,4},{4,5},{5,6},{6,7},{7,0},{8,9},{9,10},{10,1... | collective-permute-start | bytes 24584 | tf_op jit(solution)/shard_map/ppermute | solution.py:54
  240.2 39.6 %collective-permute-start.3 = (f32[32,64,1]{1,0,2:T(8,128)}, f32[32,64,1]{1,0,2:T(8,128)}, u32[]{:S(2)}, u32[]{:S(2)}) collective-permute-start(f32[32,64,1]{1,0,2:T(8,128)} %copy.1124), channel_id=1, source_target_pairs={{1,0},{2,1},{3,2},{4,3},{5,4},{6,5},{7,6},{0,7},{9,8},{10,9},{11,1... | collective-permute-start | bytes 24584 | tf_op jit(solution)/shard_map/ppermute | solution.py:55
  242.1 39.8 %collective-permute-start.1 = (f32[32,1,128]{2,1,0:T(1,128)}, f32[32,1,128]{2,1,0:T(1,128)S(1)}, u32[]{:S(2)}, u32[]{:S(2)}) collective-permute-start(f32[32,1,128]{2,1,0:T(1,128)} %get-tuple-element.1151), channel_id=1, source_target_pairs={{0,8},{8,16},{16,24},{24,32},{32,40},{40,48},{48,56},{56,64},{64,7... | collective-permute-start | bytes 49160 | tf_op jit(solution)/shard_map/ppermute | solution.py:54
  243.5 38.5 %collective-permute-start.2 = (f32[32,1,128]{2,1,0:T(1,128)}, f32[32,1,128]{2,1,0:T(1,128)}, u32[]{:S(2)}, u32[]{:S(2)}) collective-permute-start(f32[32,1,128]{2,1,0:T(1,128)} %get-tuple-element.1152), channel_id=1, source_target_pairs={{8,0},{16,8},{24,16},{32,24},{40,32},{48,40},{56,48},{64,56},{72,6... | collective-permute-start | bytes 49160 | tf_op jit(solution)/shard_map/ppermute | solution.py:55
  335.2 16.5 %collective-permute-start.5 = (f32[16,64,1]{2,1,0:T(8,128)S(1)}, f32[16,64,1]{2,1,0:T(8,128)S(1)}, u32[]{:S(2)}, u32[]{:S(2)}) collective-permute-start(f32[16,64,1]{2,1,0:T(8,128)S(1)} %get-tuple-element.1194), channel_id=1, source_target_pairs={{0,1},{1,2},{2,3},{3,4},{4,5},{5,6},{6,7},{7,0},{8,9},{9,10},{10,1... | collective-permute-start | bytes 12296 | tf_op jit(solution)/shard_map/ppermute | solution.py:54
  335.3 16.4 %collective-permute-start.8 = (f32[16,64,1]{2,1,0:T(8,128)S(1)}, f32[16,64,1]{2,1,0:T(8,128)S(1)}, u32[]{:S(2)}, u32[]{:S(2)}) collective-permute-start(f32[16,64,1]{2,1,0:T(8,128)S(1)} %get-tuple-element.1195), channel_id=1, source_target_pairs={{1,0},{2,1},{3,2},{4,3},{5,4},{6,5},{7,6},{0,7},{9,8},{10,9},{11,1... | collective-permute-start | bytes 12296 | tf_op jit(solution)/shard_map/ppermute | solution.py:55
  339.8 11.9 %collective-permute-start.6 = (f32[16,1,128]{2,1,0:T(1,128)S(1)}, f32[16,1,128]{2,1,0:T(1,128)S(1)}, u32[]{:S(2)}, u32[]{:S(2)}) collective-permute-start(f32[16,1,128]{2,1,0:T(1,128)S(1)} %get-tuple-element.1192), channel_id=1, source_target_pairs={{0,8},{8,16},{16,24},{24,32},{32,40},{40,48},{48,56},{56,64},{64,7... | collective-permute-start | bytes 24584 | tf_op jit(solution)/shard_map/ppermute | solution.py:54
  341.1 10.6 %collective-permute-start.7 = (f32[16,1,128]{2,1,0:T(1,128)S(1)}, f32[16,1,128]{2,1,0:T(1,128)S(1)}, u32[]{:S(2)}, u32[]{:S(2)}) collective-permute-start(f32[16,1,128]{2,1,0:T(1,128)S(1)} %get-tuple-element.1193), channel_id=1, source_target_pairs={{8,0},{16,8},{24,16},{32,24},{40,32},{48,40},{56,48},{64,56},{72,6... | collective-permute-start | bytes 24584 | tf_op jit(solution)/shard_map/ppermute | solution.py:55
  356.3 9.0 %collective-permute-start.10 = (f32[8,64,1]{2,1,0:T(8,128)S(1)}, f32[8,64,1]{2,1,0:T(8,128)S(1)}, u32[]{:S(2)}, u32[]{:S(2)}) collective-permute-start(f32[8,64,1]{2,1,0:T(8,128)S(1)} %get-tuple-element.1298), channel_id=1, source_target_pairs={{0,1},{1,2},{2,3},{3,4},{4,5},{5,6},{6,7},{7,0},{8,9},{9,10},{10,1... | collective-permute-start | bytes 6152 | tf_op jit(solution)/shard_map/ppermute | solution.py:54
  356.8 8.6 %collective-permute-start.13 = (f32[8,64,1]{2,1,0:T(8,128)S(1)}, f32[8,64,1]{2,1,0:T(8,128)S(1)}, u32[]{:S(2)}, u32[]{:S(2)}) collective-permute-start(f32[8,64,1]{2,1,0:T(8,128)S(1)} %get-tuple-element.1299), channel_id=1, source_target_pairs={{1,0},{2,1},{3,2},{4,3},{5,4},{6,5},{7,6},{0,7},{9,8},{10,9},{11,1... | collective-permute-start | bytes 6152 | tf_op jit(solution)/shard_map/ppermute | solution.py:55
  359.3 6.1 %collective-permute-start.11 = (f32[8,1,128]{2,1,0:T(1,128)S(1)}, f32[8,1,128]{2,1,0:T(1,128)S(1)}, u32[]{:S(2)}, u32[]{:S(2)}) collective-permute-start(f32[8,1,128]{2,1,0:T(1,128)S(1)} %get-tuple-element.1296), channel_id=1, source_target_pairs={{0,8},{8,16},{16,24},{24,32},{32,40},{40,48},{48,56},{56,64},{64,7... | collective-permute-start | bytes 12296 | tf_op jit(solution)/shard_map/ppermute | solution.py:54
  378.3 7.8 %collective-permute-start.15 = (f32[8,32,1]{2,0,1:T(8,128)S(1)}, f32[8,32,1]{2,0,1:T(8,128)S(1)}, u32[]{:S(2)}, u32[]{:S(2)}) collective-permute-start(f32[8,32,1]{2,0,1:T(8,128)S(1)} %get-tuple-element.1354), channel_id=1, source_target_pairs={{0,1},{1,2},{2,3},{3,4},{4,5},{5,6},{6,7},{7,0},{8,9},{9,10},{10,1... | collective-permute-start | bytes 3080 | tf_op jit(solution)/shard_map/ppermute | solution.py:54
  391.8 9.3 %collective-permute-start.21 = (f32[8,1,32]{0,2,1:T(8,128)S(1)}, f32[8,1,32]{0,2,1:T(8,128)S(1)}, u32[]{:S(2)}, u32[]{:S(2)}) collective-permute-start(f32[8,1,32]{0,2,1:T(8,128)S(1)} %get-tuple-element.1288), channel_id=1, source_target_pairs={{0,8},{8,16},{16,24},{24,32},{32,40},{40,48},{48,56},{56,64},{64,7... | collective-permute-start | bytes 3080 | tf_op jit(solution)/shard_map/ppermute | solution.py:54
  391.9 9.2 %collective-permute-start.22 = (f32[8,1,32]{0,2,1:T(8,128)S(1)}, f32[8,1,32]{0,2,1:T(8,128)S(1)}, u32[]{:S(2)}, u32[]{:S(2)}) collective-permute-start(f32[8,1,32]{0,2,1:T(8,128)S(1)} %get-tuple-element.1289), channel_id=1, source_target_pairs={{8,0},{16,8},{24,16},{32,24},{40,32},{48,40},{56,48},{64,56},{72,6... | collective-permute-start | bytes 3080 | tf_op jit(solution)/shard_map/ppermute | solution.py:55
  404.9 8.8 %collective-permute-start.26 = (f32[8,1,16]{0,2,1:T(8,128)S(1)}, f32[8,1,16]{0,2,1:T(8,128)S(1)}, u32[]{:S(2)}, u32[]{:S(2)}) collective-permute-start(f32[8,1,16]{0,2,1:T(8,128)S(1)} %get-tuple-element.1384), channel_id=1, source_target_pairs={{0,8},{8,16},{16,24},{24,32},{32,40},{40,48},{48,56},{56,64},{64,7... | collective-permute-start | bytes 1544 | tf_op jit(solution)/shard_map/ppermute | solution.py:54
  405.0 8.7 %collective-permute-start.27 = (f32[8,1,16]{0,2,1:T(8,128)S(1)}, f32[8,1,16]{0,2,1:T(8,128)S(1)}, u32[]{:S(2)}, u32[]{:S(2)}) collective-permute-start(f32[8,1,16]{0,2,1:T(8,128)S(1)} %get-tuple-element.1385), channel_id=1, source_target_pairs={{8,0},{16,8},{24,16},{32,24},{40,32},{48,40},{56,48},{64,56},{72,6... | collective-permute-start | bytes 1544 | tf_op jit(solution)/shard_map/ppermute | solution.py:55
  417.7 10.2 %collective-permute-start.31 = (f32[8,1,32]{0,2,1:T(8,128)S(1)}, f32[8,1,32]{0,2,1:T(8,128)S(1)}, u32[]{:S(2)}, u32[]{:S(2)}) collective-permute-start(f32[8,1,32]{0,2,1:T(8,128)S(1)} %get-tuple-element.1280), channel_id=1, source_target_pairs={{0,8},{8,16},{16,24},{24,32},{32,40},{40,48},{48,56},{56,64},{64,7... | collective-permute-start | bytes 3080 | tf_op jit(solution)/shard_map/ppermute | solution.py:54
  417.8 10.2 %collective-permute-start.32 = (f32[8,1,32]{0,2,1:T(8,128)S(1)}, f32[8,1,32]{0,2,1:T(8,128)S(1)}, u32[]{:S(2)}, u32[]{:S(2)}) collective-permute-start(f32[8,1,32]{0,2,1:T(8,128)S(1)} %get-tuple-element.1281), channel_id=1, source_target_pairs={{8,0},{16,8},{24,16},{32,24},{40,32},{48,40},{56,48},{64,56},{72,6... | collective-permute-start | bytes 3080 | tf_op jit(solution)/shard_map/ppermute | solution.py:55
  432.3 8.2 %collective-permute-start.35 = (f32[8,32,1]{2,0,1:T(8,128)S(1)}, f32[8,32,1]{2,0,1:T(8,128)S(1)}, u32[]{:S(2)}, u32[]{:S(2)}) collective-permute-start(f32[8,32,1]{2,0,1:T(8,128)S(1)} %get-tuple-element.1350), channel_id=1, source_target_pairs={{0,1},{1,2},{2,3},{3,4},{4,5},{5,6},{6,7},{7,0},{8,9},{9,10},{10,1... | collective-permute-start | bytes 3080 | tf_op jit(solution)/shard_map/ppermute | solution.py:54
  434.3 6.2 %collective-permute-start.38 = (f32[8,32,1]{2,0,1:T(8,128)S(1)}, f32[8,32,1]{2,0,1:T(8,128)S(1)}, u32[]{:S(2)}, u32[]{:S(2)}) collective-permute-start(f32[8,32,1]{2,0,1:T(8,128)S(1)} %get-tuple-element.1351), channel_id=1, source_target_pairs={{1,0},{2,1},{3,2},{4,3},{5,4},{6,5},{7,6},{0,7},{9,8},{10,9},{11,1... | collective-permute-start | bytes 3080 | tf_op jit(solution)/shard_map/ppermute | solution.py:55
  445.4 8.8 %collective-permute-start.40 = (f32[8,64,1]{2,1,0:T(8,128)S(1)}, f32[8,64,1]{2,1,0:T(8,128)S(1)}, u32[]{:S(2)}, u32[]{:S(2)}) collective-permute-start(f32[8,64,1]{2,1,0:T(8,128)S(1)} %get-tuple-element.1274), channel_id=1, source_target_pairs={{0,1},{1,2},{2,3},{3,4},{4,5},{5,6},{6,7},{7,0},{8,9},{9,10},{10,1... | collective-permute-start | bytes 6152 | tf_op jit(solution)/shard_map/ppermute | solution.py:54
  446.1 8.2 %collective-permute-start.43 = (f32[8,64,1]{2,1,0:T(8,128)S(1)}, f32[8,64,1]{2,1,0:T(8,128)S(1)}, u32[]{:S(2)}, u32[]{:S(2)}) collective-permute-start(f32[8,64,1]{2,1,0:T(8,128)S(1)} %get-tuple-element.1275), channel_id=1, source_target_pairs={{1,0},{2,1},{3,2},{4,3},{5,4},{6,5},{7,6},{0,7},{9,8},{10,9},{11,1... | collective-permute-start | bytes 6152 | tf_op jit(solution)/shard_map/ppermute | solution.py:55
  458.4 8.8 %collective-permute-start.45 = (f32[8,64,1]{2,1,0:T(8,128)S(1)}, f32[8,64,1]{2,1,0:T(8,128)S(1)}, u32[]{:S(2)}, u32[]{:S(2)}) collective-permute-start(f32[8,64,1]{2,1,0:T(8,128)S(1)} %get-tuple-element.1266), channel_id=1, source_target_pairs={{0,1},{1,2},{2,3},{3,4},{4,5},{5,6},{6,7},{7,0},{8,9},{9,10},{10,1... | collective-permute-start | bytes 6152 | tf_op jit(solution)/shard_map/ppermute | solution.py:54
  458.5 8.7 %collective-permute-start.48 = (f32[8,64,1]{2,1,0:T(8,128)S(1)}, f32[8,64,1]{2,1,0:T(8,128)S(1)}, u32[]{:S(2)}, u32[]{:S(2)}) collective-permute-start(f32[8,64,1]{2,1,0:T(8,128)S(1)} %get-tuple-element.1267), channel_id=1, source_target_pairs={{1,0},{2,1},{3,2},{4,3},{5,4},{6,5},{7,6},{0,7},{9,8},{10,9},{11,1... | collective-permute-start | bytes 6152 | tf_op jit(solution)/shard_map/ppermute | solution.py:55
  471.7 8.8 %collective-permute-start.50 = (f32[8,64,1]{2,1,0:T(8,128)S(1)}, f32[8,64,1]{2,1,0:T(8,128)S(1)}, u32[]{:S(2)}, u32[]{:S(2)}) collective-permute-start(f32[8,64,1]{2,1,0:T(8,128)S(1)} %get-tuple-element.1258), channel_id=1, source_target_pairs={{0,1},{1,2},{2,3},{3,4},{4,5},{5,6},{6,7},{7,0},{8,9},{9,10},{10,1... | collective-permute-start | bytes 6152 | tf_op jit(solution)/shard_map/ppermute | solution.py:54
  471.8 8.7 %collective-permute-start.53 = (f32[8,64,1]{2,1,0:T(8,128)S(1)}, f32[8,64,1]{2,1,0:T(8,128)S(1)}, u32[]{:S(2)}, u32[]{:S(2)}) collective-permute-start(f32[8,64,1]{2,1,0:T(8,128)S(1)} %get-tuple-element.1259), channel_id=1, source_target_pairs={{1,0},{2,1},{3,2},{4,3},{5,4},{6,5},{7,6},{0,7},{9,8},{10,9},{11,1... | collective-permute-start | bytes 6152 | tf_op jit(solution)/shard_map/ppermute | solution.py:55
  493.3 8.1 %collective-permute-start.55 = (f32[8,32,1]{2,0,1:T(8,128)S(1)}, f32[8,32,1]{2,0,1:T(8,128)S(1)}, u32[]{:S(2)}, u32[]{:S(2)}) collective-permute-start(f32[8,32,1]{2,0,1:T(8,128)S(1)} %get-tuple-element.1342), channel_id=1, source_target_pairs={{0,1},{1,2},{2,3},{3,4},{4,5},{5,6},{6,7},{7,0},{8,9},{9,10},{10,1... | collective-permute-start | bytes 3080 | tf_op jit(solution)/shard_map/ppermute | solution.py:54
  493.4 8.0 %collective-permute-start.58 = (f32[8,32,1]{2,0,1:T(8,128)S(1)}, f32[8,32,1]{2,0,1:T(8,128)S(1)}, u32[]{:S(2)}, u32[]{:S(2)}) collective-permute-start(f32[8,32,1]{2,0,1:T(8,128)S(1)} %get-tuple-element.1343), channel_id=1, source_target_pairs={{1,0},{2,1},{3,2},{4,3},{5,4},{6,5},{7,6},{0,7},{9,8},{10,9},{11,1... | collective-permute-start | bytes 3080 | tf_op jit(solution)/shard_map/ppermute | solution.py:55
  496.1 6.2 %collective-permute-start.56 = (f32[8,1,64]{2,0,1:T(8,128)S(1)}, f32[8,1,64]{2,0,1:T(8,128)S(1)}, u32[]{:S(2)}, u32[]{:S(2)}) collective-permute-start(f32[8,1,64]{2,0,1:T(8,128)S(1)} %get-tuple-element.1340), channel_id=1, source_target_pairs={{0,8},{8,16},{16,24},{24,32},{32,40},{40,48},{48,56},{56,64},{64,7... | collective-permute-start | bytes 6152 | tf_op jit(solution)/shard_map/ppermute | solution.py:54
  507.0 9.0 %collective-permute-start.61 = (f32[8,1,32]{0,2,1:T(8,128)S(1)}, f32[8,1,32]{0,2,1:T(8,128)S(1)}, u32[]{:S(2)}, u32[]{:S(2)}) collective-permute-start(f32[8,1,32]{0,2,1:T(8,128)S(1)} %get-tuple-element.1248), channel_id=1, source_target_pairs={{0,8},{8,16},{16,24},{24,32},{32,40},{40,48},{48,56},{56,64},{64,7... | collective-permute-start | bytes 3080 | tf_op jit(solution)/shard_map/ppermute | solution.py:54
  507.1 8.9 %collective-permute-start.62 = (f32[8,1,32]{0,2,1:T(8,128)S(1)}, f32[8,1,32]{0,2,1:T(8,128)S(1)}, u32[]{:S(2)}, u32[]{:S(2)}) collective-permute-start(f32[8,1,32]{0,2,1:T(8,128)S(1)} %get-tuple-element.1249), channel_id=1, source_target_pairs={{8,0},{16,8},{24,16},{32,24},{40,32},{48,40},{56,48},{64,56},{72,6... | collective-permute-start | bytes 3080 | tf_op jit(solution)/shard_map/ppermute | solution.py:55
  519.7 8.8 %collective-permute-start.66 = (f32[8,1,16]{0,2,1:T(8,128)S(1)}, f32[8,1,16]{0,2,1:T(8,128)S(1)}, u32[]{:S(2)}, u32[]{:S(2)}) collective-permute-start(f32[8,1,16]{0,2,1:T(8,128)S(1)} %get-tuple-element.1376), channel_id=1, source_target_pairs={{0,8},{8,16},{16,24},{24,32},{32,40},{40,48},{48,56},{56,64},{64,7... | collective-permute-start | bytes 1544 | tf_op jit(solution)/shard_map/ppermute | solution.py:54
  519.8 8.7 %collective-permute-start.67 = (f32[8,1,16]{0,2,1:T(8,128)S(1)}, f32[8,1,16]{0,2,1:T(8,128)S(1)}, u32[]{:S(2)}, u32[]{:S(2)}) collective-permute-start(f32[8,1,16]{0,2,1:T(8,128)S(1)} %get-tuple-element.1377), channel_id=1, source_target_pairs={{8,0},{16,8},{24,16},{32,24},{40,32},{48,40},{56,48},{64,56},{72,6... | collective-permute-start | bytes 1544 | tf_op jit(solution)/shard_map/ppermute | solution.py:55
  532.2 9.1 %collective-permute-start.71 = (f32[8,1,32]{0,2,1:T(8,128)S(1)}, f32[8,1,32]{0,2,1:T(8,128)S(1)}, u32[]{:S(2)}, u32[]{:S(2)}) collective-permute-start(f32[8,1,32]{0,2,1:T(8,128)S(1)} %get-tuple-element.1240), channel_id=1, source_target_pairs={{0,8},{8,16},{16,24},{24,32},{32,40},{40,48},{48,56},{56,64},{64,7... | collective-permute-start | bytes 3080 | tf_op jit(solution)/shard_map/ppermute | solution.py:54
  532.5 8.8 %collective-permute-start.72 = (f32[8,1,32]{0,2,1:T(8,128)S(1)}, f32[8,1,32]{0,2,1:T(8,128)S(1)}, u32[]{:S(2)}, u32[]{:S(2)}) collective-permute-start(f32[8,1,32]{0,2,1:T(8,128)S(1)} %get-tuple-element.1241), channel_id=1, source_target_pairs={{8,0},{16,8},{24,16},{32,24},{40,32},{48,40},{56,48},{64,56},{72,6... | collective-permute-start | bytes 3080 | tf_op jit(solution)/shard_map/ppermute | solution.py:55
  545.5 7.8 %collective-permute-start.75 = (f32[8,32,1]{2,0,1:T(8,128)S(1)}, f32[8,32,1]{2,0,1:T(8,128)S(1)}, u32[]{:S(2)}, u32[]{:S(2)}) collective-permute-start(f32[8,32,1]{2,0,1:T(8,128)S(1)} %get-tuple-element.1330), channel_id=1, source_target_pairs={{0,1},{1,2},{2,3},{3,4},{4,5},{5,6},{6,7},{7,0},{8,9},{9,10},{10,1... | collective-permute-start | bytes 3080 | tf_op jit(solution)/shard_map/ppermute | solution.py:54
  558.5 8.8 %collective-permute-start.80 = (f32[8,64,1]{2,1,0:T(8,128)S(1)}, f32[8,64,1]{2,1,0:T(8,128)S(1)}, u32[]{:S(2)}, u32[]{:S(2)}) collective-permute-start(f32[8,64,1]{2,1,0:T(8,128)S(1)} %get-tuple-element.1234), channel_id=1, source_target_pairs={{0,1},{1,2},{2,3},{3,4},{4,5},{5,6},{6,7},{7,0},{8,9},{9,10},{10,1... | collective-permute-start | bytes 6152 | tf_op jit(solution)/shard_map/ppermute | solution.py:54
  559.1 8.2 %collective-permute-start.83 = (f32[8,64,1]{2,1,0:T(8,128)S(1)}, f32[8,64,1]{2,1,0:T(8,128)S(1)}, u32[]{:S(2)}, u32[]{:S(2)}) collective-permute-start(f32[8,64,1]{2,1,0:T(8,128)S(1)} %get-tuple-element.1235), channel_id=1, source_target_pairs={{1,0},{2,1},{3,2},{4,3},{5,4},{6,5},{7,6},{0,7},{9,8},{10,9},{11,1... | collective-permute-start | bytes 6152 | tf_op jit(solution)/shard_map/ppermute | solution.py:55
  561.2 6.1 %collective-permute-start.81 = (f32[8,1,128]{2,1,0:T(1,128)S(1)}, f32[8,1,128]{2,1,0:T(1,128)S(1)}, u32[]{:S(2)}, u32[]{:S(2)}) collective-permute-start(f32[8,1,128]{2,1,0:T(1,128)S(1)} %get-tuple-element.1232), channel_id=1, source_target_pairs={{0,8},{8,16},{16,24},{24,32},{32,40},{40,48},{48,56},{56,64},{64,7... | collective-permute-start | bytes 12296 | tf_op jit(solution)/shard_map/ppermute | solution.py:54
  571.7 8.8 %collective-permute-start.85 = (f32[8,64,1]{2,1,0:T(8,128)S(1)}, f32[8,64,1]{2,1,0:T(8,128)S(1)}, u32[]{:S(2)}, u32[]{:S(2)}) collective-permute-start(f32[8,64,1]{2,1,0:T(8,128)S(1)} %get-tuple-element.1222), channel_id=1, source_target_pairs={{0,1},{1,2},{2,3},{3,4},{4,5},{5,6},{6,7},{7,0},{8,9},{9,10},{10,1... | collective-permute-start | bytes 6152 | tf_op jit(solution)/shard_map/ppermute | solution.py:54
  571.8 8.7 %collective-permute-start.88 = (f32[8,64,1]{2,1,0:T(8,128)S(1)}, f32[8,64,1]{2,1,0:T(8,128)S(1)}, u32[]{:S(2)}, u32[]{:S(2)}) collective-permute-start(f32[8,64,1]{2,1,0:T(8,128)S(1)} %get-tuple-element.1223), channel_id=1, source_target_pairs={{1,0},{2,1},{3,2},{4,3},{5,4},{6,5},{7,6},{0,7},{9,8},{10,9},{11,1... | collective-permute-start | bytes 6152 | tf_op jit(solution)/shard_map/ppermute | solution.py:55
  (75 other events, 409.2 us)
Sparse Core Ops, SparseCore 0:
  48.4 47.9 all-gather.1
where the time goes:
time: 607 us; the launch traced here: 602 us
  starting transfers between devices  216 us (36%)
  other arithmetic  149 us (25%)
  local copies, waits for them, and re-layouts  99.8 us (16%)
  waiting for transfers between devices  76.2 us (13%)
  matrix products  37.9 us (6%)
  between operations  16.6 us (3%)
    ppermute x36, starting transfers between devices, extended(): lax.ppermute(first, axis, [(b, a) for a, b in up])  120 us
    select_n x6, other arithmetic, derivative_rows(): jnp.where(offset == 0, 0.0, 0.5 * spacing * parity * jnp.cos(half_angle)...  94.5 us
    ppermute x36, waiting for transfers between devices, extended(): lax.ppermute(last, axis, up)  37.5 us
    dot_general x6, matrix products, add_block(): product = jnp.einsum(form, table_rows, operand, precision=highest)  36.5 us
    ppermute x18, starting transfers between devices, partner_2(): lax.ppermute(array, axis, [(i, i ^ 1 << apart) for i in range(lax.axis_si...  34 us
    unnamed x59, local copies, waits for them, and re-layouts  31.5 us
    ppermute x36, starting transfers between devices, extended(): lax.ppermute(last, axis, up)  22 us
    all_to_all x1, waiting for transfers between devices, on_device(): lax.all_to_all(stacked, ('dom', 'gx'), split_axis=0, concat_axis=1, tiled...  15.7 us
  transfers between devices with their start and end apart: 97, of which 41 were waited for; matrix products, arithmetic and copies ran while one was open for 37% of the time, Pallas kernels for 0%

commit v1 on v0

v1 whole, which is shorter than its diff:
```python
import functools

import jax
import jax.numpy as jnp
import ml_dtypes
import numpy as np
from jax import lax
from jax.experimental import pallas as pl
from jax.experimental.pallas import tpu as pltpu
from jax.sharding import PartitionSpec as P

NX = 2048
NY = 1024
NZ = 8
BX = 128
BY = 128
HALF = 64
GX = 16
GY = 8
HALO = 48
EXT = BX + 2 * HALO
F32 = jnp.float32
BF16 = jnp.bfloat16
VMEM_BYTES = 48 * 1024 * 1024


def table_entries(length):
    offset = np.arange(length, dtype=np.float64)
    spacing = 2.0 * np.pi / length
    sign = np.where(offset % 2 == 0, 1.0, -1.0)
    angle = np.pi * offset / length
    angle[0] = 1.0
    slope = 0.5 * spacing * sign * np.cos(angle) / np.sin(angle)
    bend = -0.5 * spacing * spacing * sign / np.sin(angle) ** 2
    slope[0] = 0.0
    bend[0] = -np.pi**2 / 3.0 - spacing * spacing / 6.0
    return -0.2 * slope, 0.2 * 0.05 * bend


def split_bf16(table):
    high = table.astype(np.float32).astype(ml_dtypes.bfloat16)
    low = (table - high.astype(np.float64)).astype(np.float32).astype(ml_dtypes.bfloat16)
    return high, low


def span_tables():
    tiles = []
    i = np.arange(256)
    for d in (3, 2, 1, 0, 3, 2, 1):
        index = (256 * d + i[None, :] - i[:, None]) % NY
        tiles.append(np.concatenate([entry[index] for entry in table_entries(NY)], axis=1))
    return split_bf16(np.concatenate(tiles, axis=0))


def line_tables():
    i = np.arange(256)
    both = []
    for sign in (1.0, -1.0):
        tiles = []
        for place, d in enumerate((3, 2, 1, 0, 3, 2, 1)):
            index = 256 * d + i[:, None] - i[None, :]
            flip = 1.0 if place < 4 else sign
            tiles.append(
                np.concatenate(
                    [
                        0.5 * flip * (entry[index % NX] + sign * entry[(index + NX // 2) % NX])
                        for entry in table_entries(NX)
                    ],
                    axis=0,
                )
            )
        both.append(split_bf16(np.concatenate(tiles, axis=1)))
    return both


def kernel_call(body, outs, scratch=(), scalars=1, count=0):
    specs = [pl.BlockSpec(memory_space=pltpu.SMEM)] * scalars
    specs += [pl.BlockSpec(memory_space=pltpu.VMEM)] * count
    shapes = [jax.ShapeDtypeStruct(s, F32) for s in outs]
    return pl.pallas_call(
        body,
        out_shape=shapes,
        in_specs=specs,
        out_specs=[pl.BlockSpec(memory_space=pltpu.VMEM)] * len(outs),
        scratch_shapes=list(scratch),
        compiler_params=pltpu.CompilerParams(vmem_limit_bytes=VMEM_BYTES),
    )


def lane_index(shape):
    return lax.broadcasted_iota(jnp.int32, shape, len(shape) - 1)


def halves(values):
    high = values.astype(BF16)
    return high, (values - high.astype(F32)).astype(BF16)


def send_kernel(place, own, got, ybuf, half):
    def fill(source):
        for z in range(NZ):
            for c in range(4):
                block = source(c, z)
                ybuf[z, c * HALF : (c + 1) * HALF] = block
                half[c, z] = block

    @pl.when(place[0] == 0)
    def _():
        fill(lambda c, z: own[c, z, :HALF])

    @pl.when(place[0] == 1)
    def _():
        fill(lambda c, z: got[c, z])

    plane = jnp.concatenate([own[c, :, 0, :] for c in range(4)], axis=0)
    for g in range(GY):
        ybuf[g, 4 * HALF :] = plane


def blend_kernel(half, yin, source, weight, xbuf, inflow):
    plane = jnp.concatenate([yin[g, 4 * HALF :] for g in range(GY)], axis=1)
    rows = lax.broadcasted_iota(jnp.int32, (NY, BY), 0)
    share = weight[...].astype(F32) / 16.0
    first = source[...]
    follow = jnp.where(first == NY - 1, 0, first + 1)
    table = jnp.where(rows == first, share, 0.0) + jnp.where(rows == follow, 1.0 - share, 0.0)
    blended = jnp.dot(plane, table, precision=lax.Precision.HIGHEST, preferred_element_type=F32)
    inflow[...] = blended
    lane = lane_index((HALF, BY))
    for z in range(NZ):
        for part in range(4):
            total = None
            for c in range(4):
                shift = 32 * ((c - part) % 4)
                moved = half[c, z] if shift == 0 else pltpu.roll(half[c, z], shift, 1)
                total = moved if total is None else jnp.where(lane >= 32 * c, moved, total)
            xbuf[4 * z + part, :HALF] = total
    for r in range(4 * NZ):
        xbuf[r, HALF:] = jnp.broadcast_to(blended[r : r + 1], (8, BY))


def span_kernel(yin, table_high, table_low, yout, high, low):
    for g in range(GY):
        h, l = halves(yin[g, : 4 * HALF])
        high[:, g * BY : (g + 1) * BY] = h
        low[:, g * BY : (g + 1) * BY] = l
    for i in range(4):
        at = pl.ds((3 - i) * 256, 4 * 256)
        th = table_high[at, :]
        value = jnp.dot(high[...], th, preferred_element_type=F32)
        value += jnp.dot(low[...], th, preferred_element_type=F32)
        value += jnp.dot(high[...], table_low[at, :], preferred_element_type=F32)
        for k in range(2):
            g = 2 * i + k
            v = yin[g, HALF : 2 * HALF]
            for c in range(4):
                rows = slice(c * HALF, (c + 1) * HALF)
                yout[g, rows] = (
                    v * value[rows, k * BY : (k + 1) * BY]
                    + value[rows, 256 + k * BY : 256 + (k + 1) * BY]
                )


def chunk_place(m):
    return (m % 2) * GX + m // 2


def line_kernel(xin, sh, sl, ah, al, xout, plus_h, plus_l, minus_h, minus_l):
    for m in range(16):
        a = xin[chunk_place(m), :HALF]
        b = xin[chunk_place(m + 16), :HALF]
        rows = slice(m * HALF, (m + 1) * HALF)
        plus_h[rows], plus_l[rows] = halves(a + b)
        minus_h[rows], minus_l[rows] = halves(a - b)
    lane = lane_index((HALF, BY))
    for i in range(4):
        at = pl.ds((3 - i) * 256, 4 * 256)

        def product(table_high, table_low, high, low):
            th = table_high[:, at]
            value = jnp.dot(th, high[...], preferred_element_type=F32)
            value += jnp.dot(th, low[...], preferred_element_type=F32)
            return value + jnp.dot(table_low[:, at], high[...], preferred_element_type=F32)

        even = product(sh, sl, plus_h, plus_l)
        odd = product(ah, al, minus_h, minus_l)
        for k in range(4):
            for side, value in ((0, even + odd), (1, even - odd)):
                place = chunk_place(4 * i + k + 16 * side)
                u = jnp.where(lane < 32, xin[place, :HALF], 0.0)
                u = u + pltpu.roll(u, 32, 1)
                u = u + pltpu.roll(u, 64, 1)
                rows = slice(k * HALF, (k + 1) * HALF)
                late = slice(256 + k * HALF, 256 + (k + 1) * HALF)
                xout[place] = (1.0 + u) * value[rows] + value[late]


def finish_kernel(half, yback, xback, out):
    lane = lane_index((HALF, BY))
    for z in range(NZ):
        for c in range(4):
            total = None
            for part in range(4):
                shift = 32 * ((part - c) % 4)
                tile = xback[4 * z + part]
                moved = tile if shift == 0 else pltpu.roll(tile, shift, 1)
                total = moved if total is None else jnp.where(lane >= 32 * part, moved, total)
            q = half[c, z]
            upper = half[c, min(z + 1, NZ - 1)]
            lower = half[c, max(z - 1, 0)]
            mixed = 0.02 * (upper + lower - 2.0 * q) - 0.1 * half[2, z] * (upper - lower)
            out[c, z] = q + total + yback[z, c * HALF : (c + 1) * HALF] + mixed


def turn_kernel(place, own, mask, cells, drag, row_low, row_high, col_low, col_high):
    @pl.when(place[0] == 1)
    def _():
        for z in range(NZ):
            for c in range(4):
                cells[c, pl.ds(z, BX, stride=NZ), :] = own[c, z]
            drag[pl.ds(z, BX, stride=NZ), :] = mask[z].astype(F32)
        for c in range(4):
            row_low[c] = cells[c, :NZ]
            row_high[c] = cells[c, (BX - 1) * NZ :]
        lane = lane_index((NZ, BY))

        def step(x, carry):
            low, high = carry
            hit = lane == x
            at = pl.ds(pl.multiple_of(x * NZ, NZ), NZ)
            low = tuple(jnp.where(hit, cells[c, at, 0:1], low[c]) for c in range(4))
            high = tuple(jnp.where(hit, cells[c, at, BY - 1 :], high[c]) for c in range(4))
            return low, high

        zero = tuple(jnp.zeros((NZ, BY), F32) for _ in range(4))
        low, high = lax.fori_loop(0, BX, step, (zero, zero), unroll=4)
        for c in range(4):
            col_low[c] = low[c]
            col_high[c] = high[c]


def above_below(p):
    z = lax.broadcasted_iota(jnp.int32, p.shape, p.ndim - 2)
    above = jnp.where(z == NZ - 1, p, pltpu.roll(p, NZ - 1, p.ndim - 2))
    below = jnp.where(z == 0, p, pltpu.roll(p, 1, p.ndim - 2))
    return above, below


def star_kernel(place, cells, drag, ghost_w, ghost_e, ghost_s, ghost_n, inflow,
                star, partial, strip_s, strip_n, wide):
    @pl.when(place[0] == 1)
    def _():
        first = place[1] == 0
        last = place[1] == GX - 1
        lane = lane_index((NZ, BY))
        level = lax.broadcasted_iota(jnp.int32, (NZ, BY), 0)

        def star_row(x, west_of, east_of):
            u = cells[0, x]
            v = 0.5 * cells[1, x]
            w = 0.5 * cells[2, x]
            fast = 0.5 * (1.0 + u)
            push = drag[x] * jnp.abs(u)
            for c in range(4):
                f = cells[c, x]
                west = west_of(c)
                east = east_of(c)
                north = jnp.where(
                    lane == BY - 1,
                    pltpu.roll(ghost_n[c], BY - 1 - x, 1),
                    pltpu.roll(f, BY - 1, 1),
                )
                south = jnp.where(
                    lane == 0, pltpu.roll(ghost_s[c], (BY - x) % BY, 1), pltpu.roll(f, 1, 1)
                )
                above, below = above_below(f)
                moving = -fast * (east - west) - v * (north - south) - w * (above - below)
                mixing = 0.05 * (east + west + north + south - 4.0 * f) + 0.1 * (
                    above + below - 2.0 * f
                )
                total = moving + mixing
                if c < 3:
                    total = total - push * f
                star[c, x] = f + 0.2 * total

        star_row(
            0, lambda c: jnp.where(first, inflow[c], ghost_w[c]), lambda c: cells[c, 1]
        )

        def star_rows(x, carry):
            star_row(x, lambda c: cells[c, x - 1], lambda c: cells[c, x + 1])
            return carry

        lax.fori_loop(1, BX - 1, star_rows, 0, unroll=6)
        star_row(
            BX - 1,
            lambda c: cells[c, BX - 2],
            lambda c: jnp.where(last, cells[c, BX - 1], ghost_e[c]),
        )

        def source_row(x, west, east):
            v = star[1, x]
            north = jnp.where(lane == BY - 1, 0.0, pltpu.roll(v, BY - 1, 1))
            south = jnp.where(lane == 0, 0.0, pltpu.roll(v, 1, 1))
            w = star[2, x]
            above = jnp.where(level == NZ - 1, 0.0, pltpu.roll(w, NZ - 1, 0))
            below = jnp.where(level == 0, 0.0, pltpu.roll(w, 1, 0))
            total = -0.5 * ((east - west) + (north - south) + (above - below))
            partial[x] = total
            wide[0, x] = jnp.where(lane == HALF - 1, v[:, 0:1], total)
            wide[1, x] = jnp.where(lane == HALF, v[:, BY - 1 :], total)

        source_row(0, jnp.where(first, inflow[0], 0.0), star[0, 1])

        def source_rows(x, carry):
            source_row(x, star[0, x - 1], star[0, x + 1])
            return carry

        lax.fori_loop(1, BX - 1, source_rows, 0, unroll=6)
        source_row(BX - 1, star[0, BX - 2], jnp.where(last, star[0, BX - 1], 0.0))
        for k in range(2):
            wide[k, BX] = star[0, 0]
            wide[k, BX + 1] = star[0, BX - 1]

        def fold(k, carry):
            early_s, late_s = wide[0, k], wide[0, k + 65]
            strip_s[k] = jnp.where(lane < HALF, early_s, pltpu.roll(late_s, HALF, 1))
            early_n, late_n = wide[1, k], wide[1, k + 65]
            strip_n[k] = jnp.where(lane < HALF, pltpu.roll(early_n, HALF, 1), late_n)
            return carry

        lax.fori_loop(0, 65, fold, 0, unroll=13)


def widen_kernel(place, partial, star, from_s, from_n, whole, rims, send_w, send_e):
    @pl.when(place[0] == 1)
    def _():
        lane = lane_index((NZ, BY))
        near = lane < HALF

        def pieces(k, early, own):
            s, n = from_s[k], from_n[k]
            if early:
                n = pltpu.roll(n, HALF, 1)
            else:
                s = pltpu.roll(s, HALF, 1)
            turned = pltpu.roll(own, HALF, 1)
            return jnp.where(near, s, turned), jnp.where(near, turned, n)

        def rows(offset, early):
            def step(k, carry):
                x = k + offset
                a, b = pieces(k, early, partial[x])
                v = 0.5 * star[1, x]
                a = a + jnp.where(lane == HALF, 0.5 * a[:, 0:1], 0.0)
                a = a - jnp.where(lane == HALF - 1, v[:, 0:1], 0.0)
                b = b - jnp.where(lane == HALF - 1, 0.5 * b[:, BY - 1 :], 0.0)
                b = b + jnp.where(lane == HALF, v[:, BY - 1 :], 0.0)
                whole[x, :, :BY] = a
                whole[x, :, BY:] = b
                return carry

            return step

        lax.fori_loop(0, 65, rows(0, True), 0, unroll=5)
        lax.fori_loop(0, BX - 65, rows(65, False), 0, unroll=7)
        for k, x in ((0, 0), (1, BX - 1)):
            a, b = pieces(BX + k - 65, False, star[0, x])
            rims[k, :, :BY] = a
            rims[k, :, BY:] = b
        send_w[:HALO] = whole[:HALO]
        send_w[HALO] = rims[0]
        send_e[:HALO] = whole[BX - HALO :]
        send_e[HALO] = rims[1]


def loop_rows(start, count, body):
    trips = count // 4
    unroll = trips if trips <= 13 else max(d for d in range(1, 7) if trips % d == 0)

    def step(k, carry):
        body(start + 4 * k)
        return carry

    lax.fori_loop(0, trips, step, 0, unroll=unroll)


def pressure_kernel(place, whole, star, rims, from_w, from_e, out, b0, p0, q0, b1, q1,
                    b2, q2, b3, q3, turned):
    targets = [b0, b1, b2, b3]
    results = [q0, q1, q2, q3]

    @pl.when(place[0] == 1)
    def _():
        first = place[1] == 0
        last = place[1] == GX - 1
        b0[:HALO] = from_w[:HALO]
        b0[HALO : HALO + BX] = whole[...]
        b0[HALO + BX :] = from_e[:HALO]
        b0[HALO] = b0[HALO] + 0.5 * from_w[HALO]
        b0[HALO - 1] = b0[HALO - 1] - 0.5 * rims[0]
        b0[HALO + BX - 1] = b0[HALO + BX - 1] - 0.5 * from_e[HALO]
        b0[HALO + BX] = b0[HALO + BX] + 0.5 * rims[1]

        def ghosts(p, level):
            low = HALO >> level
            high = low + (BX >> level)

            @pl.when(first)
            def _():
                p[low - 1] = p[low]

            @pl.when(last)
            def _():
                p[high] = jnp.zeros((NZ, 2 * BY), F32)

        def around(rows, level):
            mid = rows[1:5]
            gap = 1 << level
            side = rows[2:6] + rows[0:4] + pltpu.roll(mid, 2 * BY - gap, 2) + pltpu.roll(mid, gap, 2)
            above, below = above_below(mid)
            return mid, 0.25**level * side + (above + below)

        def diagonal(level):
            return 4.0 * 0.25**level + 2.0

        def each(level, halo, body):
            loop_rows((HALO >> level) - halo, (BX >> level) + 2 * halo, body)

        def scaled(b, level):
            scale = 0.8 / diagonal(level)
            return lambda r: scale * b[pl.ds(r - 1, 6)]

        def plain(p):
            return lambda r: p[pl.ds(r - 1, 6)]

        def raised(rows_of, e):
            def rows(r):
                add = e[pl.ds(r // 2 - 1, 4)]
                add = jnp.broadcast_to(add[:, None], (4, 2, NZ, 2 * BY)).reshape(8, NZ, 2 * BY)
                return rows_of(r) + add[1:7]

            return rows

        def sweep(rows_of, q, level, halo):
            b = targets[level]
            scale = 0.8 / diagonal(level)

            def rows(r):
                mid, near = around(rows_of(r), level)
                at = pl.ds(r, 4)
                q[at] = 0.2 * mid + scale * (b[at] + near)

            each(level, halo, rows)

        def descend(rows_of, level, halo):
            b = targets[level]
            coarse = targets[level + 1]
            gap = 1 << level

            def rows(r):
                mid, near = around(rows_of(r), level)
                rest = b[pl.ds(r, 4)] - diagonal(level) * mid + near
                rest = rest.reshape(2, 2, NZ, 2 * BY)
                pair = rest[:, 0] + rest[:, 1]
                lane = lane_index(pair.shape)
                other = jnp.where(
                    (lane & gap) == 0,
                    pltpu.roll(pair, 2 * BY - gap, 2),
                    pltpu.roll(pair, gap, 2),
                )
                coarse[pl.ds(r // 2, 2)] = 0.25 * (pair + other)

            each(level, halo, rows)
            ghosts(coarse, level + 1)

        def cycle(level, rows_of, down, up):
            if level == 3:
                sweep(rows_of, q3, 3, up[3])
                return
            descend(rows_of, level, down[level])
            cycle(level + 1, scaled(targets[level + 1], level + 1), down, up)
            ghosts(results[level + 1], level + 1)
            sweep(raised(rows_of, results[level + 1]), results[level], level, up[level])

        ghosts(b0, 0)
        cycle(0, scaled(b0, 0), (46, 22, 10), (24, 16, 8, 4))
        ghosts(q0, 0)
        sweep(plain(q0), p0, 0, 24)
        ghosts(p0, 0)
        cycle(0, plain(p0), (24, 10, 4), (2, 4, 2, 2))
        ghosts(q0, 0)

        def final(k, carry):
            r = HALO + 4 * k
            rows = q0[pl.ds(r - 1, 6)]
            mid = rows[1:5]

            def inner(values, shift):
                return pltpu.roll(values, shift, 2)[:, :, :BY]

            grad_x = inner(0.5 * (rows[2:6] - rows[0:4]), 2 * BY - HALF)
            grad_y = 0.5 * (inner(mid, 2 * BY - HALF - 1) - inner(mid, 2 * BY - HALF + 1))
            above, low = above_below(mid)
            grad_z = inner(0.5 * (above - low), 2 * BY - HALF)
            at = pl.ds(4 * k, 4)
            to = pl.ds(pl.multiple_of(4 * NZ * k, 4 * NZ), 4 * NZ)
            turned[0, to] = (star[0, at] - grad_x).reshape(4 * NZ, BY)
            turned[1, to] = (star[1, at] - grad_y).reshape(4 * NZ, BY)
            turned[2, to] = (star[2, at] - grad_z).reshape(4 * NZ, BY)
            turned[3, to] = star[3, at].reshape(4 * NZ, BY)
            return carry

        lax.fori_loop(0, BX // 4, final, 0, unroll=4)
        for c in range(4):
            for z in range(NZ):
                out[c, z] = turned[c, pl.ds(z, BX, stride=NZ), :]


def in_step(*arrays):
    return lax.optimization_barrier(arrays)


AXES = ("dom", "gx", "gy")


def farm_device(gx, gy):
    return (GX + gx) * GY + gy


def along_y(step):
    return [
        (farm_device(a, b), farm_device(a, (b + step) % GY)) for a in range(GX) for b in range(GY)
    ]


def along_x(step):
    return [
        (farm_device(a, b), farm_device(a + step, b))
        for a in range(GX)
        for b in range(GY)
        if 0 <= a + step < GX
    ]


def on_device(fields, turbine_mask, inflow_source, inflow_weight):
    own = fields[0]
    dom = lax.axis_index("dom")
    place = jnp.stack([dom, lax.axis_index("gx")]).astype(jnp.int32)
    span_high, span_low = [jnp.asarray(t) for t in span_tables()]
    (sh, sl), (ah, al) = line_tables()
    sh, sl, ah, al = [jnp.asarray(t) for t in (sh, sl, ah, al)]
    block = (4, BX, NZ, BY)

    got = lax.ppermute(own[:, :, HALF:], "dom", [(0, 1)])
    ybuf, half = kernel_call(
        send_kernel, [(GY, 288, BY), (4, NZ, HALF, BY)], count=2
    )(place, own, got)
    cells, drag, row_low, row_high, col_low, col_high = kernel_call(
        turn_kernel, [(4, BX * NZ, BY), (BX * NZ, BY)] + [(4, NZ, BY)] * 4, count=2
    )(place, own, turbine_mask)
    cells = cells.reshape(block)
    drag = drag.reshape(BX, NZ, BY)
    yin = lax.all_to_all(ybuf, "gy", 0, 0, tiled=True)
    ghost_e = lax.ppermute(row_low, AXES, along_x(-1))
    ghost_w = lax.ppermute(row_high, AXES, along_x(1))
    ghost_n = lax.ppermute(col_low, AXES, along_y(-1))
    ghost_s = lax.ppermute(col_high, AXES, along_y(1))

    yin, cells, drag, ghost_e, ghost_w, ghost_n, ghost_s = in_step(
        yin, cells, drag, ghost_e, ghost_w, ghost_n, ghost_s
    )
    xbuf, blended = kernel_call(
        blend_kernel, [(32, 72, BY), (32, BY)], scalars=0, count=4
    )(half, yin, inflow_source[None], inflow_weight[None])
    xin = lax.all_to_all(xbuf, ("dom", "gx"), 0, 0, tiled=True)
    inflow_row = xin[NX // 2 // BX, HALF : HALF + 1]
    inlet = lax.ppermute(blended, AXES, [(8 * GY + b, GX * GY + b) for b in range(GY)])
    (yout,) = kernel_call(
        span_kernel,
        [(GY, 4 * HALF, BY)],
        scratch=[pltpu.VMEM((4 * HALF, NY), BF16)] * 2,
        scalars=0,
        count=3,
    )(yin, span_high, span_low)
    star, partial, strip_s, strip_n = kernel_call(
        star_kernel,
        [block, (BX, NZ, BY), (65, NZ, BY), (65, NZ, BY)],
        scratch=[pltpu.VMEM((2, BX + 2, NZ, BY), F32)],
        count=7,
    )(place, cells, drag, ghost_w, ghost_e, ghost_s, ghost_n, inlet.reshape(4, NZ, BY))
    xin, yout, star, partial, strip_s, strip_n = in_step(
        xin, yout, star, partial, strip_s, strip_n
    )
    yback = lax.all_to_all(yout, "gy", 0, 0, tiled=True)

    from_n = lax.ppermute(strip_s, AXES, along_y(-1))
    from_s = lax.ppermute(strip_n, AXES, along_y(1))
    whole, rims, send_w, send_e = kernel_call(
        widen_kernel,
        [(BX, NZ, 2 * BY), (2, NZ, 2 * BY), (HALO + 1, NZ, 2 * BY), (HALO + 1, NZ, 2 * BY)],
        count=4,
    )(place, partial, star, from_s, from_n)
    from_e = lax.ppermute(send_w, AXES, along_x(-1))
    from_w = lax.ppermute(send_e, AXES, along_x(1))

    (xout,) = kernel_call(
        line_kernel,
        [(32, HALF, BY)],
        scratch=[pltpu.VMEM((NX // 2, BY), BF16)] * 4,
        scalars=0,
        count=5,
    )(xin, sh, sl, ah, al)
    yback, xout, whole, rims, from_w, from_e = in_step(yback, xout, whole, rims, from_w, from_e)
    xback = lax.all_to_all(xout, ("dom", "gx"), 0, 0, tiled=True)
    (farm_next,) = kernel_call(
        pressure_kernel,
        [(4, NZ, BX, BY)],
        scratch=[
            pltpu.VMEM((EXT >> level, NZ, 2 * BY), F32) for level in (0, 0, 0, 1, 1, 2, 2, 3, 3)
        ]
        + [pltpu.VMEM((4, BX * NZ, BY), F32)],
        count=5,
    )(place, whole, star, rims, from_w, from_e)

    xback, farm_next = in_step(xback, farm_next)
    (mine,) = kernel_call(finish_kernel, [(4, NZ, HALF, BY)], scalars=0, count=3)(
        half, yback, xback
    )
    theirs = lax.ppermute(mine, "dom", [(1, 0)])
    combined = jnp.where(dom == 0, jnp.concatenate([mine, theirs], axis=2), farm_next)
    return combined[None], inflow_row


def solution(mesh):
    placed = (P("dom", None, None, "gx", "gy"), P(None, "gx", "gy"), P("gy"), P("gy"))
    return jax.shard_map(
        on_device,
        mesh=mesh,
        in_specs=placed,
        out_specs=(P("dom", None, None, "gx", "gy"), P(("dom", "gx"), "gy")),
        check_vma=False,
    )
```

time: 607 us -> 183 us (0.30)
  starting transfers between devices: 216 us -> 51.5 us
  other arithmetic: 149 us -> 3.03 us
  local copies, waits for them, and re-layouts: 99.8 us -> 29.3 us
  Pallas kernels: 0 us -> 54.8 us
  matrix products: 37.9 us -> 0 us
  waiting for transfers between devices: 76.2 us -> 42.7 us
  between operations: 16.6 us -> 0.97 us
    ppermute x90 -> x11, starting transfers between devices: 176 us -> 26 us  [the longest x1 4.58 us: on_device(): ghost_n = lax.ppermute(col_low, AXES, along_y(-1))]
    select_n x44 -> x0, other arithmetic: 98.2 us -> none  [the longest x6 94.5 us: derivative_rows(): jnp.where(offset == 0, 0.0, 0.5 * spacing * parity * jnp.cos(half_angle)...]
    pallas_call x0 -> x9, Pallas kernels: none -> 54.8 us  [the longest x1 20.2 us: on_device(): kernel_call(pressure_kernel, [(4, NZ, BX, BY)], scratch=[pltpu.VMEM((EXT...]
    dot_general x7 -> x0, matrix products: 37.9 us -> none  [the longest x6 36.5 us: add_block(): product = jnp.einsum(form, table_rows, operand, precision=highest)]
    ppermute x90 -> x11, waiting for transfers between devices: 55.6 us -> 38.1 us  [the longest x1 15.1 us: on_device(): from_s = lax.ppermute(strip_n, AXES, along_y(1))]
    slice x107 -> x1, local copies, waits for them, and re-layouts: 18.8 us -> 2.46 us  [on_device(): got = lax.ppermute(own[:, :, HALF:], 'dom', [(0, 1)])]
    all_to_all x6 -> x4, waiting for transfers between devices: 20.6 us -> 4.52 us  [the longest x1 4.51 us: on_device(): yin = lax.all_to_all(ybuf, 'gy', 0, 0, tiled=True)]
    all_to_all x6 -> x4, starting transfers between devices: 39.3 us -> 25.5 us  [the longest x1 7.71 us: on_device(): xin = lax.all_to_all(xbuf, ('dom', 'gx'), 0, 0, tiled=True)]
  transfers between devices with their start and end apart: 97 -> 15, of which waited for: 41 -> 6; matrix products, arithmetic and copies ran while one was open for 37% -> 1% of each run, Pallas kernels for 0% -> 28%
where the time goes in v1:
time: 183 us; the launch traced here: 182 us
  Pallas kernels  54.8 us (30%)
  starting transfers between devices  51.5 us (28%)
  waiting for transfers between devices  42.7 us (23%)
  local copies, waits for them, and re-layouts  29.3 us (16%)
  other arithmetic  3.03 us (2%)
    unnamed x66, local copies, waits for them, and re-layouts  25.7 us
    pallas_call x1, Pallas kernels, on_device(): kernel_call(pressure_kernel, [(4, NZ, BX, BY)], scratch=[pltpu.VMEM((EXT...  20.2 us
    ppermute x1, waiting for transfers between devices, on_device(): from_s = lax.ppermute(strip_n, AXES, along_y(1))  15.1 us
    pallas_call x1, Pallas kernels, on_device(): kernel_call(line_kernel, [(32, HALF, BY)], scratch=[pltpu.VMEM((NX // 2,...  10.1 us
    ppermute x1, waiting for transfers between devices, on_device(): lax.ppermute(blended, AXES, [(8 * GY + b, GX * GY + b) for b in range(GY)])  9.64 us
    all_to_all x1, starting transfers between devices, on_device(): xin = lax.all_to_all(xbuf, ('dom', 'gx'), 0, 0, tiled=True)  7.71 us
    ppermute x1, waiting for transfers between devices, on_device(): ghost_n = lax.ppermute(col_low, AXES, along_y(-1))  7.67 us
    all_to_all x1, starting transfers between devices, on_device(): xback = lax.all_to_all(xout, ('dom', 'gx'), 0, 0, tiled=True)  7.31 us
  transfers between devices with their start and end apart: 15, of which 6 were waited for; matrix products, arithmetic and copies ran while one was open for 1% of the time, Pallas kernels for 28%

profile of v1, /device:TPU:1, one launch (start us, length us, event | category | flops | bytes accessed | tf_op | source)
XLA Modules:
  0.0 182.2 jit_solution(6290868328064423133)
XLA Ops:
  0.6 2.5 %slice.8 = f32[4,8,64,128]{3,2,1,0:T(8,128)} slice(f32[4,8,128,128]{3,2,1,0:T(8,128)} %bitcast.12), slice={[0:4], [0:8], [64:128], [0:128]} | slice | bytes 2097152 | tf_op jit(solution)/shard_map/slice | solution.py:555
  3.1 1.3 collective-permute-start
  4.5 5.5 %collective-permute-done.got = f32[4,8,64,128]{3,2,1,0:T(8,128)S(1)} collective-permute-done((f32[4,8,64,128]{3,2,1,0:T(8,128)}, f32[4,8,64,128]{3,2,1,0:T(8,128)S(1)}, u32[]{:S(2)}, u32[]{:S(2)}) %collective-permute-start) | collective-permute-done | bytes 1048608 | tf_op jit(solution)/shard_map/ppermute | solution.py:555
  10.0 1.0 copy-done.18
  10.9 1.2 copy-done.19
  12.9 1.0 copy-done.3
  13.9 1.1 copy-done.14
  14.9 6.9 %all-to-all-start = ((f32[8,288,128]{2,1,0:T(8,128)}), f32[8,288,128]{2,1,0:T(8,128)S(1)}, u32[]{:S(2)}, u32[]{:S(2)}) async-start(f32[8,288,128]{2,1,0:T(8,128)} %copy-done.14), calls=%async_computation | async-start | bytes 2359296 | tf_op jit(solution)/shard_map/all_to_all | solution.py:564
  21.8 1.0 copy-done.20
  22.9 4.9 %shard_map.114 = (f32[4,1024,128]{2,1,0:T(8,128)S(1)}, f32[1024,128]{1,0:T(8,128)S(1)}, f32[4,8,128]{2,1,0:T(8,128)S(1)}, f32[4,8,128]{2,1,0:T(8,128)S(1)}, f32[...) custom-call(s32[2]{0:T(128)S(1)} %pad_add_fusion.place, f32[4,8,128,128]{3,2,1,0:T(8,128)S(1)} %bitcast.14, ...), custom_call_target="tpu_custom_call" | custom-call | tf_op jit(solution)/shard_map/pallas_call | solution.py:559
  27.8 1.3 copy-done.8
  29.9 1.3 collective-permute-start.1
  31.2 4.0 %collective-permute-start.2 = (f32[4,8,128]{2,1,0:T(8,128)S(1)}, f32[4,8,128]{2,1,0:T(8,128)S(1)}, u32[]{:S(2)}, u32[]{:S(2)}) collective-permute-start(f32[4,8,128]{2,1,0:T(8,128)S(1)} %get-tuple-element.46), channel_id=1, source_target_pairs={{128,136},{129,137},{130,138},{131,139},{132,140},{133,141},{134,1... | collective-permute-start | bytes 49160 | tf_op jit(solution)/shard_map/ppermute | solution.py:566
  35.2 4.6 %collective-permute-start.3 = (f32[4,8,128]{2,1,0:T(8,128)S(1)}, f32[4,8,128]{2,1,0:T(8,128)S(1)}, u32[]{:S(2)}, u32[]{:S(2)}) collective-permute-start(f32[4,8,128]{2,1,0:T(8,128)S(1)} %get-tuple-element.47), channel_id=1, source_target_pairs={{128,135},{129,128},{130,129},{131,130},{132,131},{133,132},{134,1... | collective-permute-start | bytes 49160 | tf_op jit(solution)/shard_map/ppermute | solution.py:567
  39.8 1.9 %collective-permute-start.4 = (f32[4,8,128]{2,1,0:T(8,128)S(1)}, f32[4,8,128]{2,1,0:T(8,128)S(1)}, u32[]{:S(2)}, u32[]{:S(2)}) collective-permute-start(f32[4,8,128]{2,1,0:T(8,128)S(1)} %get-tuple-element.48), channel_id=1, source_target_pairs={{128,129},{129,130},{130,131},{131,132},{132,133},{133,134},{134,1... | collective-permute-start | bytes 49160 | tf_op jit(solution)/shard_map/ppermute | solution.py:568
  41.7 7.7 %collective-permute-done.3.ghost_n = f32[4,8,128]{2,1,0:T(8,128)S(1)} collective-permute-done((f32[4,8,128]{2,1,0:T(8,128)S(1)}, f32[4,8,128]{2,1,0:T(8,128)S(1)}, u32[]{:S(2)}, u32[]{:S(2)}) %collective-permute-start.3) | collective-permute-done | bytes 16416 | tf_op jit(solution)/shard_map/ppermute | solution.py:567
  49.4 4.5 %all-to-all-done.yin = f32[8,288,128]{2,1,0:T(8,128)S(1)} async-done(((f32[8,288,128]{2,1,0:T(8,128)}), f32[8,288,128]{2,1,0:T(8,128)S(1)}, u32[]{:S(2)}, u32[]{:S(2)}) %all-to-all-start) | async-done | bytes 1179680 | tf_op jit(solution)/shard_map/all_to_all | solution.py:564
  53.9 1.2 copy-done.4
  56.1 1.0 copy-done.15
  57.1 7.7 %all-to-all-start.1 = ((f32[32,72,128]{2,1,0:T(8,128)}), f32[32,72,128]{2,1,0:T(8,128)}, u32[]{:S(2)}, u32[]{:S(2)}) async-start(f32[32,72,128]{2,1,0:T(8,128)} %copy-done.15), calls=%async_computation.1 | async-start | bytes 2359296 | tf_op jit(solution)/shard_map/all_to_all | solution.py:576
  64.8 1.4 collective-permute-start.5
  66.3 1.5 copy-done.13
  67.7 4.5 %shard_map.116 = f32[8,256,128]{2,1,0:T(8,128)} custom-call(f32[8,288,128]{2,1,0:T(8,128)S(1)} %all-to-all-done.yin, bf16[1792,512]{1,0:T(8,128)(2,1)S(1)} %copy-done.13, bf16[1792,512]{1,0:T(8,128)(2,1)S(1)} %copy-done.12), custom_call_target="tpu_custom_call" | custom-call | tf_op jit(solution)/shard_map/pallas_call | solution.py:579
  72.3 9.6 %collective-permute-done.5 = f32[32,128]{1,0:T(8,128)S(1)} collective-permute-done((f32[32,128]{1,0:T(8,128)S(1)}, f32[32,128]{1,0:T(8,128)S(1)}, u32[]{:S(2)}, u32[]{:S(2)}) %collective-permute-start.5) | collective-permute-done | bytes 16416 | tf_op jit(solution)/shard_map/ppermute | solution.py:578
  81.9 7.2 %shard_map.117 = (f32[4,128,8,128]{3,2,1,0:T(8,128)S(1)}, f32[128,8,128]{2,1,0:T(8,128)S(1)}, f32[65,8,128]{2,1,0:T(8,128)S(1)}, f32[65,8,128]{2,1,0:T(8,128)S(1)}) custom-call(s32[2]{0:T(128)S(1)} %pad_add_fusion.place, f32[4,128,8,128]{3,2,1,0:T(8,128)S(1)} %bitcast.15, f32[128,8,128]{2,1,0:T(8,128)S(1)} %bitcast.16, ...), custom_call_target="tpu_custom_call" | custom-call | tf_op jit(solution)/shard_map/pallas_call | solution.py:586
  91.4 3.6 %all-to-all-start.2 = ((f32[8,256,128]{2,1,0:T(8,128)}), f32[8,256,128]{2,1,0:T(8,128)S(1)}, u32[]{:S(2)}, u32[]{:S(2)}) async-start(f32[8,256,128]{2,1,0:T(8,128)} %shard_map.116), calls=%async_computation.2 | async-start | bytes 2097152 | tf_op jit(solution)/shard_map/all_to_all | solution.py:595
  94.9 3.4 %collective-permute-start.6 = (f32[65,8,128]{2,1,0:T(8,128)}, f32[65,8,128]{2,1,0:T(8,128)S(1)}, u32[]{:S(2)}, u32[]{:S(2)}) collective-permute-start(f32[65,8,128]{2,1,0:T(8,128)} %copy-done.32), channel_id=1, source_target_pairs={{128,129},{129,130},{130,131},{131,132},{132,133},{133,134},{134,1... | collective-permute-start | bytes 798728 | tf_op jit(solution)/shard_map/ppermute | solution.py:598
  98.3 3.2 %collective-permute-start.7 = (f32[65,8,128]{2,1,0:T(8,128)}, f32[65,8,128]{2,1,0:T(8,128)S(1)}, u32[]{:S(2)}, u32[]{:S(2)}) collective-permute-start(f32[65,8,128]{2,1,0:T(8,128)} %copy-done.31), channel_id=1, source_target_pairs={{128,135},{129,128},{130,129},{131,130},{132,131},{133,132},{134,1... | collective-permute-start | bytes 798728 | tf_op jit(solution)/shard_map/ppermute | solution.py:597
  101.6 15.1 %collective-permute-done.6.from_s = f32[65,8,128]{2,1,0:T(8,128)S(1)} collective-permute-done((f32[65,8,128]{2,1,0:T(8,128)}, f32[65,8,128]{2,1,0:T(8,128)S(1)}, u32[]{:S(2)}, u32[]{:S(2)}) %collective-permute-start.6) | collective-permute-done | bytes 266272 | tf_op jit(solution)/shard_map/ppermute | solution.py:598
  116.7 1.0 copy-done.24
  117.7 4.1 %shard_map.119 = (f32[128,8,256]{2,1,0:T(8,128)S(1)}, f32[2,8,256]{2,1,0:T(8,128)S(1)}, f32[49,8,256]{2,1,0:T(8,128)S(1)}, f32[49,8,256]{2,1,0:T(8,128)S(1)}) custom-call(s32[2]{0:T(128)S(1)} %pad_add_fusion.place, f32[128,8,128]{2,1,0:T(8,128)S(1)} %copy-done.24, f32[4,128,8,128]{3,2,1,0:T(8,128)S(1)} %get-tuple-element.65.star, ...), custom_call_target="tpu_custom_call" | custom-call | tf_op jit(solution)/shard_map/pallas_call | solution.py:599
  121.8 1.0 copy-done.16
  122.8 1.3 collective-permute-start.8
  124.2 1.3 collective-permute-start.9
  125.5 1.5 copy-done.11
  127.0 10.1 %shard_map.118 = f32[32,64,128]{2,1,0:T(8,128)} custom-call(f32[32,72,128]{2,1,0:T(8,128)} %all-to-all-done.1.xin, bf16[512,1792]{1,0:T(8,128)(2,1)S(1)} %copy-done.11, bf16[512,1792]{1,0:T(8,128)(2,1)S(1)} %copy-done.10, bf16[512,1792]{1,0:T(8,128)(2,1)} %constant.30.clone.ah, bf16[512,1792]{1,0:T(8,128)(2,1)} %constant.31.clone.al), custom_call_target="tpu_custom_call" | custom-call | tf_op jit(solution)/shard_map/pallas_call | solution.py:607
  138.6 7.3 %all-to-all-start.3 = ((f32[32,64,128]{2,1,0:T(8,128)}), f32[32,64,128]{2,1,0:T(8,128)}, u32[]{:S(2)}, u32[]{:S(2)}) async-start(f32[32,64,128]{2,1,0:T(8,128)} %shard_map.118), calls=%async_computation.3 | async-start | bytes 2097152 | tf_op jit(solution)/shard_map/all_to_all | solution.py:615
  145.9 1.6 copy-done.2
  147.5 1.2 copy-done.17
  148.7 1.0 copy-done.26
  149.7 1.0 copy-done.28
  150.7 20.2 %shard_map.120 = f32[4,8,128,128]{3,2,1,0:T(8,128)S(1)} custom-call(s32[2]{0:T(128)S(1)} %pad_add_fusion.place, f32[128,8,256]{2,1,0:T(8,128)S(1)} %copy-done.17, f32[4,128,8,128]{3,2,1,0:T(8,128)S(1)} %copy-done.2, f32[2,8,256]{2,1,0:T(8,128)S(1)} %get-tuple-element.75.rims, f32[49,8,256]{2,1,0:T(8,128)S(1)} %copy-done.26, f32[49,8,256]{2,1,0:T(8,128)S(1)} %copy-done.28), custom_call_target="tpu_custom_call" | custom-call | tf_op jit(solution)/shard_map/pallas_call | solution.py:616
  170.9 1.2 copy-done.5
  172.2 1.2 copy-done.7
  173.4 2.2 %shard_map.121 = f32[4,8,64,128]{3,2,1,0:T(8,128)S(1)} custom-call(f32[4,8,64,128]{3,2,1,0:T(8,128)S(1)} %copy-done.5, f32[8,256,128]{2,1,0:T(8,128)S(1)} %copy-done.7, f32[32,64,128]{2,1,0:T(8,128)} %all-to-all-done.3.xback), custom_call_target="tpu_custom_call" | custom-call | tf_op jit(solution)/shard_map/pallas_call | solution.py:627
  175.6 2.3 %collective-permute-start.10 = (f32[4,8,64,128]{3,2,1,0:T(8,128)S(1)}, f32[4,8,64,128]{3,2,1,0:T(8,128)}, u32[]{:S(2)}, u32[]{:S(2)}) collective-permute-start(f32[4,8,64,128]{3,2,1,0:T(8,128)S(1)} %shard_map.121), channel_id=1, source_target_pairs={{128,0},{129,1},{130,2},{131,3},{132,4},{133,5},{134,6},{135,7},{1... | collective-permute-start | bytes 3145736 | tf_op jit(solution)/shard_map/ppermute | solution.py:630
  177.9 1.2 slice_bitcast_fusion
  179.3 3.0 %fusion = f32[1,4,8,128,128]{4,3,2,1,0:T(8,128)} fusion(f32[4,8,128,128]{3,2,1,0:T(8,128)S(1)} %shard_map.120, f32[4,8,64,128]{3,2,1,0:T(8,128)} %collective-permute-done.10, f32[4,8,64,128]{3,2,1,0:T(8,128)S(1)} %shard_map.121, pred[]{:T(512)S(6)} %eq.3), kind=kLoop, calls=%fused_computation.1 | loop fusion | flops 1048576 | bytes 6291457 | tf_op jit(solution)/shard_map/broadcast_in_dim | solution.py:632
  (61 shorter events, 6.6 us)
Async XLA Ops:
  0.6 10.3 %copy-start = (f32[1,4,8,128,128]{4,3,2,1,0:T(8,128)S(1)}, f32[1,4,8,128,128]{4,3,2,1,0:T(8,128)}, u32[]{:S(2)}) copy-start(f32[1,4,8,128,128]{4,3,2,1,0:T(8,128)} %param.10) | copy-start | bytes 6291460
  3.1 6.9 %collective-permute-start = (f32[4,8,64,128]{3,2,1,0:T(8,128)}, f32[4,8,64,128]{3,2,1,0:T(8,128)S(1)}, u32[]{:S(2)}, u32[]{:S(2)}) collective-permute-start(f32[4,8,64,128]{3,2,1,0:T(8,128)} %slice.8), channel_id=1, source_target_pairs={{0,128},{1,129},{2,130},{3,131},{4,132},{5,133},{6,134},{7,135},{8... | collective-permute-start | bytes 3145736 | tf_op jit(solution)/shard_map/ppermute | solution.py:555
  10.0 1.0 copy-start.18
  10.9 1.2 copy-start.19
  12.9 1.0 copy-start.3
  13.9 1.1 copy-start.14
  14.9 39.0 %all-to-all-start = ((f32[8,288,128]{2,1,0:T(8,128)}), f32[8,288,128]{2,1,0:T(8,128)S(1)}, u32[]{:S(2)}, u32[]{:S(2)}) async-start(f32[8,288,128]{2,1,0:T(8,128)} %copy-done.14), calls=%async_computation | async-start | bytes 2359296 | tf_op jit(solution)/shard_map/all_to_all | solution.py:564
  21.8 1.0 copy-start.20
  22.9 31.0 %copy-start.29 = (s32[128]{0:T(128)S(1)}, s32[128]{0:T(128)}, u32[]{:S(2)}) copy-start(s32[128]{0:T(128)} %param.12) | copy-start | bytes 1540
  22.9 31.0 %copy-start.30 = (s32[128]{0:T(128)S(1)}, s32[128]{0:T(128)}, u32[]{:S(2)}) copy-start(s32[128]{0:T(128)} %param.13) | copy-start | bytes 1540
  27.7 1.3 copy-start.8
  29.1 0.8 copy-start.21
  29.9 11.8 %collective-permute-start.1 = (f32[4,8,128]{2,1,0:T(8,128)S(1)}, f32[4,8,128]{2,1,0:T(8,128)S(1)}, u32[]{:S(2)}, u32[]{:S(2)}) collective-permute-start(f32[4,8,128]{2,1,0:T(8,128)S(1)} %get-tuple-element.45), channel_id=1, source_target_pairs={{136,128},{137,129},{138,130},{139,131},{140,132},{141,133},{142,1... | collective-permute-start | bytes 49160 | tf_op jit(solution)/shard_map/ppermute | solution.py:565
  31.2 10.5 %collective-permute-start.2 = (f32[4,8,128]{2,1,0:T(8,128)S(1)}, f32[4,8,128]{2,1,0:T(8,128)S(1)}, u32[]{:S(2)}, u32[]{:S(2)}) collective-permute-start(f32[4,8,128]{2,1,0:T(8,128)S(1)} %get-tuple-element.46), channel_id=1, source_target_pairs={{128,136},{129,137},{130,138},{131,139},{132,140},{133,141},{134,1... | collective-permute-start | bytes 49160 | tf_op jit(solution)/shard_map/ppermute | solution.py:566
  35.2 14.2 %collective-permute-start.3 = (f32[4,8,128]{2,1,0:T(8,128)S(1)}, f32[4,8,128]{2,1,0:T(8,128)S(1)}, u32[]{:S(2)}, u32[]{:S(2)}) collective-permute-start(f32[4,8,128]{2,1,0:T(8,128)S(1)} %get-tuple-element.47), channel_id=1, source_target_pairs={{128,135},{129,128},{130,129},{131,130},{132,131},{133,132},{134,1... | collective-permute-start | bytes 49160 | tf_op jit(solution)/shard_map/ppermute | solution.py:567
  39.8 9.6 %collective-permute-start.4 = (f32[4,8,128]{2,1,0:T(8,128)S(1)}, f32[4,8,128]{2,1,0:T(8,128)S(1)}, u32[]{:S(2)}, u32[]{:S(2)}) collective-permute-start(f32[4,8,128]{2,1,0:T(8,128)S(1)} %get-tuple-element.48), channel_id=1, source_target_pairs={{128,129},{129,130},{130,131},{131,132},{132,133},{133,134},{134,1... | collective-permute-start | bytes 49160 | tf_op jit(solution)/shard_map/ppermute | solution.py:568
  53.9 1.2 copy-start.4
  55.1 11.1 %copy-start.12 = (bf16[1792,512]{1,0:T(8,128)(2,1)S(1)}, bf16[1792,512]{1,0:T(8,128)(2,1)}, u32[]{:S(2)}) copy-start(bf16[1792,512]{1,0:T(8,128)(2,1)} %constant.27.clone.table_low) | copy-start | bytes 5505028
  56.1 1.0 copy-start.15
  57.1 34.3 %all-to-all-start.1 = ((f32[32,72,128]{2,1,0:T(8,128)}), f32[32,72,128]{2,1,0:T(8,128)}, u32[]{:S(2)}, u32[]{:S(2)}) async-start(f32[32,72,128]{2,1,0:T(8,128)} %copy-done.15), calls=%async_computation.1 | async-start | bytes 2359296 | tf_op jit(solution)/shard_map/all_to_all | solution.py:576
  64.8 17.2 %copy-start.9 = (f32[4,1024,128]{2,1,0:T(8,128)S(1)}, f32[4,1024,128]{2,1,0:T(8,128)}, u32[]{:S(2)}) copy-start(f32[4,1024,128]{2,1,0:T(8,128)} %copy-done.8) | copy-start | bytes 6291460
  64.8 17.1 %collective-permute-start.5 = (f32[32,128]{1,0:T(8,128)S(1)}, f32[32,128]{1,0:T(8,128)S(1)}, u32[]{:S(2)}, u32[]{:S(2)}) collective-permute-start(f32[32,128]{1,0:T(8,128)S(1)} %get-tuple-element.57), channel_id=1, source_target_pairs={{64,128},{65,129},{66,130},{67,131},{68,132},{69,133},{70,134},{71... | collective-permute-start | bytes 49160 | tf_op jit(solution)/shard_map/ppermute | solution.py:578
  66.2 1.5 copy-start.13
  67.7 14.2 %copy-start.22 = (f32[1024,128]{1,0:T(8,128)S(1)}, f32[1024,128]{1,0:T(8,128)}, u32[]{:S(2)}) copy-start(f32[1024,128]{1,0:T(8,128)} %copy-done.21) | copy-start | bytes 1572868
  89.1 0.8 copy-start.23
  89.9 0.7 copy-start.31
  90.7 0.7 copy-start.32
  91.4 30.5 %copy-start.1 = (f32[4,128,8,128]{3,2,1,0:T(8,128)}, f32[4,128,8,128]{3,2,1,0:T(8,128)S(1)}, u32[]{:S(2)}) copy-start(f32[4,128,8,128]{3,2,1,0:T(8,128)S(1)} %get-tuple-element.65.star) | copy-start | bytes 6291460
  91.4 47.2 %all-to-all-start.2 = ((f32[8,256,128]{2,1,0:T(8,128)}), f32[8,256,128]{2,1,0:T(8,128)S(1)}, u32[]{:S(2)}, u32[]{:S(2)}) async-start(f32[8,256,128]{2,1,0:T(8,128)} %shard_map.116), calls=%async_computation.2 | async-start | bytes 2097152 | tf_op jit(solution)/shard_map/all_to_all | solution.py:595
  94.9 30.5 %copy-start.10 = (bf16[512,1792]{1,0:T(8,128)(2,1)S(1)}, bf16[512,1792]{1,0:T(8,128)(2,1)}, u32[]{:S(2)}) copy-start(bf16[512,1792]{1,0:T(8,128)(2,1)} %constant.29.clone.sl) | copy-start | bytes 5505028
  94.9 21.7 %collective-permute-start.6 = (f32[65,8,128]{2,1,0:T(8,128)}, f32[65,8,128]{2,1,0:T(8,128)S(1)}, u32[]{:S(2)}, u32[]{:S(2)}) collective-permute-start(f32[65,8,128]{2,1,0:T(8,128)} %copy-done.32), channel_id=1, source_target_pairs={{128,129},{129,130},{130,131},{131,132},{132,133},{133,134},{134,1... | collective-permute-start | bytes 798728 | tf_op jit(solution)/shard_map/ppermute | solution.py:598
  98.3 18.3 %collective-permute-start.7 = (f32[65,8,128]{2,1,0:T(8,128)}, f32[65,8,128]{2,1,0:T(8,128)S(1)}, u32[]{:S(2)}, u32[]{:S(2)}) collective-permute-start(f32[65,8,128]{2,1,0:T(8,128)} %copy-done.31), channel_id=1, source_target_pairs={{128,135},{129,128},{130,129},{131,130},{132,131},{133,132},{134,1... | collective-permute-start | bytes 798728 | tf_op jit(solution)/shard_map/ppermute | solution.py:597
  116.7 1.0 copy-start.24
  121.8 1.0 copy-start.16
  122.8 14.3 %collective-permute-start.8 = (f32[49,8,256]{2,1,0:T(8,128)S(1)}, f32[49,8,256]{2,1,0:T(8,128)S(1)}, u32[]{:S(2)}, u32[]{:S(2)}) collective-permute-start(f32[49,8,256]{2,1,0:T(8,128)S(1)} %get-tuple-element.70), channel_id=1, source_target_pairs={{128,136},{129,137},{130,138},{131,139},{132,140},{133,141},{134,1... | collective-permute-start | bytes 1204232 | tf_op jit(solution)/shard_map/ppermute | solution.py:605
  124.2 13.7 %collective-permute-start.9 = (f32[49,8,256]{2,1,0:T(8,128)S(1)}, f32[49,8,256]{2,1,0:T(8,128)S(1)}, u32[]{:S(2)}, u32[]{:S(2)}) collective-permute-start(f32[49,8,256]{2,1,0:T(8,128)S(1)} %get-tuple-element.71), channel_id=1, source_target_pairs={{136,128},{137,129},{138,130},{139,131},{140,132},{141,133},{142,1... | collective-permute-start | bytes 1204232 | tf_op jit(solution)/shard_map/ppermute | solution.py:604
  125.5 1.5 copy-start.11
  137.1 0.7 copy-start.25
  137.8 0.8 copy-start.27
  138.6 32.3 %copy-start.6 = (f32[8,256,128]{2,1,0:T(8,128)}, f32[8,256,128]{2,1,0:T(8,128)S(1)}, u32[]{:S(2)}) copy-start(f32[8,256,128]{2,1,0:T(8,128)S(1)} %all-to-all-done.2.yback) | copy-start | bytes 3145732
  138.6 32.3 %all-to-all-start.3 = ((f32[32,64,128]{2,1,0:T(8,128)}), f32[32,64,128]{2,1,0:T(8,128)}, u32[]{:S(2)}, u32[]{:S(2)}) async-start(f32[32,64,128]{2,1,0:T(8,128)} %shard_map.118), calls=%async_computation.3 | async-start | bytes 2097152 | tf_op jit(solution)/shard_map/all_to_all | solution.py:615
  145.9 1.6 copy-start.2
  147.5 1.2 copy-start.17
  148.7 1.0 copy-start.26
  149.7 1.0 copy-start.28
  170.9 1.2 copy-start.5
  172.1 1.2 copy-start.7
  175.6 3.7 %collective-permute-start.10 = (f32[4,8,64,128]{3,2,1,0:T(8,128)S(1)}, f32[4,8,64,128]{3,2,1,0:T(8,128)}, u32[]{:S(2)}, u32[]{:S(2)}) collective-permute-start(f32[4,8,64,128]{3,2,1,0:T(8,128)S(1)} %shard_map.121), channel_id=1, source_target_pairs={{128,0},{129,1},{130,2},{131,3},{132,4},{133,5},{134,6},{135,7},{1... | collective-permute-start | bytes 3145736 | tf_op jit(solution)/shard_map/ppermute | solution.py:630

commit v2 on v0

v2 whole, which is shorter than its diff:
```python
import functools

import jax
import jax.numpy as jnp
import ml_dtypes
import numpy as np
from jax import lax
from jax.experimental import pallas as pl
from jax.experimental.pallas import tpu as pltpu
from jax.sharding import PartitionSpec as P

NX = 2048
NY = 1024
NZ = 8
BX = 128
BY = 128
HALF = 64
GX = 16
GY = 8
HALO = 48
FX = 64
FOLD = FX // 2 + 1
EXT = FX + 2 * HALO
F32 = jnp.float32
BF16 = jnp.bfloat16
VMEM_BYTES = 63 * 1024 * 1024


def table_entries(length):
    offset = np.arange(length, dtype=np.float64)
    spacing = 2.0 * np.pi / length
    sign = np.where(offset % 2 == 0, 1.0, -1.0)
    angle = np.pi * offset / length
    angle[0] = 1.0
    slope = 0.5 * spacing * sign * np.cos(angle) / np.sin(angle)
    bend = -0.5 * spacing * spacing * sign / np.sin(angle) ** 2
    slope[0] = 0.0
    bend[0] = -np.pi**2 / 3.0 - spacing * spacing / 6.0
    return -0.2 * slope, 0.2 * 0.05 * bend


def split_bf16(table):
    high = table.astype(np.float32).astype(ml_dtypes.bfloat16)
    low = (table - high.astype(np.float64)).astype(np.float32).astype(ml_dtypes.bfloat16)
    return high, low


def span_tables():
    tiles = []
    i = np.arange(256)
    for d in (3, 2, 1, 0):
        index = (256 * d + i[None, :] - i[:, None]) % NY
        tiles.append(np.concatenate([entry[index] for entry in table_entries(NY)], axis=1))
    return split_bf16(np.concatenate(tiles, axis=0))


def line_tables():
    i = np.arange(256)
    both = []
    for sign in (1.0, -1.0):
        tiles = []
        for d in (3, 2, 1, 0):
            index = 256 * d + i[:, None] - i[None, :]
            tiles.append(
                np.concatenate(
                    [
                        0.5 * (entry[index % NX] + sign * entry[(index + NX // 2) % NX])
                        for entry in table_entries(NX)
                    ],
                    axis=0,
                )
            )
        both.append(split_bf16(np.concatenate(tiles, axis=1)))
    return both


def staged_call(body, ins, outs, scratch=(), gate=None, late=()):
    n, m, k = len(ins), len(outs), len(scratch)

    def kernel(place, *refs):
        far_in, far_out = refs[:n], refs[n : n + m]
        near_in = refs[n + m : 2 * n + m]
        near_out = refs[2 * n + m : 2 * n + 2 * m]
        extra = refs[2 * n + 2 * m : 2 * n + 2 * m + k]
        sem_in, sem_out = refs[2 * n + 2 * m + k :]

        def run():
            loads = [
                pltpu.make_async_copy(far_in[i], near_in[i], sem_in.at[i]) for i in range(n)
            ]
            for load in loads:
                load.start()
            for i in range(n):
                if i not in late:
                    loads[i].wait()
            waits = [loads[i].wait for i in late]
            body(place, *waits, *near_in, *near_out, *extra)
            stores = [
                pltpu.make_async_copy(near_out[i], far_out[i], sem_out.at[i]) for i in range(m)
            ]
            for store in stores:
                store.start()
            for store in stores:
                store.wait()

        if gate is None:
            run()
        else:
            pl.when(place[0] == gate)(run)

    return raw_call(
        kernel,
        n,
        outs,
        [pltpu.VMEM(x.shape, x.dtype) for x in ins]
        + [pltpu.VMEM(shape, F32) for shape in outs]
        + list(scratch)
        + [pltpu.SemaphoreType.DMA((n,)), pltpu.SemaphoreType.DMA((m,))],
    )


def raw_call(kernel, count, outs, scratch, aliases=None):
    return pl.pallas_call(
        kernel,
        out_shape=[jax.ShapeDtypeStruct(shape, F32) for shape in outs],
        in_specs=[pl.BlockSpec(memory_space=pltpu.SMEM)]
        + [pl.BlockSpec(memory_space=pl.ANY)] * count,
        out_specs=[pl.BlockSpec(memory_space=pl.ANY)] * len(outs),
        scratch_shapes=list(scratch),
        input_output_aliases=aliases or {},
        compiler_params=pltpu.CompilerParams(vmem_limit_bytes=VMEM_BYTES),
    )


def near_call(body, outs, limit, scratch=()):
    def call(place, *operands):
        return pl.pallas_call(
            body,
            out_shape=[jax.ShapeDtypeStruct(shape, F32) for shape in outs],
            in_specs=[pl.BlockSpec(memory_space=pltpu.SMEM)]
            + [pl.BlockSpec(memory_space=pltpu.VMEM)] * len(operands),
            out_specs=[pl.BlockSpec(memory_space=pltpu.VMEM)] * len(outs),
            scratch_shapes=list(scratch),
            compiler_params=pltpu.CompilerParams(vmem_limit_bytes=limit * 1024 * 1024),
        )(place, *operands)

    return call


def lane_index(shape):
    return lax.broadcasted_iota(jnp.int32, shape, len(shape) - 1)


def halves(values):
    high = values.astype(BF16)
    return high, (values - high.astype(F32)).astype(BF16)


def lead_kernel(place, own, other, column):
    @pl.when(place[0] == 0)
    def _():
        other[...] = own[:, :, HALF:]

    @pl.when(place[0] == 1)
    def _():
        other[...] = own[:, :, :HALF]

    column[...] = own[:, :, 0, :]


def load_half(place, own, got, half, sem):
    @pl.when(place[0] == 0)
    def _():
        copy = pltpu.make_async_copy(own.at[:, :, pl.ds(0, HALF)], half, sem)
        copy.start()
        copy.wait()

    @pl.when(place[0] == 1)
    def _():
        copy = pltpu.make_async_copy(got, half, sem)
        copy.start()
        copy.wait()


def run_all(copies):
    for copy in copies:
        copy.start()
    return copies


def wait_all(copies):
    for copy in copies:
        copy.wait()


def send_kernel(place, own, got, column, ybuf):
    def fill(half):
        for z in range(NZ):
            for c in range(4):
                ybuf[z, c * HALF : (c + 1) * HALF] = half(c, z)

    pl.when(place[0] == 0)(lambda: fill(lambda c, z: own[c, z, :HALF]))
    pl.when(place[0] == 1)(lambda: fill(lambda c, z: got[c, z]))
    for c in range(4):
        piece = jnp.where(place[1] == 0, column[c], own[c, :, 0, :])
        for g in range(GY):
            ybuf[g, 4 * HALF + c * NZ : 4 * HALF + (c + 1) * NZ] = piece


def pack_kernel(place, own, got, xbuf_far, half, xbuf, sem):
    load_half(place, own, got, half, sem.at[8])
    lane = lane_index((HALF, BY))
    stores = []
    for z in range(NZ):
        for part in range(4):
            total = None
            for c in range(4):
                shift = 32 * ((c - part) % 4)
                moved = half[c, z] if shift == 0 else pltpu.roll(half[c, z], shift, 1)
                total = moved if total is None else jnp.where(lane >= 32 * c, moved, total)
            xbuf[4 * z + part] = total
        tiles = pl.ds(4 * z, 4)
        stores += run_all(
            [
                pltpu.make_async_copy(
                    xbuf.at[tiles], xbuf_far.at[tiles, pl.ds(0, HALF)], sem.at[z]
                )
            ]
        )
    wait_all(stores)


def blend_kernel(place, yin, source, weight, xbuf_in, xbuf_far, inflow_far,
                 planes, first_near, weight_near, rims, inflow, sem):
    loads = run_all(
        [
            pltpu.make_async_copy(source, first_near, sem.at[0]),
            pltpu.make_async_copy(weight, weight_near, sem.at[1]),
            pltpu.make_async_copy(yin.at[:, pl.ds(4 * HALF, 4 * NZ)], planes, sem.at[2]),
        ]
    )
    wait_all(loads[:2])
    rows = lax.broadcasted_iota(jnp.int32, (NY, BY), 0)
    share = weight_near[...].astype(F32) / 16.0
    first = first_near[...]
    follow = jnp.where(first == NY - 1, 0, first + 1)
    table = jnp.where(rows == first, share, 0.0) + jnp.where(rows == follow, 1.0 - share, 0.0)
    wait_all(loads[2:])
    plane = jnp.concatenate([planes[g] for g in range(GY)], axis=1)
    blended = jnp.dot(plane, table, precision=lax.Precision.HIGHEST, preferred_element_type=F32)
    inflow[...] = blended
    for r in range(4 * NZ):
        rims[r] = jnp.broadcast_to(blended[r : r + 1], (8, BY))
    wait_all(
        run_all(
            [
                pltpu.make_async_copy(rims, xbuf_far.at[:, pl.ds(HALF, 8)], sem.at[3]),
                pltpu.make_async_copy(inflow, inflow_far, sem.at[4]),
            ]
        )
    )


def span_kernel(place, yin, table_high, table_low, yout, both):
    lines = 4 * HALF
    for g in range(GY):
        at = slice(g * BY, (g + 1) * BY)
        both[:lines, at], both[lines:, at] = halves(yin[g, :lines])
    for i in range(4):
        near = (slice(0, (i + 1) * 256), slice((3 - i) * 256, 1024))
        far = (slice((i + 1) * 256, 1024), slice(0, (3 - i) * 256))
        value = None
        for cells, rows in (near, far)[: 1 if i == 3 else 2]:
            pair = jnp.dot(both[:, cells], table_high[rows], preferred_element_type=F32)
            part = pair[:lines] + pair[lines:]
            part += jnp.dot(both[:lines, cells], table_low[rows], preferred_element_type=F32)
            value = part if value is None else value + part
        for k in range(2):
            g = 2 * i + k
            v = yin[g, HALF : 2 * HALF]
            for c in range(4):
                rows = slice(c * HALF, (c + 1) * HALF)
                yout[g, rows] = (
                    v * value[rows, k * BY : (k + 1) * BY]
                    + value[rows, 256 + k * BY : 256 + (k + 1) * BY]
                )


def chunk_place(m):
    return (m % 2) * GX + m // 2


def line_kernel(place, r0, r1, r2, r3, xin, sh, sl, ah, al, xout, inflow_row, plus, minus):
    inflow_row[...] = xin[NX // 2 // BX, HALF : HALF + 1]
    for m in range(16):
        a = xin[chunk_place(m), :HALF]
        b = xin[chunk_place(m + 16), :HALF]
        rows = slice(m * HALF, (m + 1) * HALF)
        plus[rows, :BY], plus[rows, BY:] = halves(a + b)
        minus[rows, :BY], minus[rows, BY:] = halves(a - b)
    for ready in (r0, r1, r2, r3):
        ready()
    lane = lane_index((HALF, BY))
    for i in range(4):

        def product(table_high, table_low, both, cells, columns):
            pair = jnp.dot(table_high[:, columns], both[cells], preferred_element_type=F32)
            value = pair[:, :BY] + pair[:, BY:]
            return value + jnp.dot(
                table_low[:, columns], both[cells, :BY], preferred_element_type=F32
            )

        near = (slice(0, (i + 1) * 256), slice((3 - i) * 256, 1024))
        far = (slice((i + 1) * 256, 1024), slice(0, (3 - i) * 256))
        even = product(sh, sl, plus, *near)
        odd = product(ah, al, minus, *near)
        if i < 3:
            even = even + product(sh, sl, plus, *far)
            odd = odd - product(ah, al, minus, *far)
        for k in range(4):
            for side, value in ((0, even + odd), (1, even - odd)):
                place_of = chunk_place(4 * i + k + 16 * side)
                u = jnp.where(lane < 32, xin[place_of, :HALF], 0.0)
                u = u + pltpu.roll(u, 32, 1)
                u = u + pltpu.roll(u, 64, 1)
                rows = slice(k * HALF, (k + 1) * HALF)
                late = slice(256 + k * HALF, 256 + (k + 1) * HALF)
                xout[place_of] = (1.0 + u) * value[rows] + value[late]


def finish_kernel(place, own, got, yback_far, xback_far, joined_in, send_in, joined, send,
                  half, yback, xback, out, sem):
    loads = [
        run_all(
            [
                pltpu.make_async_copy(
                    yback_far.at[pl.ds(2 * k, 2)], yback.at[pl.ds(2 * k, 2)], sem.at[1 + k]
                ),
                pltpu.make_async_copy(
                    xback_far.at[pl.ds(8 * k, 8)], xback.at[pl.ds(8 * k, 8)], sem.at[5 + k]
                ),
            ]
        )
        for k in range(4)
    ]
    load_half(place, own, got, half, sem.at[0])
    lane = lane_index((HALF, BY))
    to_own, to_other = [], []
    for k in range(4):
        at = pl.ds(2 * k, 2)
        piece = out.at[:, at]
        to_own.append(
            pltpu.make_async_copy(piece, joined.at[:, at, pl.ds(0, HALF)], sem.at[9 + k])
        )
        to_other.append(pltpu.make_async_copy(piece, send.at[:, at], sem.at[9 + k]))
    for k in range(4):
        wait_all(loads[k])
        for z in (2 * k, 2 * k + 1):
            for c in range(4):
                total = None
                for part in range(4):
                    shift = 32 * ((part - c) % 4)
                    tile = xback[4 * z + part]
                    moved = tile if shift == 0 else pltpu.roll(tile, shift, 1)
                    total = moved if total is None else jnp.where(lane >= 32 * part, moved, total)
                q = half[c, z]
                upper = half[c, min(z + 1, NZ - 1)]
                lower = half[c, max(z - 1, 0)]
                mixed = 0.02 * (upper + lower - 2.0 * q) - 0.1 * half[2, z] * (upper - lower)
                out[c, z] = q + total + yback[z, c * HALF : (c + 1) * HALF] + mixed
        pl.when(place[0] == 0)(to_own[k].start)
        pl.when(place[0] == 1)(to_other[k].start)
    pl.when(place[0] == 0)(lambda: wait_all(to_own))
    pl.when(place[0] == 1)(lambda: wait_all(to_other))


def join_kernel(place, theirs, joined_in, joined, near, sem):
    def forward(start):
        pieces = [
            (
                pltpu.make_async_copy(theirs.at[c], near.at[c], sem.at[c]),
                pltpu.make_async_copy(
                    near.at[c], joined.at[c, :, pl.ds(start, HALF)], sem.at[4 + c]
                ),
            )
            for c in range(4)
        ]
        for load, _ in pieces:
            load.start()
        for load, store in pieces:
            load.wait()
            store.start()
        for _, store in pieces:
            store.wait()

    pl.when(place[0] == 0)(lambda: forward(HALF))
    pl.when(place[0] == 1)(lambda: forward(0))


def turn_kernel(place, own, got, mask_far, cells_far, drag_far, row_low_far, row_high_far,
                col_low_far, col_high_far,
                farm, mask, cells, drag, row_low, row_high, col_low, col_high, sem):
    at_x = pl.ds(pl.multiple_of(place[0] * FX, FX), FX)
    mask_load = pltpu.make_async_copy(mask_far.at[:, at_x], mask, sem.at[1])
    mask_load.start()

    @pl.when(place[0] == 0)
    def _():
        copy = pltpu.make_async_copy(got, farm, sem.at[0])
        copy.start()
        copy.wait()

    @pl.when(place[0] == 1)
    def _():
        copy = pltpu.make_async_copy(own.at[:, :, pl.ds(FX, FX)], farm, sem.at[0])
        copy.start()
        copy.wait()

    stores = []
    for c in range(4):
        for z in range(NZ):
            cells[c, pl.ds(z, FX, stride=NZ), :] = farm[c, z]
        stores += run_all([pltpu.make_async_copy(cells.at[c], cells_far.at[c], sem.at[2 + c])])
    mask_load.wait()
    for z in range(NZ):
        drag[pl.ds(z, FX, stride=NZ), :] = mask[z].astype(F32)
    stores += run_all([pltpu.make_async_copy(drag, drag_far, sem.at[6])])
    for c in range(4):
        row_low[c] = cells[c, :NZ]
        row_high[c] = cells[c, (FX - 1) * NZ :]
    lane = lane_index((NZ, BY))

    def step(x, carry):
        low, high = carry
        hit = lane == x
        at = pl.ds(pl.multiple_of(x * NZ, NZ), NZ)
        low = tuple(jnp.where(hit, cells[c, at, 0:1], low[c]) for c in range(4))
        high = tuple(jnp.where(hit, cells[c, at, BY - 1 :], high[c]) for c in range(4))
        return low, high

    zero = tuple(jnp.zeros((NZ, BY), F32) for _ in range(4))
    low, high = lax.fori_loop(0, FX, step, (zero, zero), unroll=4)
    for c in range(4):
        col_low[c] = low[c]
        col_high[c] = high[c]
    pairs = (
        (row_low, row_low_far), (row_high, row_high_far),
        (col_low, col_low_far), (col_high, col_high_far),
    )
    stores += run_all([pltpu.make_async_copy(a, b, sem.at[7 + k]) for k, (a, b) in enumerate(pairs)])
    wait_all(stores)


def above_below(p):
    z = lax.broadcasted_iota(jnp.int32, p.shape, p.ndim - 2)
    above = jnp.where(z == NZ - 1, p, pltpu.roll(p, NZ - 1, p.ndim - 2))
    below = jnp.where(z == 0, p, pltpu.roll(p, 1, p.ndim - 2))
    return above, below


def star_kernel(place, cells, drag, ghost_w, ghost_e, ghost_s, ghost_n, inflow,
                star, partial, strip_s, strip_n, wide):
    first = place[2] == 1
    last = place[3] == 1
    lane = lane_index((NZ, BY))
    level = lax.broadcasted_iota(jnp.int32, (NZ, BY), 0)

    def star_row(x, west_of, east_of):
        u = cells[0, x]
        v = 0.5 * cells[1, x]
        w = 0.5 * cells[2, x]
        fast = 0.5 * (1.0 + u)
        push = drag[x] * jnp.abs(u)
        for c in range(4):
            f = cells[c, x]
            west = west_of(c)
            east = east_of(c)
            north = jnp.where(
                lane == BY - 1,
                pltpu.roll(ghost_n[c], BY - 1 - x, 1),
                pltpu.roll(f, BY - 1, 1),
            )
            south = jnp.where(
                lane == 0, pltpu.roll(ghost_s[c], (BY - x) % BY, 1), pltpu.roll(f, 1, 1)
            )
            above, below = above_below(f)
            moving = -fast * (east - west) - v * (north - south) - w * (above - below)
            mixing = 0.05 * (east + west + north + south - 4.0 * f) + 0.1 * (
                above + below - 2.0 * f
            )
            total = moving + mixing
            if c < 3:
                total = total - push * f
            star[c, x] = f + 0.2 * total

    star_row(
        0, lambda c: jnp.where(first, inflow[c], ghost_w[c]), lambda c: cells[c, 1]
    )

    def star_rows(x, carry):
        star_row(x, lambda c: cells[c, x - 1], lambda c: cells[c, x + 1])
        return carry

    lax.fori_loop(1, FX - 1, star_rows, 0, unroll=2)
    star_row(
        FX - 1,
        lambda c: cells[c, FX - 2],
        lambda c: jnp.where(last, cells[c, FX - 1], ghost_e[c]),
    )

    def source_row(x, west, east):
        v = star[1, x]
        north = jnp.where(lane == BY - 1, 0.0, pltpu.roll(v, BY - 1, 1))
        south = jnp.where(lane == 0, 0.0, pltpu.roll(v, 1, 1))
        w = star[2, x]
        above = jnp.where(level == NZ - 1, 0.0, pltpu.roll(w, NZ - 1, 0))
        below = jnp.where(level == 0, 0.0, pltpu.roll(w, 1, 0))
        total = -0.5 * ((east - west) + (north - south) + (above - below))
        partial[x] = total
        wide[0, x] = jnp.where(lane == HALF - 1, v[:, 0:1], total)
        wide[1, x] = jnp.where(lane == HALF, v[:, BY - 1 :], total)

    source_row(0, jnp.where(first, inflow[0], 0.0), star[0, 1])

    def source_rows(x, carry):
        source_row(x, star[0, x - 1], star[0, x + 1])
        return carry

    lax.fori_loop(1, FX - 1, source_rows, 0, unroll=2)
    source_row(FX - 1, star[0, FX - 2], jnp.where(last, star[0, FX - 1], 0.0))
    for k in range(2):
        wide[k, FX] = star[0, 0]
        wide[k, FX + 1] = star[0, FX - 1]

    def fold(k, carry):
        early_s, late_s = wide[0, k], wide[0, k + FOLD]
        strip_s[k] = jnp.where(lane < HALF, early_s, pltpu.roll(late_s, HALF, 1))
        early_n, late_n = wide[1, k], wide[1, k + FOLD]
        strip_n[k] = jnp.where(lane < HALF, pltpu.roll(early_n, HALF, 1), late_n)
        return carry

    lax.fori_loop(0, FOLD, fold, 0, unroll=11)


def widen_kernel(place, partial, star, from_s, from_n, whole, rims, send_w, send_e):
    lane = lane_index((NZ, BY))
    near = lane < HALF

    def pieces(k, early, own):
        s, n = from_s[k], from_n[k]
        if early:
            n = pltpu.roll(n, HALF, 1)
        else:
            s = pltpu.roll(s, HALF, 1)
        turned = pltpu.roll(own, HALF, 1)
        return jnp.where(near, s, turned), jnp.where(near, turned, n)

    def rows(offset, early):
        def step(k, carry):
            x = k + offset
            a, b = pieces(k, early, partial[x])
            v = 0.5 * star[1, x]
            a = a + jnp.where(lane == HALF, 0.5 * a[:, 0:1], 0.0)
            a = a - jnp.where(lane == HALF - 1, v[:, 0:1], 0.0)
            b = b - jnp.where(lane == HALF - 1, 0.5 * b[:, BY - 1 :], 0.0)
            b = b + jnp.where(lane == HALF, v[:, BY - 1 :], 0.0)
            whole[x, :, :BY] = a
            whole[x, :, BY:] = b
            return carry

        return step

    for k in range(2):
        a, b = pieces(FX + k - FOLD, False, star[0, k * (FX - 1)])
        rims[k, :, :BY] = a
        rims[k, :, BY:] = b
    lax.fori_loop(0, FOLD, rows(0, True), 0, unroll=11)
    lax.fori_loop(0, FX - FOLD, rows(FOLD, False), 0, unroll=31)
    send_w[:HALO] = whole[:HALO]
    send_w[HALO] = rims[0]
    send_e[:HALO] = whole[FX - HALO :]
    send_e[HALO] = rims[1]


def loop_rows(start, count, body):
    trips = count // 4
    unroll = trips if trips <= 19 else max(d for d in range(1, 8) if trips % d == 0)

    def step(k, carry):
        body(start + 4 * k)
        return carry

    lax.fori_loop(0, trips, step, 0, unroll=unroll)


def pressure_kernel(place, whole_far, star_far, rims_far, from_w_far, from_e_far, joined, send,
                  star, rims, far_rims, out, b0, p0, q0, b1, q1, b2, q2, b3, q3, turned, sem):
    pairs = (
        (from_w_far.at[pl.ds(0, HALO)], b0.at[pl.ds(0, HALO)]),
        (whole_far, b0.at[pl.ds(HALO, FX)]),
        (from_e_far.at[pl.ds(0, HALO)], b0.at[pl.ds(HALO + FX, HALO)]),
        (rims_far, rims),
        (from_w_far.at[HALO], far_rims.at[0]),
        (from_e_far.at[HALO], far_rims.at[1]),
    )
    loads = run_all([pltpu.make_async_copy(a, b, sem.at[k]) for k, (a, b) in enumerate(pairs)])
    (star_load,) = run_all([pltpu.make_async_copy(star_far, star, sem.at[6])])
    wait_all(loads)
    targets = [b0, b1, b2, b3]
    results = [q0, q1, q2, q3]

    first = place[2] == 1
    last = place[3] == 1
    b0[HALO] = b0[HALO] + 0.5 * far_rims[0]
    b0[HALO - 1] = b0[HALO - 1] - 0.5 * rims[0]
    b0[HALO + FX - 1] = b0[HALO + FX - 1] - 0.5 * far_rims[1]
    b0[HALO + FX] = b0[HALO + FX] + 0.5 * rims[1]

    def ghosts(p, level):
        low = HALO >> level
        high = low + (FX >> level)

        @pl.when(first)
        def _():
            p[low - 1] = p[low]

        @pl.when(last)
        def _():
            p[high] = jnp.zeros((NZ, 2 * BY), F32)

    def around(rows, level):
        mid = rows[1:5]
        gap = 1 << level
        side = rows[2:6] + rows[0:4] + pltpu.roll(mid, 2 * BY - gap, 2) + pltpu.roll(mid, gap, 2)
        above, below = above_below(mid)
        return mid, 0.25**level * side + (above + below)

    def diagonal(level):
        return 4.0 * 0.25**level + 2.0

    def each(level, halo, body):
        loop_rows((HALO >> level) - halo, (FX >> level) + 2 * halo, body)

    def scaled(b, level):
        scale = 0.8 / diagonal(level)
        return lambda r: scale * b[pl.ds(r - 1, 6)]

    def plain(p):
        return lambda r: p[pl.ds(r - 1, 6)]

    def raised(rows_of, e):
        def rows(r):
            add = e[pl.ds(r // 2 - 1, 4)]
            add = jnp.broadcast_to(add[:, None], (4, 2, NZ, 2 * BY)).reshape(8, NZ, 2 * BY)
            return rows_of(r) + add[1:7]

        return rows

    def sweep(rows_of, q, level, halo):
        b = targets[level]
        scale = 0.8 / diagonal(level)

        def rows(r):
            mid, near = around(rows_of(r), level)
            at = pl.ds(r, 4)
            q[at] = 0.2 * mid + scale * (b[at] + near)

        each(level, halo, rows)

    def descend(rows_of, level, halo):
        b = targets[level]
        coarse = targets[level + 1]
        gap = 1 << level

        def rows(r):
            mid, near = around(rows_of(r), level)
            rest = b[pl.ds(r, 4)] - diagonal(level) * mid + near
            rest = rest.reshape(2, 2, NZ, 2 * BY)
            pair = rest[:, 0] + rest[:, 1]
            lane = lane_index(pair.shape)
            other = jnp.where(
                (lane & gap) == 0,
                pltpu.roll(pair, 2 * BY - gap, 2),
                pltpu.roll(pair, gap, 2),
            )
            coarse[pl.ds(r // 2, 2)] = 0.25 * (pair + other)

        each(level, halo, rows)
        ghosts(coarse, level + 1)

    def cycle(level, rows_of, down, up):
        if level == 3:
            sweep(rows_of, q3, 3, up[3])
            return
        descend(rows_of, level, down[level])
        cycle(level + 1, scaled(targets[level + 1], level + 1), down, up)
        ghosts(results[level + 1], level + 1)
        sweep(raised(rows_of, results[level + 1]), results[level], level, up[level])

    ghosts(b0, 0)
    cycle(0, scaled(b0, 0), (46, 22, 10), (24, 14, 8, 4))
    ghosts(q0, 0)
    sweep(plain(q0), p0, 0, 24)
    ghosts(p0, 0)
    cycle(0, plain(p0), (24, 10, 4), (4, 2, 2, 2))
    ghosts(q0, 0)

    def final(k, carry):
        r = HALO + 4 * k
        rows = q0[pl.ds(r - 1, 6)]
        mid = rows[1:5]

        def inner(values, shift):
            return pltpu.roll(values, shift, 2)[:, :, :BY]

        grad_x = inner(0.5 * (rows[2:6] - rows[0:4]), 2 * BY - HALF)
        grad_y = 0.5 * (inner(mid, 2 * BY - HALF - 1) - inner(mid, 2 * BY - HALF + 1))
        above, low = above_below(mid)
        grad_z = inner(0.5 * (above - low), 2 * BY - HALF)
        at = pl.ds(4 * k, 4)
        to = pl.ds(pl.multiple_of(4 * NZ * k, 4 * NZ), 4 * NZ)
        turned[0, to] = (star[0, at] - grad_x).reshape(4 * NZ, BY)
        turned[1, to] = (star[1, at] - grad_y).reshape(4 * NZ, BY)
        turned[2, to] = (star[2, at] - grad_z).reshape(4 * NZ, BY)
        turned[3, to] = star[3, at].reshape(4 * NZ, BY)
        return carry

    star_load.wait()
    lax.fori_loop(0, FX // 4, final, 0, unroll=4)
    stores = []
    for c in range(4):
        for z in range(NZ):
            out[c, z] = turned[c, pl.ds(z, FX, stride=NZ), :]
        to_own = pltpu.make_async_copy(out.at[c], joined.at[c, :, pl.ds(FX, FX)], sem.at[7 + c])
        to_other = pltpu.make_async_copy(out.at[c], send.at[c], sem.at[7 + c])
        pl.when(place[0] == 1)(to_own.start)
        pl.when(place[0] == 0)(to_other.start)
        stores.append((to_own, to_other))
    for to_own, to_other in stores:
        pl.when(place[0] == 1)(to_own.wait)
        pl.when(place[0] == 0)(to_other.wait)


def in_step(*arrays):
    return lax.optimization_barrier(arrays)


def along_y(step):
    return [(b, (b + step) % GY) for b in range(GY)]


def along_x(step):
    count = 2 * GX
    return [
        (chunk_place(m), chunk_place(m + step)) for m in range(count) if 0 <= m + step < count
    ]


def vmem(*shapes):
    return [pltpu.VMEM(shape, F32) for shape in shapes]


def on_device(fields, turbine_mask, inflow_source, inflow_weight):
    own = fields[0]
    dom, gx = lax.axis_index("dom"), lax.axis_index("gx")
    first, last = (gx == 0) & (dom == 0), (gx == GX - 1) & (dom == 1)
    place = jnp.stack([dom, gx, first, last]).astype(jnp.int32)
    span_high, span_low = [jnp.asarray(t) for t in span_tables()]
    (sh, sl), (ah, al) = line_tables()
    sh, sl, ah, al = [jnp.asarray(t) for t in (sh, sl, ah, al)]
    block = (4, FX, NZ, BY)
    half_block = (4, NZ, HALF, BY)
    rim = (4, NZ, BY)
    strip = (FOLD, NZ, BY)
    wide_row = (NZ, 2 * BY)
    dma = pltpu.SemaphoreType.DMA
    swap = [(0, 1), (1, 0)]
    x_axes = ("dom", "gx")

    other, column = near_call(lead_kernel, [half_block, rim], 2)(place, own)
    column = lax.ppermute(column, "gx", [(NX // 2 // BX, 0)])
    got = lax.ppermute(other, "dom", swap)
    (ybuf,) = near_call(send_kernel, [(GY, 288, BY)], 2)(place, own, got, column)
    yin = lax.all_to_all(ybuf, "gy", 0, 0, tiled=True)

    cells, drag, row_low, row_high, col_low, col_high = raw_call(
        turn_kernel,
        3,
        [(4, FX * NZ, BY), (FX * NZ, BY)] + [rim] * 4,
        vmem(half_block)
        + [pltpu.VMEM((NZ, FX, BY), jnp.int32)]
        + vmem((4, FX * NZ, BY), (FX * NZ, BY), rim, rim, rim, rim)
        + [dma((11,))],
    )(place, own, got, turbine_mask)
    cells = cells.reshape(block)
    drag = drag.reshape(FX, NZ, BY)
    ghost_e = lax.ppermute(row_low, x_axes, along_x(-1))
    ghost_w = lax.ppermute(row_high, x_axes, along_x(1))
    ghost_n = lax.ppermute(col_low, "gy", along_y(-1))
    ghost_s = lax.ppermute(col_high, "gy", along_y(1))
    (xbuf,) = raw_call(
        pack_kernel, 2, [(32, 72, BY)], vmem(half_block, (32, HALF, BY)) + [dma((9,))]
    )(place, own, got)

    yin, xbuf, cells, drag, ghost_e, ghost_w, ghost_n, ghost_s = in_step(
        yin, xbuf, cells, drag, ghost_e, ghost_w, ghost_n, ghost_s
    )
    xbuf, blended = raw_call(
        blend_kernel,
        4,
        [(32, 72, BY), (4 * NZ, BY)],
        vmem((GY, 4 * NZ, BY))
        + [pltpu.VMEM((1, BY), jnp.int32)] * 2
        + vmem((32, 8, BY), (4 * NZ, BY))
        + [dma((5,))],
        {4: 0},
    )(place, yin, inflow_source[None], inflow_weight[None], xbuf)
    xin = lax.all_to_all(xbuf, x_axes, 0, 0, tiled=True)

    outs = [block, (FX, NZ, BY), strip, strip]
    star, partial, strip_s, strip_n = near_call(
        star_kernel, outs, 4, vmem((2, FX + 2, NZ, BY))
    )(place, cells, drag, ghost_w, ghost_e, ghost_s, ghost_n, blended.reshape(rim))
    from_n = lax.ppermute(strip_s, "gy", along_y(-1))
    from_s = lax.ppermute(strip_n, "gy", along_y(1))
    (yout,) = near_call(
        span_kernel, [(GY, 4 * HALF, BY)], 8, [pltpu.VMEM((8 * HALF, NY), BF16)]
    )(place, yin, span_high, span_low)
    yout, from_n, from_s = in_step(yout, from_n, from_s)
    whole, rims, send_w, send_e = near_call(
        widen_kernel,
        [(FX, *wide_row), (2, *wide_row), (HALO + 1, *wide_row), (HALO + 1, *wide_row)],
        2,
    )(place, partial, star, from_s, from_n)
    xin, yout, whole, rims, send_w, send_e = in_step(xin, yout, whole, rims, send_w, send_e)
    yback = lax.all_to_all(yout, "gy", 0, 0, tiled=True)

    from_e = lax.ppermute(send_w, x_axes, along_x(-1))
    from_w = lax.ppermute(send_e, x_axes, along_x(1))
    ins = (xin, sh, sl, ah, al)
    xout, inflow_row = staged_call(
        line_kernel,
        ins,
        [(32, HALF, BY), (1, BY)],
        scratch=[pltpu.VMEM((NX // 2, 2 * BY), BF16)] * 2,
        late=(1, 2, 3, 4),
    )(place, *ins)
    yback, xout, from_w, from_e = in_step(yback, xout, from_w, from_e)
    xback = lax.all_to_all(xout, x_axes, 0, 0, tiled=True)
    joined, send = raw_call(
        pressure_kernel,
        5,
        [(4, NZ, BX, BY), half_block],
        vmem(block, (2, *wide_row), (2, *wide_row), half_block)
        + vmem(*[(EXT >> level, *wide_row) for level in (0, 0, 0, 1, 1, 2, 2, 3, 3)])
        + vmem((4, FX * NZ, BY))
        + [dma((11,))],
    )(place, whole, star, rims, from_w, from_e)

    xback, joined, send = in_step(xback, joined, send)
    joined, send = raw_call(
        finish_kernel,
        6,
        [(4, NZ, BX, BY), half_block],
        vmem(half_block, (GY, 4 * HALF, BY), (32, HALF, BY), half_block) + [dma((13,))],
        {5: 0, 6: 1},
    )(place, own, got, yback, xback, joined, send)
    theirs = lax.ppermute(send, "dom", swap)
    (joined,) = raw_call(
        join_kernel, 2, [(4, NZ, BX, BY)], vmem(half_block) + [dma((8,))], {2: 0}
    )(place, theirs, joined)
    return joined[None], inflow_row


def solution(mesh):
    placed = (P("dom", None, None, "gx", "gy"), P(None, "gx", "gy"), P("gy"), P("gy"))
    return jax.shard_map(
        on_device,
        mesh=mesh,
        in_specs=placed,
        out_specs=(P("dom", None, None, "gx", "gy"), P(("dom", "gx"), "gy")),
        check_vma=False,
    )
```

time: 607 us -> 150 us (0.25)
  starting transfers between devices: 216 us -> 47.4 us
  other arithmetic: 149 us -> 0.08 us
  local copies, waits for them, and re-layouts: 99.8 us -> 4.79 us
  Pallas kernels: 0 us -> 59 us
  waiting for transfers between devices: 76.2 us -> 36.4 us
  matrix products: 37.9 us -> 0 us
  between operations: 16.6 us -> 1.08 us
    ppermute x90 -> x11, starting transfers between devices: 176 us -> 21.8 us  [the longest x1 4 us: on_device(): from_w = lax.ppermute(send_e, x_axes, along_x(1))]
    select_n x44 -> x0, other arithmetic: 98.2 us -> none  [the longest x6 94.5 us: derivative_rows(): jnp.where(offset == 0, 0.0, 0.5 * spacing * parity * jnp.cos(half_angle)...]
    pallas_call x0 -> x12, Pallas kernels: none -> 59 us  [the longest x5 17.1 us: call(): pl.pallas_call(body, out_shape=[jax.ShapeDtypeStruct(shape, F32) for shap...]
    ppermute x90 -> x11, waiting for transfers between devices: 55.6 us -> 15.5 us  [the longest x1 8.14 us: on_device(): ghost_n = lax.ppermute(col_low, 'gy', along_y(-1))]
    dot_general x7 -> x0, matrix products: 37.9 us -> none  [the longest x6 36.5 us: add_block(): product = jnp.einsum(form, table_rows, operand, precision=highest)]
    unnamed x59 -> x24, local copies, waits for them, and re-layouts: 31.5 us -> 4.79 us
    slice x107 -> x0, local copies, waits for them, and re-layouts: 18.8 us -> none  [the longest x1 3.91 us: face_cells(): west_cells = padded[..., :-2, 1:-1]]
    all_to_all x6 -> x4, starting transfers between devices: 39.3 us -> 25.7 us  [the longest x1 9.74 us: on_device(): xback = lax.all_to_all(xout, x_axes, 0, 0, tiled=True)]
  transfers between devices with their start and end apart: 97 -> 15, of which waited for: 41 -> 6; matrix products, arithmetic and copies ran while one was open for 37% -> 0% of each run, Pallas kernels for 0% -> 31%
where the time goes in v2:
time: 150 us; the launch traced here: 149 us
  Pallas kernels  59 us (39%)
  starting transfers between devices  47.4 us (32%)
  waiting for transfers between devices  36.4 us (24%)
  local copies, waits for them, and re-layouts  4.79 us (3%)
    pallas_call x5, Pallas kernels, call(): pl.pallas_call(body, out_shape=[jax.ShapeDtypeStruct(shape, F32) for shap...  17.1 us
    pallas_call x1, Pallas kernels, on_device(): raw_call(pressure_kernel, 5, [(4, NZ, BX, BY), half_block], vmem(block, (...  14.9 us
    all_to_all x1, waiting for transfers between devices, on_device(): yback = lax.all_to_all(yout, 'gy', 0, 0, tiled=True)  12.1 us
    all_to_all x1, starting transfers between devices, on_device(): xback = lax.all_to_all(xout, x_axes, 0, 0, tiled=True)  9.74 us
    pallas_call x1, Pallas kernels, on_device(): staged_call(line_kernel, ins, [(32, HALF, BY), (1, BY)], scratch=[pltpu.V...  8.81 us
    ppermute x1, waiting for transfers between devices, on_device(): ghost_n = lax.ppermute(col_low, 'gy', along_y(-1))  8.14 us
    all_to_all x1, waiting for transfers between devices, on_device(): yin = lax.all_to_all(ybuf, 'gy', 0, 0, tiled=True)  7.17 us
    all_to_all x1, starting transfers between devices, on_device(): yin = lax.all_to_all(ybuf, 'gy', 0, 0, tiled=True)  6.45 us
  transfers between devices with their start and end apart: 15, of which 6 were waited for; matrix products, arithmetic and copies ran while one was open for 0% of the time, Pallas kernels for 31%

profile of v2, /device:TPU:1, one launch (start us, length us, event | category | flops | bytes accessed | tf_op | source)
XLA Modules:
  0.0 148.8 jit_solution(16607333642965886518)
XLA Ops:
  0.6 0.1 pad_add_fusion.place
  0.7 1.6 %copy-done = f32[1,4,8,128,128]{4,3,2,1,0:T(8,128)S(1)} copy-done((f32[1,4,8,128,128]{4,3,2,1,0:T(8,128)S(1)}, f32[1,4,8,128,128]{4,3,2,1,0:T(8,128)}, u32[]{:S(2)}) %copy-start) | copy-done | bytes 2097176
  2.3 0.6 shard_map.113
  3.0 3.3 %collective-permute-start = (f32[4,8,64,128]{3,2,1,0:T(8,128)S(1)}, f32[4,8,64,128]{3,2,1,0:T(8,128)S(1)}, u32[]{:S(2)}, u32[]{:S(2)}) collective-permute-start(f32[4,8,64,128]{3,2,1,0:T(8,128)S(1)} %get-tuple-element.50), channel_id=1, source_target_pairs={{0,128},{128,0},{1,129},{129,1},{2,130},{130,2},{3,131},{131,3},{4... | collective-permute-start | bytes 3145736 | tf_op jit(solution)/shard_map/ppermute | solution.py:782
  6.3 1.3 collective-permute-start.1
  7.6 4.7 %collective-permute-done.1.column = f32[4,8,128]{2,1,0:T(8,128)S(1)} collective-permute-done((f32[4,8,128]{2,1,0:T(8,128)S(1)}, f32[4,8,128]{2,1,0:T(8,128)S(1)}, u32[]{:S(2)}, u32[]{:S(2)}) %collective-permute-start.1) | collective-permute-done | bytes 16416 | tf_op jit(solution)/shard_map/ppermute | solution.py:781
  12.3 0.0 collective-permute-done.got
  12.3 1.7 %shard_map.114 = f32[8,288,128]{2,1,0:T(8,128)} custom-call(s32[4]{0:T(128)S(1)} %pad_add_fusion.place, f32[4,8,128,128]{3,2,1,0:T(8,128)S(1)} %bitcast.15, f32[4,8,64,128]{3,2,1,0:T(8,128)S(1)} %collective-permute-done.got, f32[4,8,128]{2,1,0:T(8,128)S(1)} %collective-permute-done.1.column), custom_call_target="tpu_custom_call" | custom-call | tf_op jit(solution)/shard_map/pallas_call | solution.py:137
  13.9 1.0 copy-done.1
  14.9 6.5 %all-to-all-start = ((f32[8,288,128]{2,1,0:T(8,128)}), f32[8,288,128]{2,1,0:T(8,128)}, u32[]{:S(2)}, u32[]{:S(2)}) async-start(f32[8,288,128]{2,1,0:T(8,128)} %shard_map.114), calls=%async_computation | async-start | bytes 2359296 | tf_op jit(solution)/shard_map/all_to_all | solution.py:784
  21.4 4.8 %shard_map.116 = (f32[4,512,128]{2,1,0:T(8,128)}, f32[512,128]{1,0:T(8,128)}, f32[4,8,128]{2,1,0:T(8,128)}, f32[4,8,128]{2,1,0:T(8,128)}, f32[4,8,128]{2,1,0:T(8,128)}, /*index=5*/f32[4,8,128]{2,1,0:T(8,128)}) custom-call(s32[4]{0:T(128)} %copy-done.8, f32[4,8,128,128]{3,2,1,0:T(8,128)} %bitcast.11, f32[4,8,64,128]{3,2,1,0:T(8,128)} %copy-done.1, ...), custom_call_target="tpu_custom_call" | custom-call | tf_op jit(solution)/shard_map/pallas_call | solution.py:786
  26.1 3.4 %collective-permute-start.2 = (f32[4,8,128]{2,1,0:T(8,128)}, f32[4,8,128]{2,1,0:T(8,128)S(1)}, u32[]{:S(2)}, u32[]{:S(2)}) collective-permute-start(f32[4,8,128]{2,1,0:T(8,128)} %get-tuple-element.54), channel_id=1, source_target_pairs={{128,0},{8,128},{136,8},{16,136},{144,16},{24,144},{152,24},{32,15... | collective-permute-start | bytes 49160 | tf_op jit(solution)/shard_map/ppermute | solution.py:797
  29.5 2.2 %collective-permute-start.3 = (f32[4,8,128]{2,1,0:T(8,128)}, f32[4,8,128]{2,1,0:T(8,128)S(1)}, u32[]{:S(2)}, u32[]{:S(2)}) collective-permute-start(f32[4,8,128]{2,1,0:T(8,128)} %get-tuple-element.55), channel_id=1, source_target_pairs={{0,128},{128,8},{8,136},{136,16},{16,144},{144,24},{24,152},{152,3... | collective-permute-start | bytes 49160 | tf_op jit(solution)/shard_map/ppermute | solution.py:798
  31.7 2.8 %collective-permute-start.4 = (f32[4,8,128]{2,1,0:T(8,128)}, f32[4,8,128]{2,1,0:T(8,128)S(1)}, u32[]{:S(2)}, u32[]{:S(2)}) collective-permute-start(f32[4,8,128]{2,1,0:T(8,128)} %get-tuple-element.56), channel_id=1, source_target_pairs={{0,7},{1,0},{2,1},{3,2},{4,3},{5,4},{6,5},{7,6},{8,15},{9,8},{10,9... | collective-permute-start | bytes 49160 | tf_op jit(solution)/shard_map/ppermute | solution.py:799
  34.5 0.0 collective-permute-start.5
  34.5 3.5 %shard_map.115.xbuf_in = f32[32,72,128]{2,1,0:T(8,128)} custom-call(s32[4]{0:T(128)} %copy-done.8, f32[4,8,128,128]{3,2,1,0:T(8,128)} %bitcast.12, f32[4,8,64,128]{3,2,1,0:T(8,128)} %copy-done.1), custom_call_target="tpu_custom_call" | custom-call | tf_op jit(solution)/shard_map/pallas_call | solution.py:801
  38.0 0.0 collective-permute-done.2.ghost_e
  38.0 0.0 collective-permute-done.3.ghost_w
  38.0 8.1 %collective-permute-done.4.ghost_n = f32[4,8,128]{2,1,0:T(8,128)S(1)} collective-permute-done((f32[4,8,128]{2,1,0:T(8,128)}, f32[4,8,128]{2,1,0:T(8,128)S(1)}, u32[]{:S(2)}, u32[]{:S(2)}) %collective-permute-start.4) | collective-permute-done | bytes 16416 | tf_op jit(solution)/shard_map/ppermute | solution.py:799
  46.1 0.0 collective-permute-done.5.ghost_s
  46.2 7.2 %all-to-all-done.yin = f32[8,288,128]{2,1,0:T(8,128)} async-done(((f32[8,288,128]{2,1,0:T(8,128)}), f32[8,288,128]{2,1,0:T(8,128)}, u32[]{:S(2)}, u32[]{:S(2)}) %all-to-all-start) | async-done | bytes 1179680 | tf_op jit(solution)/shard_map/all_to_all | solution.py:784
  53.3 2.7 %shard_map.117 = (f32[32,72,128]{2,1,0:T(8,128)}, f32[32,128]{1,0:T(8,128)}) custom-call(s32[4]{0:T(128)} %copy-done.8, f32[8,288,128]{2,1,0:T(8,128)} %all-to-all-done.yin, s32[1,128]{1,0:T(1,128)} %bitcast.20, s32[1,128]{1,0:T(1,128)} %bitcast.21, f32[32,72,128]{2,1,0:T(8,128)} %shard_map.115.xbuf_in), custom_call_target="tpu_custom_call", output_to_operand_aliasing={{0}: (4, {})} | custom-call | tf_op jit(solution)/shard_map/pallas_call | solution.py:808
  56.0 0.0 copy-start.4
  56.1 5.2 %all-to-all-start.1 = ((f32[32,72,128]{2,1,0:T(8,128)}), f32[32,72,128]{2,1,0:T(8,128)}, u32[]{:S(2)}, u32[]{:S(2)}) async-start(f32[32,72,128]{2,1,0:T(8,128)} %get-tuple-element.60), calls=%async_computation.1 | async-start | bytes 2359296 | tf_op jit(solution)/shard_map/all_to_all | solution.py:818
  61.3 0.0 copy-start.3
  61.3 0.0 copy-start.11
  61.3 0.8 copy-done.11
  62.1 6.8 %shard_map.119 = (f32[4,64,8,128]{3,2,1,0:T(8,128)S(1)}, f32[64,8,128]{2,1,0:T(8,128)S(1)}, f32[33,8,128]{2,1,0:T(8,128)S(1)}, f32[33,8,128]{2,1,0:T(8,128)S(1)}) custom-call(s32[4]{0:T(128)S(1)} %copy-done.9, f32[4,64,8,128]{3,2,1,0:T(8,128)S(1)} %bitcast.16, f32[64,8,128]{2,1,0:T(8,128)S(1)} %bitcast.17, f32[4,8,128]{2,1,0:T(8,128)S(1)} %collective-permute-done.3.ghost_w, ...), custom_call_target="tpu_custom_call" | custom-call | tf_op jit(solution)/shard_map/pallas_call | solution.py:137
  69.0 0.1 collective-permute-start.6
  69.0 1.5 collective-permute-start.7
  70.5 5.7 %shard_map.118 = f32[8,256,128]{2,1,0:T(8,128)} custom-call(s32[4]{0:T(128)S(1)} %copy-done.9, f32[8,288,128]{2,1,0:T(8,128)} %all-to-all-done.yin, bf16[1024,512]{1,0:T(8,128)(2,1)S(1)} %copy-done.4, bf16[1024,512]{1,0:T(8,128)(2,1)S(1)} %copy-done.3), custom_call_target="tpu_custom_call" | custom-call | tf_op jit(solution)/shard_map/pallas_call | solution.py:137
  76.2 2.3 %shard_map.120 = (f32[64,8,256]{2,1,0:T(8,128)S(1)}, f32[2,8,256]{2,1,0:T(8,128)S(1)}, f32[49,8,256]{2,1,0:T(8,128)S(1)}, f32[49,8,256]{2,1,0:T(8,128)S(1)}) custom-call(s32[4]{0:T(128)S(1)} %copy-done.9, f32[64,8,128]{2,1,0:T(8,128)S(1)} %get-tuple-element.71.partial, f32[4,64,8,128]{3,2,1,0:T(8,128)S(1)} %get-tuple-element.72.star.star_far, ...), custom_call_target="tpu_custom_call" | custom-call | tf_op jit(solution)/shard_map/pallas_call | solution.py:137
  78.6 0.8 copy-done.6
  79.3 0.6 copy-done.10
  79.9 0.0 all-to-all-done.1.refs_0_
  79.9 4.2 %all-to-all-start.2 = ((f32[8,256,128]{2,1,0:T(8,128)}), f32[8,256,128]{2,1,0:T(8,128)}, u32[]{:S(2)}, u32[]{:S(2)}) async-start(f32[8,256,128]{2,1,0:T(8,128)} %shard_map.118), calls=%async_computation.2 | async-start | bytes 2097152 | tf_op jit(solution)/shard_map/all_to_all | solution.py:836
  84.2 4.0 %collective-permute-start.8 = (f32[49,8,256]{2,1,0:T(8,128)S(1)}, f32[49,8,256]{2,1,0:T(8,128)}, u32[]{:S(2)}, u32[]{:S(2)}) collective-permute-start(f32[49,8,256]{2,1,0:T(8,128)S(1)} %get-tuple-element.82), channel_id=1, source_target_pairs={{0,128},{128,8},{8,136},{136,16},{16,144},{144,24},{24,152},{152,3... | collective-permute-start | bytes 1204232 | tf_op jit(solution)/shard_map/ppermute | solution.py:839
  88.2 2.1 %collective-permute-start.9 = (f32[49,8,256]{2,1,0:T(8,128)S(1)}, f32[49,8,256]{2,1,0:T(8,128)}, u32[]{:S(2)}, u32[]{:S(2)}) collective-permute-start(f32[49,8,256]{2,1,0:T(8,128)S(1)} %get-tuple-element.83), channel_id=1, source_target_pairs={{128,0},{8,128},{136,8},{16,136},{144,16},{24,144},{152,24},{32,15... | collective-permute-start | bytes 1204232 | tf_op jit(solution)/shard_map/ppermute | solution.py:838
  90.3 8.8 %shard_map.121 = (f32[32,64,128]{2,1,0:T(8,128)}, f32[1,128]{1,0:T(1,128)}) custom-call(s32[4]{0:T(128)} %copy-done.8, f32[32,72,128]{2,1,0:T(8,128)} %all-to-all-done.1.refs_0_, bf16[512,1024]{1,0:T(8,128)(2,1)} %constant.32.clone.refs_1_, bf16[512,1024]{1,0:T(8,128)(2,1)} %constant.33.clone.refs_2_, bf16[512,1024]{1,0:T(8,128)(2,1)} %constant.34.clone.refs_3_, ...), custom_call_target="tpu_custom_call" | custom-call | tf_op jit(solution)/shard_map/pallas_call | solution.py:841
  99.1 0.0 collective-permute-done.9.from_e_far
  99.1 12.1 %all-to-all-done.2.yback_far = f32[8,256,128]{2,1,0:T(8,128)} async-done(((f32[8,256,128]{2,1,0:T(8,128)}), f32[8,256,128]{2,1,0:T(8,128)}, u32[]{:S(2)}, u32[]{:S(2)}) %all-to-all-start.2) | async-done | bytes 1048608 | tf_op jit(solution)/shard_map/all_to_all | solution.py:836
  111.3 9.7 %all-to-all-start.3 = ((f32[32,64,128]{2,1,0:T(8,128)}), f32[32,64,128]{2,1,0:T(8,128)}, u32[]{:S(2)}, u32[]{:S(2)}) async-start(f32[32,64,128]{2,1,0:T(8,128)} %get-tuple-element.85), calls=%async_computation.3 | async-start | bytes 2097152 | tf_op jit(solution)/shard_map/all_to_all | solution.py:849
  121.0 14.9 %shard_map.122 = (f32[4,8,128,128]{3,2,1,0:T(8,128)}, f32[4,8,64,128]{3,2,1,0:T(8,128)}) custom-call(s32[4]{0:T(128)} %copy-done.8, f32[64,8,256]{2,1,0:T(8,128)} %copy-done.6, f32[4,64,8,128]{3,2,1,0:T(8,128)} %copy-done.2, f32[2,8,256]{2,1,0:T(8,128)} %copy-done.10, f32[49,8,256]{2,1,0:T(8,128)} %collective-permute-done.8.from_w_far, ...), custom_call_target="tpu_custom_call" | custom-call | tf_op jit(solution)/shard_map/pallas_call | solution.py:850
  136.0 1.6 %all-to-all-done.3.xback_far = f32[32,64,128]{2,1,0:T(8,128)} async-done(((f32[32,64,128]{2,1,0:T(8,128)}), f32[32,64,128]{2,1,0:T(8,128)}, u32[]{:S(2)}, u32[]{:S(2)}) %all-to-all-start.3) | async-done | bytes 1048608 | tf_op jit(solution)/shard_map/all_to_all | solution.py:849
  137.6 4.5 %shard_map.123 = (f32[4,8,128,128]{3,2,1,0:T(8,128)}, f32[4,8,64,128]{3,2,1,0:T(8,128)}) custom-call(s32[4]{0:T(128)} %copy-done.8, f32[4,8,128,128]{3,2,1,0:T(8,128)} %bitcast.13, f32[4,8,64,128]{3,2,1,0:T(8,128)} %copy-done.1, f32[8,256,128]{2,1,0:T(8,128)} %all-to-all-done.2.yback_far, ...), custom_call_target="tpu_custom_call", output_to_operand_aliasing={{0}: (5, {}), {1}: (6, {})} | custom-call | tf_op jit(solution)/shard_map/pallas_call | solution.py:861
  142.1 1.2 collective-permute-start.10
  143.3 2.6 %collective-permute-done.10.theirs = f32[4,8,64,128]{3,2,1,0:T(8,128)} collective-permute-done((f32[4,8,64,128]{3,2,1,0:T(8,128)}, f32[4,8,64,128]{3,2,1,0:T(8,128)}, u32[]{:S(2)}, u32[]{:S(2)}) %collective-permute-start.10) | collective-permute-done | bytes 1048608 | tf_op jit(solution)/shard_map/ppermute | solution.py:868
  145.9 2.7 %shard_map.124 = f32[4,8,128,128]{3,2,1,0:T(8,128)} custom-call(s32[4]{0:T(128)} %copy-done.8, f32[4,8,64,128]{3,2,1,0:T(8,128)} %collective-permute-done.10.theirs, f32[4,8,128,128]{3,2,1,0:T(8,128)} %get-tuple-element.96.joined_in), custom_call_target="tpu_custom_call", output_to_operand_aliasing={{}: (2, {})} | custom-call | tf_op jit(solution)/shard_map/pallas_call | solution.py:869
  (19 shorter events, 0.0 us)
Async XLA Ops:
  0.7 13.2 %copy-start.8 = (s32[4]{0:T(128)}, s32[4]{0:T(128)S(1)}, u32[]{:S(2)}) copy-start(s32[4]{0:T(128)S(1)} %pad_add_fusion.place) | copy-start | bytes 52
  0.7 1.6 %copy-start = (f32[1,4,8,128,128]{4,3,2,1,0:T(8,128)S(1)}, f32[1,4,8,128,128]{4,3,2,1,0:T(8,128)}, u32[]{:S(2)}) copy-start(f32[1,4,8,128,128]{4,3,2,1,0:T(8,128)} %param.10) | copy-start | bytes 6291460
  3.0 9.3 %collective-permute-start = (f32[4,8,64,128]{3,2,1,0:T(8,128)S(1)}, f32[4,8,64,128]{3,2,1,0:T(8,128)S(1)}, u32[]{:S(2)}, u32[]{:S(2)}) collective-permute-start(f32[4,8,64,128]{3,2,1,0:T(8,128)S(1)} %get-tuple-element.50), channel_id=1, source_target_pairs={{0,128},{128,0},{1,129},{129,1},{2,130},{130,2},{3,131},{131,3},{4... | collective-permute-start | bytes 3145736 | tf_op jit(solution)/shard_map/ppermute | solution.py:782
  6.3 6.0 %collective-permute-start.1 = (f32[4,8,128]{2,1,0:T(8,128)S(1)}, f32[4,8,128]{2,1,0:T(8,128)S(1)}, u32[]{:S(2)}, u32[]{:S(2)}) collective-permute-start(f32[4,8,128]{2,1,0:T(8,128)S(1)} %get-tuple-element.51), channel_id=1, source_target_pairs={{64,0},{65,1},{66,2},{67,3},{68,4},{69,5},{70,6},{71,7},{192,128},... | collective-permute-start | bytes 49160 | tf_op jit(solution)/shard_map/ppermute | solution.py:781
  13.9 1.0 copy-start.1
  14.9 38.4 %all-to-all-start = ((f32[8,288,128]{2,1,0:T(8,128)}), f32[8,288,128]{2,1,0:T(8,128)}, u32[]{:S(2)}, u32[]{:S(2)}) async-start(f32[8,288,128]{2,1,0:T(8,128)} %shard_map.114), calls=%async_computation | async-start | bytes 2359296 | tf_op jit(solution)/shard_map/all_to_all | solution.py:784
  26.1 11.8 %collective-permute-start.2 = (f32[4,8,128]{2,1,0:T(8,128)}, f32[4,8,128]{2,1,0:T(8,128)S(1)}, u32[]{:S(2)}, u32[]{:S(2)}) collective-permute-start(f32[4,8,128]{2,1,0:T(8,128)} %get-tuple-element.54), channel_id=1, source_target_pairs={{128,0},{8,128},{136,8},{16,136},{144,16},{24,144},{152,24},{32,15... | collective-permute-start | bytes 49160 | tf_op jit(solution)/shard_map/ppermute | solution.py:797
  29.5 8.5 %collective-permute-start.3 = (f32[4,8,128]{2,1,0:T(8,128)}, f32[4,8,128]{2,1,0:T(8,128)S(1)}, u32[]{:S(2)}, u32[]{:S(2)}) collective-permute-start(f32[4,8,128]{2,1,0:T(8,128)} %get-tuple-element.55), channel_id=1, source_target_pairs={{0,128},{128,8},{8,136},{136,16},{16,144},{144,24},{24,152},{152,3... | collective-permute-start | bytes 49160 | tf_op jit(solution)/shard_map/ppermute | solution.py:798
  31.7 14.4 %collective-permute-start.4 = (f32[4,8,128]{2,1,0:T(8,128)}, f32[4,8,128]{2,1,0:T(8,128)S(1)}, u32[]{:S(2)}, u32[]{:S(2)}) collective-permute-start(f32[4,8,128]{2,1,0:T(8,128)} %get-tuple-element.56), channel_id=1, source_target_pairs={{0,7},{1,0},{2,1},{3,2},{4,3},{5,4},{6,5},{7,6},{8,15},{9,8},{10,9... | collective-permute-start | bytes 49160 | tf_op jit(solution)/shard_map/ppermute | solution.py:799
  34.5 11.7 %collective-permute-start.5 = (f32[4,8,128]{2,1,0:T(8,128)}, f32[4,8,128]{2,1,0:T(8,128)S(1)}, u32[]{:S(2)}, u32[]{:S(2)}) collective-permute-start(f32[4,8,128]{2,1,0:T(8,128)} %get-tuple-element.57), channel_id=1, source_target_pairs={{0,1},{1,2},{2,3},{3,4},{4,5},{5,6},{6,7},{7,0},{8,9},{9,10},{10,1... | collective-permute-start | bytes 49160 | tf_op jit(solution)/shard_map/ppermute | solution.py:800
  56.0 5.3 %copy-start.5 = (f32[4,512,128]{2,1,0:T(8,128)S(1)}, f32[4,512,128]{2,1,0:T(8,128)}, u32[]{:S(2)}) copy-start(f32[4,512,128]{2,1,0:T(8,128)} %get-tuple-element.52) | copy-start | bytes 3145732
  56.0 5.3 %copy-start.7 = (f32[512,128]{1,0:T(8,128)S(1)}, f32[512,128]{1,0:T(8,128)}, u32[]{:S(2)}) copy-start(f32[512,128]{1,0:T(8,128)} %get-tuple-element.53) | copy-start | bytes 786436
  56.0 5.3 %copy-start.9 = (s32[4]{0:T(128)S(1)}, s32[4]{0:T(128)}, u32[]{:S(2)}) copy-start(s32[4]{0:T(128)} %copy-done.8) | copy-start | bytes 52
  56.0 14.5 %copy-start.4 = (bf16[1024,512]{1,0:T(8,128)(2,1)S(1)}, bf16[1024,512]{1,0:T(8,128)(2,1)}, u32[]{:S(2)}) copy-start(bf16[1024,512]{1,0:T(8,128)(2,1)} %constant.30.clone.table_high) | copy-start | bytes 3145732
  56.1 23.9 %all-to-all-start.1 = ((f32[32,72,128]{2,1,0:T(8,128)}), f32[32,72,128]{2,1,0:T(8,128)}, u32[]{:S(2)}, u32[]{:S(2)}) async-start(f32[32,72,128]{2,1,0:T(8,128)} %get-tuple-element.60), calls=%async_computation.1 | async-start | bytes 2359296 | tf_op jit(solution)/shard_map/all_to_all | solution.py:818
  61.3 9.2 %copy-start.3 = (bf16[1024,512]{1,0:T(8,128)(2,1)S(1)}, bf16[1024,512]{1,0:T(8,128)(2,1)}, u32[]{:S(2)}) copy-start(bf16[1024,512]{1,0:T(8,128)(2,1)} %constant.31.clone.table_low) | copy-start | bytes 3145732
  61.3 0.8 copy-start.11
  68.9 7.3 %copy-start.2 = (f32[4,64,8,128]{3,2,1,0:T(8,128)}, f32[4,64,8,128]{3,2,1,0:T(8,128)S(1)}, u32[]{:S(2)}) copy-start(f32[4,64,8,128]{3,2,1,0:T(8,128)S(1)} %get-tuple-element.72.star.star_far) | copy-start | bytes 3145732
  69.0 7.3 %collective-permute-start.6 = (f32[33,8,128]{2,1,0:T(8,128)S(1)}, f32[33,8,128]{2,1,0:T(8,128)S(1)}, u32[]{:S(2)}, u32[]{:S(2)}) collective-permute-start(f32[33,8,128]{2,1,0:T(8,128)S(1)} %get-tuple-element.68), channel_id=1, source_target_pairs={{0,7},{1,0},{2,1},{3,2},{4,3},{5,4},{6,5},{7,6},{8,15},{9,8},{10,9... | collective-permute-start | bytes 405512 | tf_op jit(solution)/shard_map/ppermute | solution.py:824
  69.0 7.2 %collective-permute-start.7 = (f32[33,8,128]{2,1,0:T(8,128)S(1)}, f32[33,8,128]{2,1,0:T(8,128)S(1)}, u32[]{:S(2)}, u32[]{:S(2)}) collective-permute-start(f32[33,8,128]{2,1,0:T(8,128)S(1)} %get-tuple-element.69), channel_id=1, source_target_pairs={{0,1},{1,2},{2,3},{3,4},{4,5},{5,6},{6,7},{7,0},{8,9},{9,10},{10,1... | collective-permute-start | bytes 405512 | tf_op jit(solution)/shard_map/ppermute | solution.py:825
  78.5 0.8 copy-start.6
  79.3 0.6 copy-start.10
  79.9 31.3 %all-to-all-start.2 = ((f32[8,256,128]{2,1,0:T(8,128)}), f32[8,256,128]{2,1,0:T(8,128)}, u32[]{:S(2)}, u32[]{:S(2)}) async-start(f32[8,256,128]{2,1,0:T(8,128)} %shard_map.118), calls=%async_computation.2 | async-start | bytes 2097152 | tf_op jit(solution)/shard_map/all_to_all | solution.py:836
  84.2 14.9 %collective-permute-start.8 = (f32[49,8,256]{2,1,0:T(8,128)S(1)}, f32[49,8,256]{2,1,0:T(8,128)}, u32[]{:S(2)}, u32[]{:S(2)}) collective-permute-start(f32[49,8,256]{2,1,0:T(8,128)S(1)} %get-tuple-element.82), channel_id=1, source_target_pairs={{0,128},{128,8},{8,136},{136,16},{16,144},{144,24},{24,152},{152,3... | collective-permute-start | bytes 1204232 | tf_op jit(solution)/shard_map/ppermute | solution.py:839
  88.2 10.9 %collective-permute-start.9 = (f32[49,8,256]{2,1,0:T(8,128)S(1)}, f32[49,8,256]{2,1,0:T(8,128)}, u32[]{:S(2)}, u32[]{:S(2)}) collective-permute-start(f32[49,8,256]{2,1,0:T(8,128)S(1)} %get-tuple-element.83), channel_id=1, source_target_pairs={{128,0},{8,128},{136,8},{16,136},{144,16},{24,144},{152,24},{32,15... | collective-permute-start | bytes 1204232 | tf_op jit(solution)/shard_map/ppermute | solution.py:838
  111.3 26.4 %all-to-all-start.3 = ((f32[32,64,128]{2,1,0:T(8,128)}), f32[32,64,128]{2,1,0:T(8,128)}, u32[]{:S(2)}, u32[]{:S(2)}) async-start(f32[32,64,128]{2,1,0:T(8,128)} %get-tuple-element.85), calls=%async_computation.3 | async-start | bytes 2097152 | tf_op jit(solution)/shard_map/all_to_all | solution.py:849
  142.1 3.8 %collective-permute-start.10 = (f32[4,8,64,128]{3,2,1,0:T(8,128)}, f32[4,8,64,128]{3,2,1,0:T(8,128)}, u32[]{:S(2)}, u32[]{:S(2)}) collective-permute-start(f32[4,8,64,128]{3,2,1,0:T(8,128)} %get-tuple-element.95), channel_id=1, source_target_pairs={{0,128},{128,0},{1,129},{129,1},{2,130},{130,2},{3,131},{131,3},{4... | collective-permute-start | bytes 3145736 | tf_op jit(solution)/shard_map/ppermute | solution.py:868

commit v3 on v2

--- a/solution.py
+++ b/solution.py
@@ -207,27 +207,22 @@
             ybuf[g, 4 * HALF + c * NZ : 4 * HALF + (c + 1) * NZ] = piece
 
 
-def pack_kernel(place, own, got, xbuf_far, half, xbuf, sem):
-    load_half(place, own, got, half, sem.at[8])
+def pack_kernel(place, own, got, packed):
     lane = lane_index((HALF, BY))
-    stores = []
-    for z in range(NZ):
-        for part in range(4):
-            total = None
-            for c in range(4):
-                shift = 32 * ((c - part) % 4)
-                moved = half[c, z] if shift == 0 else pltpu.roll(half[c, z], shift, 1)
-                total = moved if total is None else jnp.where(lane >= 32 * c, moved, total)
-            xbuf[4 * z + part] = total
-        tiles = pl.ds(4 * z, 4)
-        stores += run_all(
-            [
-                pltpu.make_async_copy(
-                    xbuf.at[tiles], xbuf_far.at[tiles, pl.ds(0, HALF)], sem.at[z]
-                )
-            ]
-        )
-    wait_all(stores)
+
+    def fill(half):
+        for z in range(NZ):
+            rows = [half(c, z) for c in range(4)]
+            for part in range(4):
+                total = None
+                for c in range(4):
+                    shift = 32 * ((c - part) % 4)
+                    moved = rows[c] if shift == 0 else pltpu.roll(rows[c], shift, 1)
+                    total = moved if total is None else jnp.where(lane >= 32 * c, moved, total)
+                packed[4 * z + part] = total
+
+    pl.when(place[0] == 0)(lambda: fill(lambda c, z: own[c, z, :HALF]))
+    pl.when(place[0] == 1)(lambda: fill(lambda c, z: got[c, z]))
 
 
 def blend_kernel(place, yin, source, weight, xbuf_in, xbuf_far, inflow_far,
@@ -290,11 +285,10 @@
     return (m % 2) * GX + m // 2
 
 
-def line_kernel(place, r0, r1, r2, r3, xin, sh, sl, ah, al, xout, inflow_row, plus, minus):
-    inflow_row[...] = xin[NX // 2 // BX, HALF : HALF + 1]
+def line_kernel(place, r0, r1, r2, r3, xin, sh, sl, ah, al, xout, plus, minus):
     for m in range(16):
-        a = xin[chunk_place(m), :HALF]
-        b = xin[chunk_place(m + 16), :HALF]
+        a = xin[chunk_place(m)]
+        b = xin[chunk_place(m + 16)]
         rows = slice(m * HALF, (m + 1) * HALF)
         plus[rows, :BY], plus[rows, BY:] = halves(a + b)
         minus[rows, :BY], minus[rows, BY:] = halves(a - b)
@@ -320,81 +314,83 @@
         for k in range(4):
             for side, value in ((0, even + odd), (1, even - odd)):
                 place_of = chunk_place(4 * i + k + 16 * side)
-                u = jnp.where(lane < 32, xin[place_of, :HALF], 0.0)
+                u = jnp.where(lane < 32, xin[place_of], 0.0)
                 u = u + pltpu.roll(u, 32, 1)
                 u = u + pltpu.roll(u, 64, 1)
                 rows = slice(k * HALF, (k + 1) * HALF)
                 late = slice(256 + k * HALF, 256 + (k + 1) * HALF)
-                xout[place_of] = (1.0 + u) * value[rows] + value[late]
-
-
-def finish_kernel(place, own, got, yback_far, xback_far, joined_in, send_in, joined, send,
-                  half, yback, xback, out, sem):
+                xout[place_of, :HALF] = (1.0 + u) * value[rows] + value[late]
+
+
+def base_kernel(place, own, got, xback_far, base_far, row_far, half, xback, rim, base, row, sem):
+    loads = run_all(
+        [
+            pltpu.make_async_copy(xback_far.at[:, pl.ds(0, HALF)], xback, sem.at[1]),
+            pltpu.make_async_copy(xback_far.at[NX // 2 // BX, pl.ds(HALF, 8)], rim, sem.at[2]),
+        ]
+    )
+    load_half(place, own, got, half, sem.at[0])
+    wait_all(loads)
+    row[...] = rim[:1]
+    stores = run_all([pltpu.make_async_copy(row, row_far, sem.at[3])])
+    lane = lane_index((HALF, BY))
+    for z in range(NZ):
+        for c in range(4):
+            total = None
+            for part in range(4):
+                shift = 32 * ((part - c) % 4)
+                tile = xback[4 * z + part]
+                moved = tile if shift == 0 else pltpu.roll(tile, shift, 1)
+                total = moved if total is None else jnp.where(lane >= 32 * part, moved, total)
+            q = half[c, z]
+            upper = half[c, min(z + 1, NZ - 1)]
+            lower = half[c, max(z - 1, 0)]
+            mixed = 0.02 * (upper + lower - 2.0 * q) - 0.1 * half[2, z] * (upper - lower)
+            base[z, c * HALF : (c + 1) * HALF] = q + total + mixed
+    stores += run_all([pltpu.make_async_copy(base, base_far, sem.at[4])])
+    wait_all(stores)
+
+
+def finish_kernel(place, base_far, yback_far, joined_in, send_in, joined, send,
+                  base, yback, out, sem):
+    pairs = [pl.ds(2 * k, 2) for k in range(4)]
     loads = [
         run_all(
             [
-                pltpu.make_async_copy(
-                    yback_far.at[pl.ds(2 * k, 2)], yback.at[pl.ds(2 * k, 2)], sem.at[1 + k]
-                ),
-                pltpu.make_async_copy(
-                    xback_far.at[pl.ds(8 * k, 8)], xback.at[pl.ds(8 * k, 8)], sem.at[5 + k]
-                ),
+                pltpu.make_async_copy(base_far.at[at], base.at[at], sem.at[k]),
+                pltpu.make_async_copy(yback_far.at[at], yback.at[at], sem.at[4 + k]),
             ]
         )
-        for k in range(4)
+        for k, at in enumerate(pairs)
     ]
-    load_half(place, own, got, half, sem.at[0])
-    lane = lane_index((HALF, BY))
     to_own, to_other = [], []
-    for k in range(4):
-        at = pl.ds(2 * k, 2)
+    for k, at in enumerate(pairs):
         piece = out.at[:, at]
         to_own.append(
-            pltpu.make_async_copy(piece, joined.at[:, at, pl.ds(0, HALF)], sem.at[9 + k])
+            pltpu.make_async_copy(piece, joined.at[:, at, pl.ds(0, HALF)], sem.at[8 + k])
         )
-        to_other.append(pltpu.make_async_copy(piece, send.at[:, at], sem.at[9 + k]))
+        to_other.append(pltpu.make_async_copy(piece, send.at[:, at], sem.at[8 + k]))
     for k in range(4):
         wait_all(loads[k])
         for z in (2 * k, 2 * k + 1):
             for c in range(4):
-                total = None
-                for part in range(4):
-                    shift = 32 * ((part - c) % 4)
-                    tile = xback[4 * z + part]
-                    moved = tile if shift == 0 else pltpu.roll(tile, shift, 1)
-                    total = moved if total is None else jnp.where(lane >= 32 * part, moved, total)
-                q = half[c, z]
-                upper = half[c, min(z + 1, NZ - 1)]
-                lower = half[c, max(z - 1, 0)]
-                mixed = 0.02 * (upper + lower - 2.0 * q) - 0.1 * half[2, z] * (upper - lower)
-                out[c, z] = q + total + yback[z, c * HALF : (c + 1) * HALF] + mixed
+                rows = slice(c * HALF, (c + 1) * HALF)
+                out[c, z] = base[z, rows] + yback[z, rows]
         pl.when(place[0] == 0)(to_own[k].start)
         pl.when(place[0] == 1)(to_other[k].start)
     pl.when(place[0] == 0)(lambda: wait_all(to_own))
     pl.when(place[0] == 1)(lambda: wait_all(to_other))
 
 
-def join_kernel(place, theirs, joined_in, joined, near, sem):
-    def forward(start):
-        pieces = [
-            (
-                pltpu.make_async_copy(theirs.at[c], near.at[c], sem.at[c]),
-                pltpu.make_async_copy(
-                    near.at[c], joined.at[c, :, pl.ds(start, HALF)], sem.at[4 + c]
-                ),
-            )
+def join_kernel(place, theirs, joined_in, joined, sem):
+    def copies(start):
+        return [
+            pltpu.make_async_copy(theirs.at[c], joined.at[c, :, pl.ds(start, HALF)], sem.at[c])
             for c in range(4)
         ]
-        for load, _ in pieces:
-            load.start()
-        for load, store in pieces:
-            load.wait()
-            store.start()
-        for _, store in pieces:
-            store.wait()
-
-    pl.when(place[0] == 0)(lambda: forward(HALF))
-    pl.when(place[0] == 1)(lambda: forward(0))
+
+    pl.when(place[0] == 0)(lambda: wait_all(run_all(copies(HALF))))
+    pl.when(place[0] == 1)(lambda: wait_all(run_all(copies(0))))
 
 
 def turn_kernel(place, own, got, mask_far, cells_far, drag_far, row_low_far, row_high_far,
@@ -501,7 +497,9 @@
         star_row(x, lambda c: cells[c, x - 1], lambda c: cells[c, x + 1])
         return carry
 
-    lax.fori_loop(1, FX - 1, star_rows, 0, unroll=2)
+    lax.fori_loop(1, FX - 3, star_rows, 0, unroll=6)
+    for x in (FX - 3, FX - 2):
+        star_rows(x, 0)
     star_row(
         FX - 1,
         lambda c: cells[c, FX - 2],
@@ -526,7 +524,9 @@
         source_row(x, star[0, x - 1], star[0, x + 1])
         return carry
 
-    lax.fori_loop(1, FX - 1, source_rows, 0, unroll=2)
+    lax.fori_loop(1, FX - 3, source_rows, 0, unroll=6)
+    for x in (FX - 3, FX - 2):
+        source_rows(x, 0)
     source_row(FX - 1, star[0, FX - 2], jnp.where(last, star[0, FX - 1], 0.0))
     for k in range(2):
         wide[k, FX] = star[0, 0]
@@ -780,8 +780,9 @@
     other, column = near_call(lead_kernel, [half_block, rim], 2)(place, own)
     column = lax.ppermute(column, "gx", [(NX // 2 // BX, 0)])
     got = lax.ppermute(other, "dom", swap)
-    (ybuf,) = near_call(send_kernel, [(GY, 288, BY)], 2)(place, own, got, column)
-    yin = lax.all_to_all(ybuf, "gy", 0, 0, tiled=True)
+    (packed,) = near_call(pack_kernel, [(32, HALF, BY)], 3)(place, own, got)
+    packed, column = in_step(packed, column)
+    xin = lax.all_to_all(packed, x_axes, 0, 0, tiled=True)
 
     cells, drag, row_low, row_high, col_low, col_high = raw_call(
         turn_kernel,
@@ -794,18 +795,27 @@
     )(place, own, got, turbine_mask)
     cells = cells.reshape(block)
     drag = drag.reshape(FX, NZ, BY)
+    (ybuf,) = near_call(send_kernel, [(GY, 288, BY)], 2)(place, own, got, column)
+    ybuf, cells, drag, row_low, row_high, col_low, col_high = in_step(
+        ybuf, cells, drag, row_low, row_high, col_low, col_high
+    )
+    yin = lax.all_to_all(ybuf, "gy", 0, 0, tiled=True)
     ghost_e = lax.ppermute(row_low, x_axes, along_x(-1))
     ghost_w = lax.ppermute(row_high, x_axes, along_x(1))
     ghost_n = lax.ppermute(col_low, "gy", along_y(-1))
     ghost_s = lax.ppermute(col_high, "gy", along_y(1))
-    (xbuf,) = raw_call(
-        pack_kernel, 2, [(32, 72, BY)], vmem(half_block, (32, HALF, BY)) + [dma((9,))]
-    )(place, own, got)
-
-    yin, xbuf, cells, drag, ghost_e, ghost_w, ghost_n, ghost_s = in_step(
-        yin, xbuf, cells, drag, ghost_e, ghost_w, ghost_n, ghost_s
-    )
-    xbuf, blended = raw_call(
+    ins = (xin, sh, sl, ah, al)
+    (xout,) = staged_call(
+        line_kernel,
+        ins,
+        [(32, 72, BY)],
+        scratch=[pltpu.VMEM((NX // 2, 2 * BY), BF16)] * 2,
+        late=(1, 2, 3, 4),
+    )(place, *ins)
+    yin, xout, ghost_e, ghost_w, ghost_n, ghost_s = in_step(
+        yin, xout, ghost_e, ghost_w, ghost_n, ghost_s
+    )
+    xout, blended = raw_call(
         blend_kernel,
         4,
         [(32, 72, BY), (4 * NZ, BY)],
@@ -814,8 +824,8 @@
         + vmem((32, 8, BY), (4 * NZ, BY))
         + [dma((5,))],
         {4: 0},
-    )(place, yin, inflow_source[None], inflow_weight[None], xbuf)
-    xin = lax.all_to_all(xbuf, x_axes, 0, 0, tiled=True)
+    )(place, yin, inflow_source[None], inflow_weight[None], xout)
+    xback = lax.all_to_all(xout, x_axes, 0, 0, tiled=True)
 
     outs = [block, (FX, NZ, BY), strip, strip]
     star, partial, strip_s, strip_n = near_call(
@@ -832,21 +842,18 @@
         [(FX, *wide_row), (2, *wide_row), (HALO + 1, *wide_row), (HALO + 1, *wide_row)],
         2,
     )(place, partial, star, from_s, from_n)
-    xin, yout, whole, rims, send_w, send_e = in_step(xin, yout, whole, rims, send_w, send_e)
+    xback, yout, whole, rims, send_w, send_e = in_step(xback, yout, whole, rims, send_w, send_e)
     yback = lax.all_to_all(yout, "gy", 0, 0, tiled=True)
 
     from_e = lax.ppermute(send_w, x_axes, along_x(-1))
     from_w = lax.ppermute(send_e, x_axes, along_x(1))
-    ins = (xin, sh, sl, ah, al)
-    xout, inflow_row = staged_call(
-        line_kernel,
-        ins,
-        [(32, HALF, BY), (1, BY)],
-        scratch=[pltpu.VMEM((NX // 2, 2 * BY), BF16)] * 2,
-        late=(1, 2, 3, 4),
-    )(place, *ins)
-    yback, xout, from_w, from_e = in_step(yback, xout, from_w, from_e)
-    xback = lax.all_to_all(xout, x_axes, 0, 0, tiled=True)
+    base, inflow_row = raw_call(
+        base_kernel,
+        3,
+        [(GY, 4 * HALF, BY), (1, BY)],
+        vmem(half_block, (32, HALF, BY), (8, BY), (GY, 4 * HALF, BY), (1, BY)) + [dma((5,))],
+    )(place, own, got, xback)
+    base, from_e, from_w = in_step(base, from_e, from_w)
     joined, send = raw_call(
         pressure_kernel,
         5,
@@ -857,17 +864,27 @@
         + [dma((11,))],
     )(place, whole, star, rims, from_w, from_e)
 
-    xback, joined, send = in_step(xback, joined, send)
+    yback, base, joined, send = in_step(yback, base, joined, send)
     joined, send = raw_call(
         finish_kernel,
-        6,
+        4,
         [(4, NZ, BX, BY), half_block],
-        vmem(half_block, (GY, 4 * HALF, BY), (32, HALF, BY), half_block) + [dma((13,))],
-        {5: 0, 6: 1},
-    )(place, own, got, yback, xback, joined, send)
+        vmem((GY, 4 * HALF, BY), (GY, 4 * HALF, BY), half_block) + [dma((12,))],
+        {3: 0, 4: 1},
+    )(place, base, yback, joined, send)
     theirs = lax.ppermute(send, "dom", swap)
-    (joined,) = raw_call(
-        join_kernel, 2, [(4, NZ, BX, BY)], vmem(half_block) + [dma((8,))], {2: 0}
+    (joined,) = pl.pallas_call(
+        join_kernel,
+        out_shape=[jax.ShapeDtypeStruct((4, NZ, BX, BY), F32)],
+        in_specs=[
+            pl.BlockSpec(memory_space=pltpu.SMEM),
+            pl.BlockSpec(memory_space=pltpu.VMEM),
+            pl.BlockSpec(memory_space=pl.ANY),
+        ],
+        out_specs=[pl.BlockSpec(memory_space=pl.ANY)],
+        scratch_shapes=[dma((4,))],
+        input_output_aliases={2: 0},
+        compiler_params=pltpu.CompilerParams(vmem_limit_bytes=2 * 1024 * 1024),
     )(place, theirs, joined)
     return joined[None], inflow_row
 

time: 150 us -> 142 us (0.947)
  Pallas kernels: 59 us -> 54.6 us
  starting transfers between devices: 47.4 us -> 44.8 us
  waiting for transfers between devices: 36.4 us -> 34.4 us
    all_to_all x1, waiting for transfers between devices: 12.1 us -> 1.7 us  [on_device(): yback = lax.all_to_all(yout, 'gy', 0, 0, tiled=True)]
    all_to_all x1, waiting for transfers between devices: 0.01 us -> 10.2 us  [on_device(): xin = lax.all_to_all(packed, x_axes, 0, 0, tiled=True)]
    all_to_all x1, starting transfers between devices: 9.74 us -> 5.19 us  [on_device(): xback = lax.all_to_all(xout, x_axes, 0, 0, tiled=True)]
    ppermute x1, waiting for transfers between devices: 4.69 us -> 1.24 us  [on_device(): column = lax.ppermute(column, 'gx', [(NX // 2 // BX, 0)])]
    pallas_call x5 -> x6, Pallas kernels: 17.1 us -> 14.6 us  [call(): pl.pallas_call(body, out_shape=[jax.ShapeDtypeStruct(shape, F32) for shap...]
    pallas_call x4, Pallas kernels: 19.4 us -> 17.6 us  [the longest x1 8.79 us: on_device(): staged_call(line_kernel, ins, [(32, 72, BY)], scratch=[pltpu.VMEM((NX //...]
    ppermute x1, starting transfers between devices: 4 us -> 2.45 us  [on_device(): from_w = lax.ppermute(send_e, x_axes, along_x(1))]
    unnamed x24 -> x40, local copies, waits for them, and re-layouts: 4.79 us -> 5.84 us
  transfers between devices with their start and end apart: 15 -> 15, of which waited for: 6 -> 9; matrix products, arithmetic and copies ran while one was open for 0% -> 0% of each run, Pallas kernels for 31% -> 33%
where the time goes in v3:
time: 142 us; the launch traced here: 141 us
  Pallas kernels  54.6 us (38%)
  starting transfers between devices  44.8 us (32%)
  waiting for transfers between devices  34.4 us (24%)
  local copies, waits for them, and re-layouts  5.84 us (4%)
    pallas_call x1, Pallas kernels, on_device(): raw_call(pressure_kernel, 5, [(4, NZ, BX, BY), half_block], vmem(block, (...  14.9 us
    pallas_call x6, Pallas kernels, call(): pl.pallas_call(body, out_shape=[jax.ShapeDtypeStruct(shape, F32) for shap...  14.6 us
    all_to_all x1, waiting for transfers between devices, on_device(): xin = lax.all_to_all(packed, x_axes, 0, 0, tiled=True)  10.2 us
    pallas_call x1, Pallas kernels, on_device(): staged_call(line_kernel, ins, [(32, 72, BY)], scratch=[pltpu.VMEM((NX //...  8.79 us
    ppermute x1, waiting for transfers between devices, on_device(): ghost_n = lax.ppermute(col_low, 'gy', along_y(-1))  7.71 us
    all_to_all x1, starting transfers between devices, on_device(): yin = lax.all_to_all(ybuf, 'gy', 0, 0, tiled=True)  7.13 us
    all_to_all x1, waiting for transfers between devices, on_device(): yin = lax.all_to_all(ybuf, 'gy', 0, 0, tiled=True)  7.13 us
    unnamed x40, local copies, waits for them, and re-layouts  5.84 us
  transfers between devices with their start and end apart: 15, of which 9 were waited for; matrix products, arithmetic and copies ran while one was open for 0% of the time, Pallas kernels for 33%

profile of v3, /device:TPU:1, one launch (start us, length us, event | category | flops | bytes accessed | tf_op | source)
XLA Modules:
  0.0 140.9 jit_solution(84472569844021442)
XLA Ops:
  0.6 0.1 pad_add_fusion.place
  0.7 1.6 %copy-done = f32[1,4,8,128,128]{4,3,2,1,0:T(8,128)S(1)} copy-done((f32[1,4,8,128,128]{4,3,2,1,0:T(8,128)S(1)}, f32[1,4,8,128,128]{4,3,2,1,0:T(8,128)}, u32[]{:S(2)}) %copy-start) | copy-done | bytes 2097176
  2.3 0.6 shard_map.113
  3.0 3.3 %collective-permute-start = (f32[4,8,64,128]{3,2,1,0:T(8,128)S(1)}, f32[4,8,64,128]{3,2,1,0:T(8,128)S(1)}, u32[]{:S(2)}, u32[]{:S(2)}) collective-permute-start(f32[4,8,64,128]{3,2,1,0:T(8,128)S(1)} %get-tuple-element.57), channel_id=1, source_target_pairs={{0,128},{128,0},{1,129},{129,1},{2,130},{130,2},{3,131},{131,3},{4... | collective-permute-start | bytes 3145736 | tf_op jit(solution)/shard_map/ppermute | solution.py:782
  6.3 1.3 collective-permute-start.1
  7.6 1.0 collective-permute-done.got
  8.6 1.4 %shard_map.114 = f32[32,64,128]{2,1,0:T(8,128)S(1)} custom-call(s32[4]{0:T(128)S(1)} %pad_add_fusion.place, f32[4,8,128,128]{3,2,1,0:T(8,128)S(1)} %bitcast.14, f32[4,8,64,128]{3,2,1,0:T(8,128)S(1)} %collective-permute-done.got), custom_call_target="tpu_custom_call" | custom-call | tf_op jit(solution)/shard_map/pallas_call | solution.py:137
  10.0 1.0 copy-done.4
  11.0 1.2 collective-permute-done.1.column
  12.3 5.5 %all-to-all-start.1 = ((f32[32,64,128]{2,1,0:T(8,128)}), f32[32,64,128]{2,1,0:T(8,128)}, u32[]{:S(2)}, u32[]{:S(2)}) async-start(f32[32,64,128]{2,1,0:T(8,128)} %copy-done.4), calls=%async_computation.1 | async-start | bytes 2097152 | tf_op jit(solution)/shard_map/all_to_all | solution.py:785
  17.8 0.6 shard_map.115
  18.5 0.0 copy-start.3
  18.5 1.0 copy-done.3
  19.5 4.8 %shard_map.116 = (f32[4,512,128]{2,1,0:T(8,128)}, f32[512,128]{1,0:T(8,128)}, f32[4,8,128]{2,1,0:T(8,128)}, f32[4,8,128]{2,1,0:T(8,128)}, f32[4,8,128]{2,1,0:T(8,128)}, /*index=5*/f32[4,8,128]{2,1,0:T(8,128)}) custom-call(s32[4]{0:T(128)} %copy-done.11, f32[4,8,128,128]{3,2,1,0:T(8,128)} %bitcast.11, f32[4,8,64,128]{3,2,1,0:T(8,128)} %copy-done.2, ...), custom_call_target="tpu_custom_call" | custom-call | tf_op jit(solution)/shard_map/pallas_call | solution.py:787
  24.3 10.2 %all-to-all-done.1.refs_0_ = f32[32,64,128]{2,1,0:T(8,128)} async-done(((f32[32,64,128]{2,1,0:T(8,128)}), f32[32,64,128]{2,1,0:T(8,128)}, u32[]{:S(2)}, u32[]{:S(2)}) %all-to-all-start.1) | async-done | bytes 1048608 | tf_op jit(solution)/shard_map/all_to_all | solution.py:785
  34.5 7.1 %all-to-all-start = ((f32[8,288,128]{2,1,0:T(8,128)}), f32[8,288,128]{2,1,0:T(8,128)}, u32[]{:S(2)}, u32[]{:S(2)}) async-start(f32[8,288,128]{2,1,0:T(8,128)} %copy-done.3), calls=%async_computation | async-start | bytes 2359296 | tf_op jit(solution)/shard_map/all_to_all | solution.py:802
  41.6 3.3 %collective-permute-start.2 = (f32[4,8,128]{2,1,0:T(8,128)S(1)}, f32[4,8,128]{2,1,0:T(8,128)S(1)}, u32[]{:S(2)}, u32[]{:S(2)}) collective-permute-start(f32[4,8,128]{2,1,0:T(8,128)S(1)} %copy-done.19), channel_id=1, source_target_pairs={{128,0},{8,128},{136,8},{16,136},{144,16},{24,144},{152,24},{32,15... | collective-permute-start | bytes 49160 | tf_op jit(solution)/shard_map/ppermute | solution.py:803
  45.0 2.2 %collective-permute-start.3 = (f32[4,8,128]{2,1,0:T(8,128)S(1)}, f32[4,8,128]{2,1,0:T(8,128)S(1)}, u32[]{:S(2)}, u32[]{:S(2)}) collective-permute-start(f32[4,8,128]{2,1,0:T(8,128)S(1)} %copy-done.18), channel_id=1, source_target_pairs={{0,128},{128,8},{8,136},{136,16},{16,144},{144,24},{24,152},{152,3... | collective-permute-start | bytes 49160 | tf_op jit(solution)/shard_map/ppermute | solution.py:804
  47.2 2.7 %collective-permute-start.4 = (f32[4,8,128]{2,1,0:T(8,128)S(1)}, f32[4,8,128]{2,1,0:T(8,128)S(1)}, u32[]{:S(2)}, u32[]{:S(2)}) collective-permute-start(f32[4,8,128]{2,1,0:T(8,128)S(1)} %copy-done.17), channel_id=1, source_target_pairs={{0,7},{1,0},{2,1},{3,2},{4,3},{5,4},{6,5},{7,6},{8,15},{9,8},{10,9... | collective-permute-start | bytes 49160 | tf_op jit(solution)/shard_map/ppermute | solution.py:805
  50.0 0.0 collective-permute-start.5
  50.0 8.8 %shard_map.117.xbuf_in = f32[32,72,128]{2,1,0:T(8,128)} custom-call(s32[4]{0:T(128)} %copy-done.11, f32[32,64,128]{2,1,0:T(8,128)} %all-to-all-done.1.refs_0_, bf16[512,1024]{1,0:T(8,128)(2,1)} %constant.32.clone.refs_1_, bf16[512,1024]{1,0:T(8,128)(2,1)} %constant.33.clone.refs_2_, bf16[512,1024]{1,0:T(8,128)(2,1)} %constant.34.clone.refs_3_, ...), custom_call_target="tpu_custom_call" | custom-call | tf_op jit(solution)/shard_map/pallas_call | solution.py:808
  58.8 7.7 %collective-permute-done.4.ghost_n = f32[4,8,128]{2,1,0:T(8,128)S(1)} collective-permute-done((f32[4,8,128]{2,1,0:T(8,128)S(1)}, f32[4,8,128]{2,1,0:T(8,128)S(1)}, u32[]{:S(2)}, u32[]{:S(2)}) %collective-permute-start.4) | collective-permute-done | bytes 16416 | tf_op jit(solution)/shard_map/ppermute | solution.py:805
  66.5 7.1 %all-to-all-done.yin = f32[8,288,128]{2,1,0:T(8,128)} async-done(((f32[8,288,128]{2,1,0:T(8,128)}), f32[8,288,128]{2,1,0:T(8,128)}, u32[]{:S(2)}, u32[]{:S(2)}) %all-to-all-start) | async-done | bytes 1179680 | tf_op jit(solution)/shard_map/all_to_all | solution.py:802
  73.6 2.7 %shard_map.118 = (f32[32,72,128]{2,1,0:T(8,128)}, f32[32,128]{1,0:T(8,128)}) custom-call(s32[4]{0:T(128)} %copy-done.11, f32[8,288,128]{2,1,0:T(8,128)} %all-to-all-done.yin, s32[1,128]{1,0:T(1,128)} %bitcast.20, s32[1,128]{1,0:T(1,128)} %bitcast.21, f32[32,72,128]{2,1,0:T(8,128)} %shard_map.117.xbuf_in), custom_call_target="tpu_custom_call", output_to_operand_aliasing={{0}: (4, {})} | custom-call | tf_op jit(solution)/shard_map/pallas_call | solution.py:818
  76.3 0.0 copy-start.7
  76.3 5.2 %all-to-all-start.2 = ((f32[32,72,128]{2,1,0:T(8,128)}), f32[32,72,128]{2,1,0:T(8,128)}, u32[]{:S(2)}, u32[]{:S(2)}) async-start(f32[32,72,128]{2,1,0:T(8,128)} %get-tuple-element.74), calls=%async_computation.2 | async-start | bytes 2359296 | tf_op jit(solution)/shard_map/all_to_all | solution.py:828
  81.5 0.0 copy-start.6
  81.6 0.0 copy-start.15
  81.6 0.8 copy-done.15
  82.4 3.9 %shard_map.120 = (f32[4,64,8,128]{3,2,1,0:T(8,128)S(1)}, f32[64,8,128]{2,1,0:T(8,128)S(1)}, f32[33,8,128]{2,1,0:T(8,128)S(1)}, f32[33,8,128]{2,1,0:T(8,128)S(1)}) custom-call(s32[4]{0:T(128)S(1)} %copy-done.12, f32[4,64,8,128]{3,2,1,0:T(8,128)S(1)} %bitcast.16, f32[64,8,128]{2,1,0:T(8,128)S(1)} %bitcast.17, f32[4,8,128]{2,1,0:T(8,128)S(1)} %collective-permute-done.3.ghost_w, ...), custom_call_target="tpu_custom_call" | custom-call | tf_op jit(solution)/shard_map/pallas_call | solution.py:137
  86.3 0.1 collective-permute-start.6
  86.4 1.5 %collective-permute-start.7 = (f32[33,8,128]{2,1,0:T(8,128)S(1)}, f32[33,8,128]{2,1,0:T(8,128)S(1)}, u32[]{:S(2)}, u32[]{:S(2)}) collective-permute-start(f32[33,8,128]{2,1,0:T(8,128)S(1)} %get-tuple-element.83), channel_id=1, source_target_pairs={{0,1},{1,2},{2,3},{3,4},{4,5},{5,6},{6,7},{7,0},{8,9},{9,10},{10,1... | collective-permute-start | bytes 405512 | tf_op jit(solution)/shard_map/ppermute | solution.py:835
  87.8 5.7 %shard_map.119 = f32[8,256,128]{2,1,0:T(8,128)} custom-call(s32[4]{0:T(128)S(1)} %copy-done.12, f32[8,288,128]{2,1,0:T(8,128)} %all-to-all-done.yin, bf16[1024,512]{1,0:T(8,128)(2,1)S(1)} %copy-done.7, bf16[1024,512]{1,0:T(8,128)(2,1)S(1)} %copy-done.6), custom_call_target="tpu_custom_call" | custom-call | tf_op jit(solution)/shard_map/pallas_call | solution.py:137
  93.5 2.3 %shard_map.121 = (f32[64,8,256]{2,1,0:T(8,128)S(1)}, f32[2,8,256]{2,1,0:T(8,128)S(1)}, f32[49,8,256]{2,1,0:T(8,128)S(1)}, f32[49,8,256]{2,1,0:T(8,128)S(1)}) custom-call(s32[4]{0:T(128)S(1)} %copy-done.12, f32[64,8,128]{2,1,0:T(8,128)S(1)} %get-tuple-element.85.partial, f32[4,64,8,128]{3,2,1,0:T(8,128)S(1)} %get-tuple-element.86.star.star_far, ...), custom_call_target="tpu_custom_call" | custom-call | tf_op jit(solution)/shard_map/pallas_call | solution.py:137
  95.9 0.8 copy-done.9
  96.6 0.6 copy-done.14
  97.2 2.3 %all-to-all-done.2.xback_far = f32[32,72,128]{2,1,0:T(8,128)} async-done(((f32[32,72,128]{2,1,0:T(8,128)}), f32[32,72,128]{2,1,0:T(8,128)}, u32[]{:S(2)}, u32[]{:S(2)}) %all-to-all-start.2) | async-done | bytes 1179680 | tf_op jit(solution)/shard_map/all_to_all | solution.py:828
  99.5 4.2 %all-to-all-start.3 = ((f32[8,256,128]{2,1,0:T(8,128)}), f32[8,256,128]{2,1,0:T(8,128)}, u32[]{:S(2)}, u32[]{:S(2)}) async-start(f32[8,256,128]{2,1,0:T(8,128)} %shard_map.119), calls=%async_computation.3 | async-start | bytes 2097152 | tf_op jit(solution)/shard_map/all_to_all | solution.py:846
  103.8 3.1 %collective-permute-start.8 = (f32[49,8,256]{2,1,0:T(8,128)S(1)}, f32[49,8,256]{2,1,0:T(8,128)}, u32[]{:S(2)}, u32[]{:S(2)}) collective-permute-start(f32[49,8,256]{2,1,0:T(8,128)S(1)} %get-tuple-element.96), channel_id=1, source_target_pairs={{128,0},{8,128},{136,8},{16,136},{144,16},{24,144},{152,24},{32,15... | collective-permute-start | bytes 1204232 | tf_op jit(solution)/shard_map/ppermute | solution.py:848
  106.9 2.5 %collective-permute-start.9 = (f32[49,8,256]{2,1,0:T(8,128)S(1)}, f32[49,8,256]{2,1,0:T(8,128)}, u32[]{:S(2)}, u32[]{:S(2)}) collective-permute-start(f32[49,8,256]{2,1,0:T(8,128)S(1)} %get-tuple-element.97), channel_id=1, source_target_pairs={{0,128},{128,8},{8,136},{136,16},{16,144},{144,24},{24,152},{152,3... | collective-permute-start | bytes 1204232 | tf_op jit(solution)/shard_map/ppermute | solution.py:849
  109.3 4.1 %shard_map.122 = (f32[8,256,128]{2,1,0:T(8,128)}, f32[1,128]{1,0:T(1,128)}) custom-call(s32[4]{0:T(128)} %copy-done.11, f32[4,8,128,128]{3,2,1,0:T(8,128)} %bitcast.12, f32[4,8,64,128]{3,2,1,0:T(8,128)} %copy-done.2, f32[32,72,128]{2,1,0:T(8,128)} %all-to-all-done.2.xback_far), custom_call_target="tpu_custom_call" | custom-call | tf_op jit(solution)/shard_map/pallas_call | solution.py:850
  113.5 0.7 collective-permute-done.9.from_w_far
  114.1 14.9 %shard_map.123 = (f32[4,8,128,128]{3,2,1,0:T(8,128)}, f32[4,8,64,128]{3,2,1,0:T(8,128)}) custom-call(s32[4]{0:T(128)} %copy-done.11, f32[64,8,256]{2,1,0:T(8,128)} %copy-done.9, f32[4,64,8,128]{3,2,1,0:T(8,128)} %copy-done.5, f32[2,8,256]{2,1,0:T(8,128)} %copy-done.14, f32[49,8,256]{2,1,0:T(8,128)} %collective-permute-done.9.from_w_far, ...), custom_call_target="tpu_custom_call" | custom-call | tf_op jit(solution)/shard_map/pallas_call | solution.py:857
  129.1 1.7 %all-to-all-done.3.yback_far = f32[8,256,128]{2,1,0:T(8,128)} async-done(((f32[8,256,128]{2,1,0:T(8,128)}), f32[8,256,128]{2,1,0:T(8,128)}, u32[]{:S(2)}, u32[]{:S(2)}) %all-to-all-start.3) | async-done | bytes 1048608 | tf_op jit(solution)/shard_map/all_to_all | solution.py:846
  130.8 3.2 %shard_map.124 = (f32[4,8,128,128]{3,2,1,0:T(8,128)}, f32[4,8,64,128]{3,2,1,0:T(8,128)}) custom-call(s32[4]{0:T(128)} %copy-done.11, f32[8,256,128]{2,1,0:T(8,128)} %get-tuple-element.105.base_far, f32[8,256,128]{2,1,0:T(8,128)} %all-to-all-done.3.yback_far, ...), custom_call_target="tpu_custom_call", output_to_operand_aliasing={{0}: (3, {}), {1}: (4, {})} | custom-call | tf_op jit(solution)/shard_map/pallas_call | solution.py:868
  134.0 2.7 %collective-permute-start.10 = (f32[4,8,64,128]{3,2,1,0:T(8,128)}, f32[4,8,64,128]{3,2,1,0:T(8,128)S(1)}, u32[]{:S(2)}, u32[]{:S(2)}) collective-permute-start(f32[4,8,64,128]{3,2,1,0:T(8,128)} %get-tuple-element.109), channel_id=1, source_target_pairs={{0,128},{128,0},{1,129},{129,1},{2,130},{130,2},{3,131},{131,3},{4... | collective-permute-start | bytes 3145736 | tf_op jit(solution)/shard_map/ppermute | solution.py:875
  136.7 2.5 %collective-permute-done.10.theirs = f32[4,8,64,128]{3,2,1,0:T(8,128)S(1)} collective-permute-done((f32[4,8,64,128]{3,2,1,0:T(8,128)}, f32[4,8,64,128]{3,2,1,0:T(8,128)S(1)}, u32[]{:S(2)}, u32[]{:S(2)}) %collective-permute-start.10) | collective-permute-done | bytes 1048608 | tf_op jit(solution)/shard_map/ppermute | solution.py:875
  139.2 1.5 %shard_map.125 = f32[4,8,128,128]{3,2,1,0:T(8,128)} custom-call(s32[4]{0:T(128)S(1)} %copy-done.13, f32[4,8,64,128]{3,2,1,0:T(8,128)S(1)} %collective-permute-done.10.theirs, f32[4,8,128,128]{3,2,1,0:T(8,128)} %get-tuple-element.110.joined_in), custom_call_target="tpu_custom_call", output_to_operand_aliasing={{}: (2, {})} | custom-call | tf_op jit(solution)/shard_map/pallas_call | solution.py:876
  (36 shorter events, 0.1 us)
Async XLA Ops:
  0.7 17.1 %copy-start.11 = (s32[4]{0:T(128)}, s32[4]{0:T(128)S(1)}, u32[]{:S(2)}) copy-start(s32[4]{0:T(128)S(1)} %pad_add_fusion.place) | copy-start | bytes 52
  0.7 1.6 %copy-start = (f32[1,4,8,128,128]{4,3,2,1,0:T(8,128)S(1)}, f32[1,4,8,128,128]{4,3,2,1,0:T(8,128)}, u32[]{:S(2)}) copy-start(f32[1,4,8,128,128]{4,3,2,1,0:T(8,128)} %param.10) | copy-start | bytes 6291460
  2.3 6.3 %copy-start.1 = (f32[1,4,8,128,128]{4,3,2,1,0:T(8,128)S(1)}, f32[1,4,8,128,128]{4,3,2,1,0:T(8,128)}, u32[]{:S(2)}) copy-start(f32[1,4,8,128,128]{4,3,2,1,0:T(8,128)} %param.10) | copy-start | bytes 6291460
  3.0 5.6 %collective-permute-start = (f32[4,8,64,128]{3,2,1,0:T(8,128)S(1)}, f32[4,8,64,128]{3,2,1,0:T(8,128)S(1)}, u32[]{:S(2)}, u32[]{:S(2)}) collective-permute-start(f32[4,8,64,128]{3,2,1,0:T(8,128)S(1)} %get-tuple-element.57), channel_id=1, source_target_pairs={{0,128},{128,0},{1,129},{129,1},{2,130},{130,2},{3,131},{131,3},{4... | collective-permute-start | bytes 3145736 | tf_op jit(solution)/shard_map/ppermute | solution.py:782
  6.3 6.0 %collective-permute-start.1 = (f32[4,8,128]{2,1,0:T(8,128)S(1)}, f32[4,8,128]{2,1,0:T(8,128)S(1)}, u32[]{:S(2)}, u32[]{:S(2)}) collective-permute-start(f32[4,8,128]{2,1,0:T(8,128)S(1)} %get-tuple-element.58), channel_id=1, source_target_pairs={{64,0},{65,1},{66,2},{67,3},{68,4},{69,5},{70,6},{71,7},{192,128},... | collective-permute-start | bytes 49160 | tf_op jit(solution)/shard_map/ppermute | solution.py:781
  8.6 9.2 %copy-start.2 = (f32[4,8,64,128]{3,2,1,0:T(8,128)}, f32[4,8,64,128]{3,2,1,0:T(8,128)S(1)}, u32[]{:S(2)}) copy-start(f32[4,8,64,128]{3,2,1,0:T(8,128)S(1)} %collective-permute-done.got) | copy-start | bytes 3145732
  10.0 1.0 copy-start.4
  12.3 22.2 %all-to-all-start.1 = ((f32[32,64,128]{2,1,0:T(8,128)}), f32[32,64,128]{2,1,0:T(8,128)}, u32[]{:S(2)}, u32[]{:S(2)}) async-start(f32[32,64,128]{2,1,0:T(8,128)} %copy-done.4), calls=%async_computation.1 | async-start | bytes 2097152 | tf_op jit(solution)/shard_map/all_to_all | solution.py:785
  18.5 1.0 copy-start.3
  24.3 17.4 %copy-start.19 = (f32[4,8,128]{2,1,0:T(8,128)S(1)}, f32[4,8,128]{2,1,0:T(8,128)}, u32[]{:S(2)}) copy-start(f32[4,8,128]{2,1,0:T(8,128)} %get-tuple-element.68) | copy-start | bytes 49156
  24.3 20.7 %copy-start.18 = (f32[4,8,128]{2,1,0:T(8,128)S(1)}, f32[4,8,128]{2,1,0:T(8,128)}, u32[]{:S(2)}) copy-start(f32[4,8,128]{2,1,0:T(8,128)} %get-tuple-element.69) | copy-start | bytes 49156
  24.3 22.9 %copy-start.17 = (f32[4,8,128]{2,1,0:T(8,128)S(1)}, f32[4,8,128]{2,1,0:T(8,128)}, u32[]{:S(2)}) copy-start(f32[4,8,128]{2,1,0:T(8,128)} %get-tuple-element.70) | copy-start | bytes 49156
  24.3 25.7 %copy-start.16 = (f32[4,8,128]{2,1,0:T(8,128)S(1)}, f32[4,8,128]{2,1,0:T(8,128)}, u32[]{:S(2)}) copy-start(f32[4,8,128]{2,1,0:T(8,128)} %get-tuple-element.71) | copy-start | bytes 49156
  34.5 39.1 %all-to-all-start = ((f32[8,288,128]{2,1,0:T(8,128)}), f32[8,288,128]{2,1,0:T(8,128)}, u32[]{:S(2)}, u32[]{:S(2)}) async-start(f32[8,288,128]{2,1,0:T(8,128)} %copy-done.3), calls=%async_computation | async-start | bytes 2359296 | tf_op jit(solution)/shard_map/all_to_all | solution.py:802
  41.6 17.1 %collective-permute-start.2 = (f32[4,8,128]{2,1,0:T(8,128)S(1)}, f32[4,8,128]{2,1,0:T(8,128)S(1)}, u32[]{:S(2)}, u32[]{:S(2)}) collective-permute-start(f32[4,8,128]{2,1,0:T(8,128)S(1)} %copy-done.19), channel_id=1, source_target_pairs={{128,0},{8,128},{136,8},{16,136},{144,16},{24,144},{152,24},{32,15... | collective-permute-start | bytes 49160 | tf_op jit(solution)/shard_map/ppermute | solution.py:803
  45.0 13.8 %collective-permute-start.3 = (f32[4,8,128]{2,1,0:T(8,128)S(1)}, f32[4,8,128]{2,1,0:T(8,128)S(1)}, u32[]{:S(2)}, u32[]{:S(2)}) collective-permute-start(f32[4,8,128]{2,1,0:T(8,128)S(1)} %copy-done.18), channel_id=1, source_target_pairs={{0,128},{128,8},{8,136},{136,16},{16,144},{144,24},{24,152},{152,3... | collective-permute-start | bytes 49160 | tf_op jit(solution)/shard_map/ppermute | solution.py:804
  47.2 19.3 %collective-permute-start.4 = (f32[4,8,128]{2,1,0:T(8,128)S(1)}, f32[4,8,128]{2,1,0:T(8,128)S(1)}, u32[]{:S(2)}, u32[]{:S(2)}) collective-permute-start(f32[4,8,128]{2,1,0:T(8,128)S(1)} %copy-done.17), channel_id=1, source_target_pairs={{0,7},{1,0},{2,1},{3,2},{4,3},{5,4},{6,5},{7,6},{8,15},{9,8},{10,9... | collective-permute-start | bytes 49160 | tf_op jit(solution)/shard_map/ppermute | solution.py:805
  50.0 16.5 %collective-permute-start.5 = (f32[4,8,128]{2,1,0:T(8,128)S(1)}, f32[4,8,128]{2,1,0:T(8,128)S(1)}, u32[]{:S(2)}, u32[]{:S(2)}) collective-permute-start(f32[4,8,128]{2,1,0:T(8,128)S(1)} %copy-done.16), channel_id=1, source_target_pairs={{0,1},{1,2},{2,3},{3,4},{4,5},{5,6},{6,7},{7,0},{8,9},{9,10},{10,1... | collective-permute-start | bytes 49160 | tf_op jit(solution)/shard_map/ppermute | solution.py:806
  76.3 5.3 %copy-start.8 = (f32[4,512,128]{2,1,0:T(8,128)S(1)}, f32[4,512,128]{2,1,0:T(8,128)}, u32[]{:S(2)}) copy-start(f32[4,512,128]{2,1,0:T(8,128)} %get-tuple-element.60) | copy-start | bytes 3145732
  76.3 5.3 %copy-start.10 = (f32[512,128]{1,0:T(8,128)S(1)}, f32[512,128]{1,0:T(8,128)}, u32[]{:S(2)}) copy-start(f32[512,128]{1,0:T(8,128)} %get-tuple-element.61) | copy-start | bytes 786436
  76.3 5.3 %copy-start.12 = (s32[4]{0:T(128)S(1)}, s32[4]{0:T(128)}, u32[]{:S(2)}) copy-start(s32[4]{0:T(128)} %copy-done.11) | copy-start | bytes 52
  76.3 11.5 %copy-start.7 = (bf16[1024,512]{1,0:T(8,128)(2,1)S(1)}, bf16[1024,512]{1,0:T(8,128)(2,1)}, u32[]{:S(2)}) copy-start(bf16[1024,512]{1,0:T(8,128)(2,1)} %constant.30.clone.table_high) | copy-start | bytes 3145732
  76.3 23.2 %all-to-all-start.2 = ((f32[32,72,128]{2,1,0:T(8,128)}), f32[32,72,128]{2,1,0:T(8,128)}, u32[]{:S(2)}, u32[]{:S(2)}) async-start(f32[32,72,128]{2,1,0:T(8,128)} %get-tuple-element.74), calls=%async_computation.2 | async-start | bytes 2359296 | tf_op jit(solution)/shard_map/all_to_all | solution.py:828
  81.5 6.3 %copy-start.6 = (bf16[1024,512]{1,0:T(8,128)(2,1)S(1)}, bf16[1024,512]{1,0:T(8,128)(2,1)}, u32[]{:S(2)}) copy-start(bf16[1024,512]{1,0:T(8,128)(2,1)} %constant.31.clone.table_low) | copy-start | bytes 3145732
  81.6 0.8 copy-start.15
  86.3 7.3 %copy-start.5 = (f32[4,64,8,128]{3,2,1,0:T(8,128)}, f32[4,64,8,128]{3,2,1,0:T(8,128)S(1)}, u32[]{:S(2)}) copy-start(f32[4,64,8,128]{3,2,1,0:T(8,128)S(1)} %get-tuple-element.86.star.star_far) | copy-start | bytes 3145732
  86.3 7.3 %collective-permute-start.6 = (f32[33,8,128]{2,1,0:T(8,128)S(1)}, f32[33,8,128]{2,1,0:T(8,128)S(1)}, u32[]{:S(2)}, u32[]{:S(2)}) collective-permute-start(f32[33,8,128]{2,1,0:T(8,128)S(1)} %get-tuple-element.82), channel_id=1, source_target_pairs={{0,7},{1,0},{2,1},{3,2},{4,3},{5,4},{6,5},{7,6},{8,15},{9,8},{10,9... | collective-permute-start | bytes 405512 | tf_op jit(solution)/shard_map/ppermute | solution.py:834
  86.4 7.2 %collective-permute-start.7 = (f32[33,8,128]{2,1,0:T(8,128)S(1)}, f32[33,8,128]{2,1,0:T(8,128)S(1)}, u32[]{:S(2)}, u32[]{:S(2)}) collective-permute-start(f32[33,8,128]{2,1,0:T(8,128)S(1)} %get-tuple-element.83), channel_id=1, source_target_pairs={{0,1},{1,2},{2,3},{3,4},{4,5},{5,6},{6,7},{7,0},{8,9},{9,10},{10,1... | collective-permute-start | bytes 405512 | tf_op jit(solution)/shard_map/ppermute | solution.py:835
  95.9 0.8 copy-start.9
  96.6 0.6 copy-start.14
  99.5 31.3 %all-to-all-start.3 = ((f32[8,256,128]{2,1,0:T(8,128)}), f32[8,256,128]{2,1,0:T(8,128)}, u32[]{:S(2)}, u32[]{:S(2)}) async-start(f32[8,256,128]{2,1,0:T(8,128)} %shard_map.119), calls=%async_computation.3 | async-start | bytes 2097152 | tf_op jit(solution)/shard_map/all_to_all | solution.py:846
  103.8 9.7 %collective-permute-start.8 = (f32[49,8,256]{2,1,0:T(8,128)S(1)}, f32[49,8,256]{2,1,0:T(8,128)}, u32[]{:S(2)}, u32[]{:S(2)}) collective-permute-start(f32[49,8,256]{2,1,0:T(8,128)S(1)} %get-tuple-element.96), channel_id=1, source_target_pairs={{128,0},{8,128},{136,8},{16,136},{144,16},{24,144},{152,24},{32,15... | collective-permute-start | bytes 1204232 | tf_op jit(solution)/shard_map/ppermute | solution.py:848
  106.9 7.2 %collective-permute-start.9 = (f32[49,8,256]{2,1,0:T(8,128)S(1)}, f32[49,8,256]{2,1,0:T(8,128)}, u32[]{:S(2)}, u32[]{:S(2)}) collective-permute-start(f32[49,8,256]{2,1,0:T(8,128)S(1)} %get-tuple-element.97), channel_id=1, source_target_pairs={{0,128},{128,8},{8,136},{136,16},{16,144},{144,24},{24,152},{152,3... | collective-permute-start | bytes 1204232 | tf_op jit(solution)/shard_map/ppermute | solution.py:849
  130.8 8.4 %copy-start.13 = (s32[4]{0:T(128)S(1)}, s32[4]{0:T(128)}, u32[]{:S(2)}) copy-start(s32[4]{0:T(128)} %copy-done.11) | copy-start | bytes 52
  134.0 5.2 %collective-permute-start.10 = (f32[4,8,64,128]{3,2,1,0:T(8,128)}, f32[4,8,64,128]{3,2,1,0:T(8,128)S(1)}, u32[]{:S(2)}, u32[]{:S(2)}) collective-permute-start(f32[4,8,64,128]{3,2,1,0:T(8,128)} %get-tuple-element.109), channel_id=1, source_target_pairs={{0,128},{128,0},{1,129},{129,1},{2,130},{130,2},{3,131},{131,3},{4... | collective-permute-start | bytes 3145736 | tf_op jit(solution)/shard_map/ppermute | solution.py:875

commit v4 on v3

--- a/solution.py
+++ b/solution.py
@@ -239,10 +239,17 @@
     share = weight_near[...].astype(F32) / 16.0
     first = first_near[...]
     follow = jnp.where(first == NY - 1, 0, first + 1)
-    table = jnp.where(rows == first, share, 0.0) + jnp.where(rows == follow, 1.0 - share, 0.0)
+    table = jnp.where(rows == first, share, jnp.where(rows == follow, 1.0 - share, 0.0))
+    table = table.astype(BF16)
     wait_all(loads[2:])
     plane = jnp.concatenate([planes[g] for g in range(GY)], axis=1)
-    blended = jnp.dot(plane, table, precision=lax.Precision.HIGHEST, preferred_element_type=F32)
+    high, rest = halves(plane)
+    middle = plane - high.astype(F32)
+    low = (middle - rest.astype(F32)).astype(BF16)
+    parts = jnp.dot(
+        jnp.concatenate([high, rest, low], axis=0), table, preferred_element_type=F32
+    )
+    blended = parts[: 4 * NZ] + (parts[4 * NZ : 8 * NZ] + parts[8 * NZ :])
     inflow[...] = blended
     for r in range(4 * NZ):
         rims[r] = jnp.broadcast_to(blended[r : r + 1], (8, BY))

time: 142 us -> 142 us (level)
  no operation moved by 1% of the time
where the time goes in v4:
time: 142 us; the launch traced here: 141 us
  Pallas kernels  54.4 us (38%)
  starting transfers between devices  44.8 us (32%)
  waiting for transfers between devices  34.4 us (24%)
  local copies, waits for them, and re-layouts  5.84 us (4%)
    pallas_call x1, Pallas kernels, on_device(): raw_call(pressure_kernel, 5, [(4, NZ, BX, BY), half_block], vmem(block, (...  14.9 us
    pallas_call x6, Pallas kernels, call(): pl.pallas_call(body, out_shape=[jax.ShapeDtypeStruct(shape, F32) for shap...  14.6 us
    all_to_all x1, waiting for transfers between devices, on_device(): xin = lax.all_to_all(packed, x_axes, 0, 0, tiled=True)  10.2 us
    pallas_call x1, Pallas kernels, on_device(): staged_call(line_kernel, ins, [(32, 72, BY)], scratch=[pltpu.VMEM((NX //...  8.79 us
    ppermute x1, waiting for transfers between devices, on_device(): ghost_n = lax.ppermute(col_low, 'gy', along_y(-1))  7.71 us
    all_to_all x1, starting transfers between devices, on_device(): yin = lax.all_to_all(ybuf, 'gy', 0, 0, tiled=True)  7.13 us
    all_to_all x1, waiting for transfers between devices, on_device(): yin = lax.all_to_all(ybuf, 'gy', 0, 0, tiled=True)  7.13 us
    unnamed x40, local copies, waits for them, and re-layouts  5.84 us
  transfers between devices with their start and end apart: 15, of which 9 were waited for; matrix products, arithmetic and copies ran while one was open for 0% of the time, Pallas kernels for 33%

profile of v4, /device:TPU:1, one launch (start us, length us, event | category | flops | bytes accessed | tf_op | source)
XLA Modules:
  0.0 140.7 jit_solution(5813391572419721932)
XLA Ops:
  0.6 0.1 pad_add_fusion.place
  0.7 1.6 %copy-done = f32[1,4,8,128,128]{4,3,2,1,0:T(8,128)S(1)} copy-done((f32[1,4,8,128,128]{4,3,2,1,0:T(8,128)S(1)}, f32[1,4,8,128,128]{4,3,2,1,0:T(8,128)}, u32[]{:S(2)}) %copy-start) | copy-done | bytes 2097176
  2.3 0.6 shard_map.113
  3.0 3.3 %collective-permute-start = (f32[4,8,64,128]{3,2,1,0:T(8,128)S(1)}, f32[4,8,64,128]{3,2,1,0:T(8,128)S(1)}, u32[]{:S(2)}, u32[]{:S(2)}) collective-permute-start(f32[4,8,64,128]{3,2,1,0:T(8,128)S(1)} %get-tuple-element.57), channel_id=1, source_target_pairs={{0,128},{128,0},{1,129},{129,1},{2,130},{130,2},{3,131},{131,3},{4... | collective-permute-start | bytes 3145736 | tf_op jit(solution)/shard_map/ppermute | solution.py:789
  6.3 1.3 collective-permute-start.1
  7.6 1.0 collective-permute-done.got
  8.6 1.4 %shard_map.114 = f32[32,64,128]{2,1,0:T(8,128)S(1)} custom-call(s32[4]{0:T(128)S(1)} %pad_add_fusion.place, f32[4,8,128,128]{3,2,1,0:T(8,128)S(1)} %bitcast.14, f32[4,8,64,128]{3,2,1,0:T(8,128)S(1)} %collective-permute-done.got), custom_call_target="tpu_custom_call" | custom-call | tf_op jit(solution)/shard_map/pallas_call | solution.py:137
  10.0 1.0 copy-done.4
  11.0 1.2 collective-permute-done.1.column
  12.3 5.5 %all-to-all-start.1 = ((f32[32,64,128]{2,1,0:T(8,128)}), f32[32,64,128]{2,1,0:T(8,128)}, u32[]{:S(2)}, u32[]{:S(2)}) async-start(f32[32,64,128]{2,1,0:T(8,128)} %copy-done.4), calls=%async_computation.1 | async-start | bytes 2097152 | tf_op jit(solution)/shard_map/all_to_all | solution.py:792
  17.8 0.6 shard_map.115
  18.5 0.0 copy-start.3
  18.5 1.0 copy-done.3
  19.5 4.8 %shard_map.116 = (f32[4,512,128]{2,1,0:T(8,128)}, f32[512,128]{1,0:T(8,128)}, f32[4,8,128]{2,1,0:T(8,128)}, f32[4,8,128]{2,1,0:T(8,128)}, f32[4,8,128]{2,1,0:T(8,128)}, /*index=5*/f32[4,8,128]{2,1,0:T(8,128)}) custom-call(s32[4]{0:T(128)} %copy-done.11, f32[4,8,128,128]{3,2,1,0:T(8,128)} %bitcast.11, f32[4,8,64,128]{3,2,1,0:T(8,128)} %copy-done.2, ...), custom_call_target="tpu_custom_call" | custom-call | tf_op jit(solution)/shard_map/pallas_call | solution.py:794
  24.3 10.2 %all-to-all-done.1.refs_0_ = f32[32,64,128]{2,1,0:T(8,128)} async-done(((f32[32,64,128]{2,1,0:T(8,128)}), f32[32,64,128]{2,1,0:T(8,128)}, u32[]{:S(2)}, u32[]{:S(2)}) %all-to-all-start.1) | async-done | bytes 1048608 | tf_op jit(solution)/shard_map/all_to_all | solution.py:792
  34.5 7.1 %all-to-all-start = ((f32[8,288,128]{2,1,0:T(8,128)}), f32[8,288,128]{2,1,0:T(8,128)}, u32[]{:S(2)}, u32[]{:S(2)}) async-start(f32[8,288,128]{2,1,0:T(8,128)} %copy-done.3), calls=%async_computation | async-start | bytes 2359296 | tf_op jit(solution)/shard_map/all_to_all | solution.py:809
  41.6 3.3 %collective-permute-start.2 = (f32[4,8,128]{2,1,0:T(8,128)S(1)}, f32[4,8,128]{2,1,0:T(8,128)S(1)}, u32[]{:S(2)}, u32[]{:S(2)}) collective-permute-start(f32[4,8,128]{2,1,0:T(8,128)S(1)} %copy-done.19), channel_id=1, source_target_pairs={{128,0},{8,128},{136,8},{16,136},{144,16},{24,144},{152,24},{32,15... | collective-permute-start | bytes 49160 | tf_op jit(solution)/shard_map/ppermute | solution.py:810
  45.0 2.2 %collective-permute-start.3 = (f32[4,8,128]{2,1,0:T(8,128)S(1)}, f32[4,8,128]{2,1,0:T(8,128)S(1)}, u32[]{:S(2)}, u32[]{:S(2)}) collective-permute-start(f32[4,8,128]{2,1,0:T(8,128)S(1)} %copy-done.18), channel_id=1, source_target_pairs={{0,128},{128,8},{8,136},{136,16},{16,144},{144,24},{24,152},{152,3... | collective-permute-start | bytes 49160 | tf_op jit(solution)/shard_map/ppermute | solution.py:811
  47.2 2.7 %collective-permute-start.4 = (f32[4,8,128]{2,1,0:T(8,128)S(1)}, f32[4,8,128]{2,1,0:T(8,128)S(1)}, u32[]{:S(2)}, u32[]{:S(2)}) collective-permute-start(f32[4,8,128]{2,1,0:T(8,128)S(1)} %copy-done.17), channel_id=1, source_target_pairs={{0,7},{1,0},{2,1},{3,2},{4,3},{5,4},{6,5},{7,6},{8,15},{9,8},{10,9... | collective-permute-start | bytes 49160 | tf_op jit(solution)/shard_map/ppermute | solution.py:812
  50.0 8.8 %shard_map.117.xbuf_in = f32[32,72,128]{2,1,0:T(8,128)} custom-call(s32[4]{0:T(128)} %copy-done.11, f32[32,64,128]{2,1,0:T(8,128)} %all-to-all-done.1.refs_0_, bf16[512,1024]{1,0:T(8,128)(2,1)} %constant.32.clone.refs_1_, bf16[512,1024]{1,0:T(8,128)(2,1)} %constant.33.clone.refs_2_, bf16[512,1024]{1,0:T(8,128)(2,1)} %constant.34.clone.refs_3_, ...), custom_call_target="tpu_custom_call" | custom-call | tf_op jit(solution)/shard_map/pallas_call | solution.py:815
  58.8 0.0 collective-permute-done.3.ghost_w
  58.8 7.7 %collective-permute-done.4.ghost_n = f32[4,8,128]{2,1,0:T(8,128)S(1)} collective-permute-done((f32[4,8,128]{2,1,0:T(8,128)S(1)}, f32[4,8,128]{2,1,0:T(8,128)S(1)}, u32[]{:S(2)}, u32[]{:S(2)}) %collective-permute-start.4) | collective-permute-done | bytes 16416 | tf_op jit(solution)/shard_map/ppermute | solution.py:812
  66.5 7.1 %all-to-all-done.yin = f32[8,288,128]{2,1,0:T(8,128)} async-done(((f32[8,288,128]{2,1,0:T(8,128)}), f32[8,288,128]{2,1,0:T(8,128)}, u32[]{:S(2)}, u32[]{:S(2)}) %all-to-all-start) | async-done | bytes 1179680 | tf_op jit(solution)/shard_map/all_to_all | solution.py:809
  73.6 2.5 %shard_map.118 = (f32[32,72,128]{2,1,0:T(8,128)}, f32[32,128]{1,0:T(8,128)}) custom-call(s32[4]{0:T(128)} %copy-done.11, f32[8,288,128]{2,1,0:T(8,128)} %all-to-all-done.yin, s32[1,128]{1,0:T(1,128)} %bitcast.20, s32[1,128]{1,0:T(1,128)} %bitcast.21, f32[32,72,128]{2,1,0:T(8,128)} %shard_map.117.xbuf_in), custom_call_target="tpu_custom_call", output_to_operand_aliasing={{0}: (4, {})} | custom-call | tf_op jit(solution)/shard_map/pallas_call | solution.py:825
  76.2 0.0 copy-start.7
  76.2 5.2 %all-to-all-start.2 = ((f32[32,72,128]{2,1,0:T(8,128)}), f32[32,72,128]{2,1,0:T(8,128)}, u32[]{:S(2)}, u32[]{:S(2)}) async-start(f32[32,72,128]{2,1,0:T(8,128)} %get-tuple-element.74), calls=%async_computation.2 | async-start | bytes 2359296 | tf_op jit(solution)/shard_map/all_to_all | solution.py:835
  81.4 0.0 copy-start.6
  81.4 0.0 copy-start.15
  81.4 0.8 copy-done.15
  82.2 3.9 %shard_map.120 = (f32[4,64,8,128]{3,2,1,0:T(8,128)S(1)}, f32[64,8,128]{2,1,0:T(8,128)S(1)}, f32[33,8,128]{2,1,0:T(8,128)S(1)}, f32[33,8,128]{2,1,0:T(8,128)S(1)}) custom-call(s32[4]{0:T(128)S(1)} %copy-done.12, f32[4,64,8,128]{3,2,1,0:T(8,128)S(1)} %bitcast.16, f32[64,8,128]{2,1,0:T(8,128)S(1)} %bitcast.17, f32[4,8,128]{2,1,0:T(8,128)S(1)} %collective-permute-done.3.ghost_w, ...), custom_call_target="tpu_custom_call" | custom-call | tf_op jit(solution)/shard_map/pallas_call | solution.py:137
  86.1 0.1 collective-permute-start.6
  86.2 1.5 %collective-permute-start.7 = (f32[33,8,128]{2,1,0:T(8,128)S(1)}, f32[33,8,128]{2,1,0:T(8,128)S(1)}, u32[]{:S(2)}, u32[]{:S(2)}) collective-permute-start(f32[33,8,128]{2,1,0:T(8,128)S(1)} %get-tuple-element.83), channel_id=1, source_target_pairs={{0,1},{1,2},{2,3},{3,4},{4,5},{5,6},{6,7},{7,0},{8,9},{9,10},{10,1... | collective-permute-start | bytes 405512 | tf_op jit(solution)/shard_map/ppermute | solution.py:842
  87.7 5.7 %shard_map.119 = f32[8,256,128]{2,1,0:T(8,128)} custom-call(s32[4]{0:T(128)S(1)} %copy-done.12, f32[8,288,128]{2,1,0:T(8,128)} %all-to-all-done.yin, bf16[1024,512]{1,0:T(8,128)(2,1)S(1)} %copy-done.7, bf16[1024,512]{1,0:T(8,128)(2,1)S(1)} %copy-done.6), custom_call_target="tpu_custom_call" | custom-call | tf_op jit(solution)/shard_map/pallas_call | solution.py:137
  93.4 2.3 %shard_map.121 = (f32[64,8,256]{2,1,0:T(8,128)S(1)}, f32[2,8,256]{2,1,0:T(8,128)S(1)}, f32[49,8,256]{2,1,0:T(8,128)S(1)}, f32[49,8,256]{2,1,0:T(8,128)S(1)}) custom-call(s32[4]{0:T(128)S(1)} %copy-done.12, f32[64,8,128]{2,1,0:T(8,128)S(1)} %get-tuple-element.85.partial, f32[4,64,8,128]{3,2,1,0:T(8,128)S(1)} %get-tuple-element.86.star.star_far, ...), custom_call_target="tpu_custom_call" | custom-call | tf_op jit(solution)/shard_map/pallas_call | solution.py:137
  95.7 0.8 copy-done.9
  96.5 0.6 copy-done.14
  97.1 2.3 %all-to-all-done.2.xback_far = f32[32,72,128]{2,1,0:T(8,128)} async-done(((f32[32,72,128]{2,1,0:T(8,128)}), f32[32,72,128]{2,1,0:T(8,128)}, u32[]{:S(2)}, u32[]{:S(2)}) %all-to-all-start.2) | async-done | bytes 1179680 | tf_op jit(solution)/shard_map/all_to_all | solution.py:835
  99.4 4.2 %all-to-all-start.3 = ((f32[8,256,128]{2,1,0:T(8,128)}), f32[8,256,128]{2,1,0:T(8,128)}, u32[]{:S(2)}, u32[]{:S(2)}) async-start(f32[8,256,128]{2,1,0:T(8,128)} %shard_map.119), calls=%async_computation.3 | async-start | bytes 2097152 | tf_op jit(solution)/shard_map/all_to_all | solution.py:853
  103.6 3.1 %collective-permute-start.8 = (f32[49,8,256]{2,1,0:T(8,128)S(1)}, f32[49,8,256]{2,1,0:T(8,128)}, u32[]{:S(2)}, u32[]{:S(2)}) collective-permute-start(f32[49,8,256]{2,1,0:T(8,128)S(1)} %get-tuple-element.96), channel_id=1, source_target_pairs={{128,0},{8,128},{136,8},{16,136},{144,16},{24,144},{152,24},{32,15... | collective-permute-start | bytes 1204232 | tf_op jit(solution)/shard_map/ppermute | solution.py:855
  106.7 2.5 %collective-permute-start.9 = (f32[49,8,256]{2,1,0:T(8,128)S(1)}, f32[49,8,256]{2,1,0:T(8,128)}, u32[]{:S(2)}, u32[]{:S(2)}) collective-permute-start(f32[49,8,256]{2,1,0:T(8,128)S(1)} %get-tuple-element.97), channel_id=1, source_target_pairs={{0,128},{128,8},{8,136},{136,16},{16,144},{144,24},{24,152},{152,3... | collective-permute-start | bytes 1204232 | tf_op jit(solution)/shard_map/ppermute | solution.py:856
  109.2 4.1 %shard_map.122 = (f32[8,256,128]{2,1,0:T(8,128)}, f32[1,128]{1,0:T(1,128)}) custom-call(s32[4]{0:T(128)} %copy-done.11, f32[4,8,128,128]{3,2,1,0:T(8,128)} %bitcast.12, f32[4,8,64,128]{3,2,1,0:T(8,128)} %copy-done.2, f32[32,72,128]{2,1,0:T(8,128)} %all-to-all-done.2.xback_far), custom_call_target="tpu_custom_call" | custom-call | tf_op jit(solution)/shard_map/pallas_call | solution.py:857
  113.3 0.7 collective-permute-done.9.from_w_far
  114.0 14.9 %shard_map.123 = (f32[4,8,128,128]{3,2,1,0:T(8,128)}, f32[4,8,64,128]{3,2,1,0:T(8,128)}) custom-call(s32[4]{0:T(128)} %copy-done.11, f32[64,8,256]{2,1,0:T(8,128)} %copy-done.9, f32[4,64,8,128]{3,2,1,0:T(8,128)} %copy-done.5, f32[2,8,256]{2,1,0:T(8,128)} %copy-done.14, f32[49,8,256]{2,1,0:T(8,128)} %collective-permute-done.9.from_w_far, ...), custom_call_target="tpu_custom_call" | custom-call | tf_op jit(solution)/shard_map/pallas_call | solution.py:864
  128.9 1.7 %all-to-all-done.3.yback_far = f32[8,256,128]{2,1,0:T(8,128)} async-done(((f32[8,256,128]{2,1,0:T(8,128)}), f32[8,256,128]{2,1,0:T(8,128)}, u32[]{:S(2)}, u32[]{:S(2)}) %all-to-all-start.3) | async-done | bytes 1048608 | tf_op jit(solution)/shard_map/all_to_all | solution.py:853
  130.6 3.2 %shard_map.124 = (f32[4,8,128,128]{3,2,1,0:T(8,128)}, f32[4,8,64,128]{3,2,1,0:T(8,128)}) custom-call(s32[4]{0:T(128)} %copy-done.11, f32[8,256,128]{2,1,0:T(8,128)} %get-tuple-element.105.base_far, f32[8,256,128]{2,1,0:T(8,128)} %all-to-all-done.3.yback_far, ...), custom_call_target="tpu_custom_call", output_to_operand_aliasing={{0}: (3, {}), {1}: (4, {})} | custom-call | tf_op jit(solution)/shard_map/pallas_call | solution.py:875
  133.8 2.7 %collective-permute-start.10 = (f32[4,8,64,128]{3,2,1,0:T(8,128)}, f32[4,8,64,128]{3,2,1,0:T(8,128)S(1)}, u32[]{:S(2)}, u32[]{:S(2)}) collective-permute-start(f32[4,8,64,128]{3,2,1,0:T(8,128)} %get-tuple-element.109), channel_id=1, source_target_pairs={{0,128},{128,0},{1,129},{129,1},{2,130},{130,2},{3,131},{131,3},{4... | collective-permute-start | bytes 3145736 | tf_op jit(solution)/shard_map/ppermute | solution.py:882
  136.5 2.5 %collective-permute-done.10.theirs = f32[4,8,64,128]{3,2,1,0:T(8,128)S(1)} collective-permute-done((f32[4,8,64,128]{3,2,1,0:T(8,128)}, f32[4,8,64,128]{3,2,1,0:T(8,128)S(1)}, u32[]{:S(2)}, u32[]{:S(2)}) %collective-permute-start.10) | collective-permute-done | bytes 1048608 | tf_op jit(solution)/shard_map/ppermute | solution.py:882
  139.0 1.5 %shard_map.125 = f32[4,8,128,128]{3,2,1,0:T(8,128)} custom-call(s32[4]{0:T(128)S(1)} %copy-done.13, f32[4,8,64,128]{3,2,1,0:T(8,128)S(1)} %collective-permute-done.10.theirs, f32[4,8,128,128]{3,2,1,0:T(8,128)} %get-tuple-element.110.joined_in), custom_call_target="tpu_custom_call", output_to_operand_aliasing={{}: (2, {})} | custom-call | tf_op jit(solution)/shard_map/pallas_call | solution.py:883
  (36 shorter events, 0.1 us)
Async XLA Ops:
  0.7 17.1 %copy-start.11 = (s32[4]{0:T(128)}, s32[4]{0:T(128)S(1)}, u32[]{:S(2)}) copy-start(s32[4]{0:T(128)S(1)} %pad_add_fusion.place) | copy-start | bytes 52
  0.7 1.6 %copy-start = (f32[1,4,8,128,128]{4,3,2,1,0:T(8,128)S(1)}, f32[1,4,8,128,128]{4,3,2,1,0:T(8,128)}, u32[]{:S(2)}) copy-start(f32[1,4,8,128,128]{4,3,2,1,0:T(8,128)} %param.10) | copy-start | bytes 6291460
  2.3 6.3 %copy-start.1 = (f32[1,4,8,128,128]{4,3,2,1,0:T(8,128)S(1)}, f32[1,4,8,128,128]{4,3,2,1,0:T(8,128)}, u32[]{:S(2)}) copy-start(f32[1,4,8,128,128]{4,3,2,1,0:T(8,128)} %param.10) | copy-start | bytes 6291460
  3.0 5.6 %collective-permute-start = (f32[4,8,64,128]{3,2,1,0:T(8,128)S(1)}, f32[4,8,64,128]{3,2,1,0:T(8,128)S(1)}, u32[]{:S(2)}, u32[]{:S(2)}) collective-permute-start(f32[4,8,64,128]{3,2,1,0:T(8,128)S(1)} %get-tuple-element.57), channel_id=1, source_target_pairs={{0,128},{128,0},{1,129},{129,1},{2,130},{130,2},{3,131},{131,3},{4... | collective-permute-start | bytes 3145736 | tf_op jit(solution)/shard_map/ppermute | solution.py:789
  6.3 6.0 %collective-permute-start.1 = (f32[4,8,128]{2,1,0:T(8,128)S(1)}, f32[4,8,128]{2,1,0:T(8,128)S(1)}, u32[]{:S(2)}, u32[]{:S(2)}) collective-permute-start(f32[4,8,128]{2,1,0:T(8,128)S(1)} %get-tuple-element.58), channel_id=1, source_target_pairs={{64,0},{65,1},{66,2},{67,3},{68,4},{69,5},{70,6},{71,7},{192,128},... | collective-permute-start | bytes 49160 | tf_op jit(solution)/shard_map/ppermute | solution.py:788
  8.6 9.2 %copy-start.2 = (f32[4,8,64,128]{3,2,1,0:T(8,128)}, f32[4,8,64,128]{3,2,1,0:T(8,128)S(1)}, u32[]{:S(2)}) copy-start(f32[4,8,64,128]{3,2,1,0:T(8,128)S(1)} %collective-permute-done.got) | copy-start | bytes 3145732
  10.0 1.0 copy-start.4
  12.3 22.2 %all-to-all-start.1 = ((f32[32,64,128]{2,1,0:T(8,128)}), f32[32,64,128]{2,1,0:T(8,128)}, u32[]{:S(2)}, u32[]{:S(2)}) async-start(f32[32,64,128]{2,1,0:T(8,128)} %copy-done.4), calls=%async_computation.1 | async-start | bytes 2097152 | tf_op jit(solution)/shard_map/all_to_all | solution.py:792
  18.5 1.0 copy-start.3
  24.3 17.4 %copy-start.19 = (f32[4,8,128]{2,1,0:T(8,128)S(1)}, f32[4,8,128]{2,1,0:T(8,128)}, u32[]{:S(2)}) copy-start(f32[4,8,128]{2,1,0:T(8,128)} %get-tuple-element.68) | copy-start | bytes 49156
  24.3 20.7 %copy-start.18 = (f32[4,8,128]{2,1,0:T(8,128)S(1)}, f32[4,8,128]{2,1,0:T(8,128)}, u32[]{:S(2)}) copy-start(f32[4,8,128]{2,1,0:T(8,128)} %get-tuple-element.69) | copy-start | bytes 49156
  24.3 22.9 %copy-start.17 = (f32[4,8,128]{2,1,0:T(8,128)S(1)}, f32[4,8,128]{2,1,0:T(8,128)}, u32[]{:S(2)}) copy-start(f32[4,8,128]{2,1,0:T(8,128)} %get-tuple-element.70) | copy-start | bytes 49156
  24.3 25.7 %copy-start.16 = (f32[4,8,128]{2,1,0:T(8,128)S(1)}, f32[4,8,128]{2,1,0:T(8,128)}, u32[]{:S(2)}) copy-start(f32[4,8,128]{2,1,0:T(8,128)} %get-tuple-element.71) | copy-start | bytes 49156
  34.5 39.1 %all-to-all-start = ((f32[8,288,128]{2,1,0:T(8,128)}), f32[8,288,128]{2,1,0:T(8,128)}, u32[]{:S(2)}, u32[]{:S(2)}) async-start(f32[8,288,128]{2,1,0:T(8,128)} %copy-done.3), calls=%async_computation | async-start | bytes 2359296 | tf_op jit(solution)/shard_map/all_to_all | solution.py:809
  41.6 17.1 %collective-permute-start.2 = (f32[4,8,128]{2,1,0:T(8,128)S(1)}, f32[4,8,128]{2,1,0:T(8,128)S(1)}, u32[]{:S(2)}, u32[]{:S(2)}) collective-permute-start(f32[4,8,128]{2,1,0:T(8,128)S(1)} %copy-done.19), channel_id=1, source_target_pairs={{128,0},{8,128},{136,8},{16,136},{144,16},{24,144},{152,24},{32,15... | collective-permute-start | bytes 49160 | tf_op jit(solution)/shard_map/ppermute | solution.py:810
  45.0 13.8 %collective-permute-start.3 = (f32[4,8,128]{2,1,0:T(8,128)S(1)}, f32[4,8,128]{2,1,0:T(8,128)S(1)}, u32[]{:S(2)}, u32[]{:S(2)}) collective-permute-start(f32[4,8,128]{2,1,0:T(8,128)S(1)} %copy-done.18), channel_id=1, source_target_pairs={{0,128},{128,8},{8,136},{136,16},{16,144},{144,24},{24,152},{152,3... | collective-permute-start | bytes 49160 | tf_op jit(solution)/shard_map/ppermute | solution.py:811
  47.2 19.3 %collective-permute-start.4 = (f32[4,8,128]{2,1,0:T(8,128)S(1)}, f32[4,8,128]{2,1,0:T(8,128)S(1)}, u32[]{:S(2)}, u32[]{:S(2)}) collective-permute-start(f32[4,8,128]{2,1,0:T(8,128)S(1)} %copy-done.17), channel_id=1, source_target_pairs={{0,7},{1,0},{2,1},{3,2},{4,3},{5,4},{6,5},{7,6},{8,15},{9,8},{10,9... | collective-permute-start | bytes 49160 | tf_op jit(solution)/shard_map/ppermute | solution.py:812
  50.0 16.5 %collective-permute-start.5 = (f32[4,8,128]{2,1,0:T(8,128)S(1)}, f32[4,8,128]{2,1,0:T(8,128)S(1)}, u32[]{:S(2)}, u32[]{:S(2)}) collective-permute-start(f32[4,8,128]{2,1,0:T(8,128)S(1)} %copy-done.16), channel_id=1, source_target_pairs={{0,1},{1,2},{2,3},{3,4},{4,5},{5,6},{6,7},{7,0},{8,9},{9,10},{10,1... | collective-permute-start | bytes 49160 | tf_op jit(solution)/shard_map/ppermute | solution.py:813
  76.1 5.3 %copy-start.8 = (f32[4,512,128]{2,1,0:T(8,128)S(1)}, f32[4,512,128]{2,1,0:T(8,128)}, u32[]{:S(2)}) copy-start(f32[4,512,128]{2,1,0:T(8,128)} %get-tuple-element.60) | copy-start | bytes 3145732
  76.1 5.3 %copy-start.10 = (f32[512,128]{1,0:T(8,128)S(1)}, f32[512,128]{1,0:T(8,128)}, u32[]{:S(2)}) copy-start(f32[512,128]{1,0:T(8,128)} %get-tuple-element.61) | copy-start | bytes 786436
  76.1 5.3 %copy-start.12 = (s32[4]{0:T(128)S(1)}, s32[4]{0:T(128)}, u32[]{:S(2)}) copy-start(s32[4]{0:T(128)} %copy-done.11) | copy-start | bytes 52
  76.2 11.5 %copy-start.7 = (bf16[1024,512]{1,0:T(8,128)(2,1)S(1)}, bf16[1024,512]{1,0:T(8,128)(2,1)}, u32[]{:S(2)}) copy-start(bf16[1024,512]{1,0:T(8,128)(2,1)} %constant.30.clone.table_high) | copy-start | bytes 3145732
  76.2 23.2 %all-to-all-start.2 = ((f32[32,72,128]{2,1,0:T(8,128)}), f32[32,72,128]{2,1,0:T(8,128)}, u32[]{:S(2)}, u32[]{:S(2)}) async-start(f32[32,72,128]{2,1,0:T(8,128)} %get-tuple-element.74), calls=%async_computation.2 | async-start | bytes 2359296 | tf_op jit(solution)/shard_map/all_to_all | solution.py:835
  81.4 6.3 %copy-start.6 = (bf16[1024,512]{1,0:T(8,128)(2,1)S(1)}, bf16[1024,512]{1,0:T(8,128)(2,1)}, u32[]{:S(2)}) copy-start(bf16[1024,512]{1,0:T(8,128)(2,1)} %constant.31.clone.table_low) | copy-start | bytes 3145732
  81.4 0.8 copy-start.15
  86.1 7.3 %copy-start.5 = (f32[4,64,8,128]{3,2,1,0:T(8,128)}, f32[4,64,8,128]{3,2,1,0:T(8,128)S(1)}, u32[]{:S(2)}) copy-start(f32[4,64,8,128]{3,2,1,0:T(8,128)S(1)} %get-tuple-element.86.star.star_far) | copy-start | bytes 3145732
  86.1 7.3 %collective-permute-start.6 = (f32[33,8,128]{2,1,0:T(8,128)S(1)}, f32[33,8,128]{2,1,0:T(8,128)S(1)}, u32[]{:S(2)}, u32[]{:S(2)}) collective-permute-start(f32[33,8,128]{2,1,0:T(8,128)S(1)} %get-tuple-element.82), channel_id=1, source_target_pairs={{0,7},{1,0},{2,1},{3,2},{4,3},{5,4},{6,5},{7,6},{8,15},{9,8},{10,9... | collective-permute-start | bytes 405512 | tf_op jit(solution)/shard_map/ppermute | solution.py:841
  86.2 7.2 %collective-permute-start.7 = (f32[33,8,128]{2,1,0:T(8,128)S(1)}, f32[33,8,128]{2,1,0:T(8,128)S(1)}, u32[]{:S(2)}, u32[]{:S(2)}) collective-permute-start(f32[33,8,128]{2,1,0:T(8,128)S(1)} %get-tuple-element.83), channel_id=1, source_target_pairs={{0,1},{1,2},{2,3},{3,4},{4,5},{5,6},{6,7},{7,0},{8,9},{9,10},{10,1... | collective-permute-start | bytes 405512 | tf_op jit(solution)/shard_map/ppermute | solution.py:842
  95.7 0.8 copy-start.9
  96.5 0.6 copy-start.14
  99.4 31.3 %all-to-all-start.3 = ((f32[8,256,128]{2,1,0:T(8,128)}), f32[8,256,128]{2,1,0:T(8,128)}, u32[]{:S(2)}, u32[]{:S(2)}) async-start(f32[8,256,128]{2,1,0:T(8,128)} %shard_map.119), calls=%async_computation.3 | async-start | bytes 2097152 | tf_op jit(solution)/shard_map/all_to_all | solution.py:853
  103.6 9.7 %collective-permute-start.8 = (f32[49,8,256]{2,1,0:T(8,128)S(1)}, f32[49,8,256]{2,1,0:T(8,128)}, u32[]{:S(2)}, u32[]{:S(2)}) collective-permute-start(f32[49,8,256]{2,1,0:T(8,128)S(1)} %get-tuple-element.96), channel_id=1, source_target_pairs={{128,0},{8,128},{136,8},{16,136},{144,16},{24,144},{152,24},{32,15... | collective-permute-start | bytes 1204232 | tf_op jit(solution)/shard_map/ppermute | solution.py:855
  106.7 7.2 %collective-permute-start.9 = (f32[49,8,256]{2,1,0:T(8,128)S(1)}, f32[49,8,256]{2,1,0:T(8,128)}, u32[]{:S(2)}, u32[]{:S(2)}) collective-permute-start(f32[49,8,256]{2,1,0:T(8,128)S(1)} %get-tuple-element.97), channel_id=1, source_target_pairs={{0,128},{128,8},{8,136},{136,16},{16,144},{144,24},{24,152},{152,3... | collective-permute-start | bytes 1204232 | tf_op jit(solution)/shard_map/ppermute | solution.py:856
  130.6 8.4 %copy-start.13 = (s32[4]{0:T(128)S(1)}, s32[4]{0:T(128)}, u32[]{:S(2)}) copy-start(s32[4]{0:T(128)} %copy-done.11) | copy-start | bytes 52
  133.8 5.2 %collective-permute-start.10 = (f32[4,8,64,128]{3,2,1,0:T(8,128)}, f32[4,8,64,128]{3,2,1,0:T(8,128)S(1)}, u32[]{:S(2)}, u32[]{:S(2)}) collective-permute-start(f32[4,8,64,128]{3,2,1,0:T(8,128)} %get-tuple-element.109), channel_id=1, source_target_pairs={{0,128},{128,0},{1,129},{129,1},{2,130},{130,2},{3,131},{131,3},{4... | collective-permute-start | bytes 3145736 | tf_op jit(solution)/shard_map/ppermute | solution.py:882

commit v5 on v4

--- a/solution.py
+++ b/solution.py
@@ -332,29 +332,41 @@
 def base_kernel(place, own, got, xback_far, base_far, row_far, half, xback, rim, base, row, sem):
     loads = run_all(
         [
-            pltpu.make_async_copy(xback_far.at[:, pl.ds(0, HALF)], xback, sem.at[1]),
-            pltpu.make_async_copy(xback_far.at[NX // 2 // BX, pl.ds(HALF, 8)], rim, sem.at[2]),
+            pltpu.make_async_copy(
+                xback_far.at[pl.ds(8 * k, 8), pl.ds(0, HALF)],
+                xback.at[pl.ds(8 * k, 8)],
+                sem.at[1 + k],
+            )
+            for k in range(4)
         ]
     )
+    (last,) = run_all(
+        [pltpu.make_async_copy(xback_far.at[NX // 2 // BX, pl.ds(HALF, 8)], rim, sem.at[5])]
+    )
     load_half(place, own, got, half, sem.at[0])
-    wait_all(loads)
+    lane = lane_index((HALF, BY))
+    stores = []
+    for k in range(4):
+        loads[k].wait()
+        for z in (2 * k, 2 * k + 1):
+            w = 0.1 * half[2, z]
+            for c in range(4):
+                total = None
+                for part in range(4):
+                    shift = 32 * ((part - c) % 4)
+                    tile = xback[4 * z + part]
+                    moved = tile if shift == 0 else pltpu.roll(tile, shift, 1)
+                    total = moved if total is None else jnp.where(lane >= 32 * part, moved, total)
+                q = half[c, z]
+                upper = half[c, min(z + 1, NZ - 1)]
+                lower = half[c, max(z - 1, 0)]
+                mixed = 0.02 * (upper + lower - 2.0 * q) - w * (upper - lower)
+                base[z, c * HALF : (c + 1) * HALF] = q + total + mixed
+        at = pl.ds(2 * k, 2)
+        stores += run_all([pltpu.make_async_copy(base.at[at], base_far.at[at], sem.at[7 + k])])
+    last.wait()
     row[...] = rim[:1]
-    stores = run_all([pltpu.make_async_copy(row, row_far, sem.at[3])])
-    lane = lane_index((HALF, BY))
-    for z in range(NZ):
-        for c in range(4):
-            total = None
-            for part in range(4):
-                shift = 32 * ((part - c) % 4)
-                tile = xback[4 * z + part]
-                moved = tile if shift == 0 else pltpu.roll(tile, shift, 1)
-                total = moved if total is None else jnp.where(lane >= 32 * part, moved, total)
-            q = half[c, z]
-            upper = half[c, min(z + 1, NZ - 1)]
-            lower = half[c, max(z - 1, 0)]
-            mixed = 0.02 * (upper + lower - 2.0 * q) - 0.1 * half[2, z] * (upper - lower)
-            base[z, c * HALF : (c + 1) * HALF] = q + total + mixed
-    stores += run_all([pltpu.make_async_copy(base, base_far, sem.at[4])])
+    stores += run_all([pltpu.make_async_copy(row, row_far, sem.at[6])])
     wait_all(stores)
 
 
@@ -858,7 +870,7 @@
         base_kernel,
         3,
         [(GY, 4 * HALF, BY), (1, BY)],
-        vmem(half_block, (32, HALF, BY), (8, BY), (GY, 4 * HALF, BY), (1, BY)) + [dma((5,))],
+        vmem(half_block, (32, HALF, BY), (8, BY), (GY, 4 * HALF, BY), (1, BY)) + [dma((11,))],
     )(place, own, got, xback)
     base, from_e, from_w = in_step(base, from_e, from_w)
     joined, send = raw_call(

time: 142 us -> 142 us (level)
  no operation moved by 1% of the time
where the time goes in v5:
time: 142 us; the launch traced here: 141 us
  Pallas kernels  54.5 us (38%)
  starting transfers between devices  44.8 us (32%)
  waiting for transfers between devices  34.4 us (24%)
  local copies, waits for them, and re-layouts  5.84 us (4%)
    pallas_call x1, Pallas kernels, on_device(): raw_call(pressure_kernel, 5, [(4, NZ, BX, BY), half_block], vmem(block, (...  14.9 us
    pallas_call x6, Pallas kernels, call(): pl.pallas_call(body, out_shape=[jax.ShapeDtypeStruct(shape, F32) for shap...  14.6 us
    all_to_all x1, waiting for transfers between devices, on_device(): xin = lax.all_to_all(packed, x_axes, 0, 0, tiled=True)  10.2 us
    pallas_call x1, Pallas kernels, on_device(): staged_call(line_kernel, ins, [(32, 72, BY)], scratch=[pltpu.VMEM((NX //...  8.79 us
    ppermute x1, waiting for transfers between devices, on_device(): ghost_n = lax.ppermute(col_low, 'gy', along_y(-1))  7.71 us
    all_to_all x1, starting transfers between devices, on_device(): yin = lax.all_to_all(ybuf, 'gy', 0, 0, tiled=True)  7.13 us
    all_to_all x1, waiting for transfers between devices, on_device(): yin = lax.all_to_all(ybuf, 'gy', 0, 0, tiled=True)  7.13 us
    unnamed x40, local copies, waits for them, and re-layouts  5.84 us
  transfers between devices with their start and end apart: 15, of which 9 were waited for; matrix products, arithmetic and copies ran while one was open for 0% of the time, Pallas kernels for 33%

profile of v5, /device:TPU:1, one launch (start us, length us, event | category | flops | bytes accessed | tf_op | source)
XLA Modules:
  0.0 140.7 jit_solution(6244416433630534692)
XLA Ops:
  0.6 0.1 pad_add_fusion.place
  0.7 1.6 %copy-done = f32[1,4,8,128,128]{4,3,2,1,0:T(8,128)S(1)} copy-done((f32[1,4,8,128,128]{4,3,2,1,0:T(8,128)S(1)}, f32[1,4,8,128,128]{4,3,2,1,0:T(8,128)}, u32[]{:S(2)}) %copy-start) | copy-done | bytes 2097176
  2.3 0.6 shard_map.113
  3.0 3.3 %collective-permute-start = (f32[4,8,64,128]{3,2,1,0:T(8,128)S(1)}, f32[4,8,64,128]{3,2,1,0:T(8,128)S(1)}, u32[]{:S(2)}, u32[]{:S(2)}) collective-permute-start(f32[4,8,64,128]{3,2,1,0:T(8,128)S(1)} %get-tuple-element.57), channel_id=1, source_target_pairs={{0,128},{128,0},{1,129},{129,1},{2,130},{130,2},{3,131},{131,3},{4... | collective-permute-start | bytes 3145736 | tf_op jit(solution)/shard_map/ppermute | solution.py:801
  6.3 1.3 collective-permute-start.1
  7.6 1.0 collective-permute-done.got
  8.6 1.4 %shard_map.114 = f32[32,64,128]{2,1,0:T(8,128)S(1)} custom-call(s32[4]{0:T(128)S(1)} %pad_add_fusion.place, f32[4,8,128,128]{3,2,1,0:T(8,128)S(1)} %bitcast.14, f32[4,8,64,128]{3,2,1,0:T(8,128)S(1)} %collective-permute-done.got), custom_call_target="tpu_custom_call" | custom-call | tf_op jit(solution)/shard_map/pallas_call | solution.py:137
  10.0 1.0 copy-done.4
  11.0 1.2 collective-permute-done.1.column
  12.3 5.5 %all-to-all-start.1 = ((f32[32,64,128]{2,1,0:T(8,128)}), f32[32,64,128]{2,1,0:T(8,128)}, u32[]{:S(2)}, u32[]{:S(2)}) async-start(f32[32,64,128]{2,1,0:T(8,128)} %copy-done.4), calls=%async_computation.1 | async-start | bytes 2097152 | tf_op jit(solution)/shard_map/all_to_all | solution.py:804
  17.8 0.6 shard_map.115
  18.5 0.0 copy-start.3
  18.5 1.0 copy-done.3
  19.5 4.8 %shard_map.116 = (f32[4,512,128]{2,1,0:T(8,128)}, f32[512,128]{1,0:T(8,128)}, f32[4,8,128]{2,1,0:T(8,128)}, f32[4,8,128]{2,1,0:T(8,128)}, f32[4,8,128]{2,1,0:T(8,128)}, /*index=5*/f32[4,8,128]{2,1,0:T(8,128)}) custom-call(s32[4]{0:T(128)} %copy-done.11, f32[4,8,128,128]{3,2,1,0:T(8,128)} %bitcast.11, f32[4,8,64,128]{3,2,1,0:T(8,128)} %copy-done.2, ...), custom_call_target="tpu_custom_call" | custom-call | tf_op jit(solution)/shard_map/pallas_call | solution.py:806
  24.3 10.2 %all-to-all-done.1.refs_0_ = f32[32,64,128]{2,1,0:T(8,128)} async-done(((f32[32,64,128]{2,1,0:T(8,128)}), f32[32,64,128]{2,1,0:T(8,128)}, u32[]{:S(2)}, u32[]{:S(2)}) %all-to-all-start.1) | async-done | bytes 1048608 | tf_op jit(solution)/shard_map/all_to_all | solution.py:804
  34.5 7.1 %all-to-all-start = ((f32[8,288,128]{2,1,0:T(8,128)}), f32[8,288,128]{2,1,0:T(8,128)}, u32[]{:S(2)}, u32[]{:S(2)}) async-start(f32[8,288,128]{2,1,0:T(8,128)} %copy-done.3), calls=%async_computation | async-start | bytes 2359296 | tf_op jit(solution)/shard_map/all_to_all | solution.py:821
  41.6 3.3 %collective-permute-start.2 = (f32[4,8,128]{2,1,0:T(8,128)S(1)}, f32[4,8,128]{2,1,0:T(8,128)S(1)}, u32[]{:S(2)}, u32[]{:S(2)}) collective-permute-start(f32[4,8,128]{2,1,0:T(8,128)S(1)} %copy-done.19), channel_id=1, source_target_pairs={{128,0},{8,128},{136,8},{16,136},{144,16},{24,144},{152,24},{32,15... | collective-permute-start | bytes 49160 | tf_op jit(solution)/shard_map/ppermute | solution.py:822
  45.0 2.2 %collective-permute-start.3 = (f32[4,8,128]{2,1,0:T(8,128)S(1)}, f32[4,8,128]{2,1,0:T(8,128)S(1)}, u32[]{:S(2)}, u32[]{:S(2)}) collective-permute-start(f32[4,8,128]{2,1,0:T(8,128)S(1)} %copy-done.18), channel_id=1, source_target_pairs={{0,128},{128,8},{8,136},{136,16},{16,144},{144,24},{24,152},{152,3... | collective-permute-start | bytes 49160 | tf_op jit(solution)/shard_map/ppermute | solution.py:823
  47.2 2.7 %collective-permute-start.4 = (f32[4,8,128]{2,1,0:T(8,128)S(1)}, f32[4,8,128]{2,1,0:T(8,128)S(1)}, u32[]{:S(2)}, u32[]{:S(2)}) collective-permute-start(f32[4,8,128]{2,1,0:T(8,128)S(1)} %copy-done.17), channel_id=1, source_target_pairs={{0,7},{1,0},{2,1},{3,2},{4,3},{5,4},{6,5},{7,6},{8,15},{9,8},{10,9... | collective-permute-start | bytes 49160 | tf_op jit(solution)/shard_map/ppermute | solution.py:824
  50.0 8.8 %shard_map.117.xbuf_in = f32[32,72,128]{2,1,0:T(8,128)} custom-call(s32[4]{0:T(128)} %copy-done.11, f32[32,64,128]{2,1,0:T(8,128)} %all-to-all-done.1.refs_0_, bf16[512,1024]{1,0:T(8,128)(2,1)} %constant.32.clone.refs_1_, bf16[512,1024]{1,0:T(8,128)(2,1)} %constant.33.clone.refs_2_, bf16[512,1024]{1,0:T(8,128)(2,1)} %constant.34.clone.refs_3_, ...), custom_call_target="tpu_custom_call" | custom-call | tf_op jit(solution)/shard_map/pallas_call | solution.py:827
  58.8 0.0 collective-permute-done.3.ghost_w
  58.8 7.7 %collective-permute-done.4.ghost_n = f32[4,8,128]{2,1,0:T(8,128)S(1)} collective-permute-done((f32[4,8,128]{2,1,0:T(8,128)S(1)}, f32[4,8,128]{2,1,0:T(8,128)S(1)}, u32[]{:S(2)}, u32[]{:S(2)}) %collective-permute-start.4) | collective-permute-done | bytes 16416 | tf_op jit(solution)/shard_map/ppermute | solution.py:824
  66.5 7.1 %all-to-all-done.yin = f32[8,288,128]{2,1,0:T(8,128)} async-done(((f32[8,288,128]{2,1,0:T(8,128)}), f32[8,288,128]{2,1,0:T(8,128)}, u32[]{:S(2)}, u32[]{:S(2)}) %all-to-all-start) | async-done | bytes 1179680 | tf_op jit(solution)/shard_map/all_to_all | solution.py:821
  73.6 2.5 %shard_map.118 = (f32[32,72,128]{2,1,0:T(8,128)}, f32[32,128]{1,0:T(8,128)}) custom-call(s32[4]{0:T(128)} %copy-done.11, f32[8,288,128]{2,1,0:T(8,128)} %all-to-all-done.yin, s32[1,128]{1,0:T(1,128)} %bitcast.20, s32[1,128]{1,0:T(1,128)} %bitcast.21, f32[32,72,128]{2,1,0:T(8,128)} %shard_map.117.xbuf_in), custom_call_target="tpu_custom_call", output_to_operand_aliasing={{0}: (4, {})} | custom-call | tf_op jit(solution)/shard_map/pallas_call | solution.py:837
  76.2 0.0 copy-start.7
  76.2 5.2 %all-to-all-start.2 = ((f32[32,72,128]{2,1,0:T(8,128)}), f32[32,72,128]{2,1,0:T(8,128)}, u32[]{:S(2)}, u32[]{:S(2)}) async-start(f32[32,72,128]{2,1,0:T(8,128)} %get-tuple-element.74), calls=%async_computation.2 | async-start | bytes 2359296 | tf_op jit(solution)/shard_map/all_to_all | solution.py:847
  81.4 0.0 copy-start.6
  81.4 0.0 copy-start.15
  81.4 0.8 copy-done.15
  82.2 3.9 %shard_map.120 = (f32[4,64,8,128]{3,2,1,0:T(8,128)S(1)}, f32[64,8,128]{2,1,0:T(8,128)S(1)}, f32[33,8,128]{2,1,0:T(8,128)S(1)}, f32[33,8,128]{2,1,0:T(8,128)S(1)}) custom-call(s32[4]{0:T(128)S(1)} %copy-done.12, f32[4,64,8,128]{3,2,1,0:T(8,128)S(1)} %bitcast.16, f32[64,8,128]{2,1,0:T(8,128)S(1)} %bitcast.17, f32[4,8,128]{2,1,0:T(8,128)S(1)} %collective-permute-done.3.ghost_w, ...), custom_call_target="tpu_custom_call" | custom-call | tf_op jit(solution)/shard_map/pallas_call | solution.py:137
  86.1 0.1 collective-permute-start.6
  86.2 1.5 %collective-permute-start.7 = (f32[33,8,128]{2,1,0:T(8,128)S(1)}, f32[33,8,128]{2,1,0:T(8,128)S(1)}, u32[]{:S(2)}, u32[]{:S(2)}) collective-permute-start(f32[33,8,128]{2,1,0:T(8,128)S(1)} %get-tuple-element.83), channel_id=1, source_target_pairs={{0,1},{1,2},{2,3},{3,4},{4,5},{5,6},{6,7},{7,0},{8,9},{9,10},{10,1... | collective-permute-start | bytes 405512 | tf_op jit(solution)/shard_map/ppermute | solution.py:854
  87.7 5.7 %shard_map.119 = f32[8,256,128]{2,1,0:T(8,128)} custom-call(s32[4]{0:T(128)S(1)} %copy-done.12, f32[8,288,128]{2,1,0:T(8,128)} %all-to-all-done.yin, bf16[1024,512]{1,0:T(8,128)(2,1)S(1)} %copy-done.7, bf16[1024,512]{1,0:T(8,128)(2,1)S(1)} %copy-done.6), custom_call_target="tpu_custom_call" | custom-call | tf_op jit(solution)/shard_map/pallas_call | solution.py:137
  93.4 2.3 %shard_map.121 = (f32[64,8,256]{2,1,0:T(8,128)S(1)}, f32[2,8,256]{2,1,0:T(8,128)S(1)}, f32[49,8,256]{2,1,0:T(8,128)S(1)}, f32[49,8,256]{2,1,0:T(8,128)S(1)}) custom-call(s32[4]{0:T(128)S(1)} %copy-done.12, f32[64,8,128]{2,1,0:T(8,128)S(1)} %get-tuple-element.85.partial, f32[4,64,8,128]{3,2,1,0:T(8,128)S(1)} %get-tuple-element.86.star.star_far, ...), custom_call_target="tpu_custom_call" | custom-call | tf_op jit(solution)/shard_map/pallas_call | solution.py:137
  95.7 0.8 copy-done.9
  96.5 0.6 copy-done.14
  97.1 2.3 %all-to-all-done.2.xback_far = f32[32,72,128]{2,1,0:T(8,128)} async-done(((f32[32,72,128]{2,1,0:T(8,128)}), f32[32,72,128]{2,1,0:T(8,128)}, u32[]{:S(2)}, u32[]{:S(2)}) %all-to-all-start.2) | async-done | bytes 1179680 | tf_op jit(solution)/shard_map/all_to_all | solution.py:847
  99.4 4.2 %all-to-all-start.3 = ((f32[8,256,128]{2,1,0:T(8,128)}), f32[8,256,128]{2,1,0:T(8,128)}, u32[]{:S(2)}, u32[]{:S(2)}) async-start(f32[8,256,128]{2,1,0:T(8,128)} %shard_map.119), calls=%async_computation.3 | async-start | bytes 2097152 | tf_op jit(solution)/shard_map/all_to_all | solution.py:865
  103.6 3.1 %collective-permute-start.8 = (f32[49,8,256]{2,1,0:T(8,128)S(1)}, f32[49,8,256]{2,1,0:T(8,128)}, u32[]{:S(2)}, u32[]{:S(2)}) collective-permute-start(f32[49,8,256]{2,1,0:T(8,128)S(1)} %get-tuple-element.96), channel_id=1, source_target_pairs={{128,0},{8,128},{136,8},{16,136},{144,16},{24,144},{152,24},{32,15... | collective-permute-start | bytes 1204232 | tf_op jit(solution)/shard_map/ppermute | solution.py:867
  106.7 2.5 %collective-permute-start.9 = (f32[49,8,256]{2,1,0:T(8,128)S(1)}, f32[49,8,256]{2,1,0:T(8,128)}, u32[]{:S(2)}, u32[]{:S(2)}) collective-permute-start(f32[49,8,256]{2,1,0:T(8,128)S(1)} %get-tuple-element.97), channel_id=1, source_target_pairs={{0,128},{128,8},{8,136},{136,16},{16,144},{144,24},{24,152},{152,3... | collective-permute-start | bytes 1204232 | tf_op jit(solution)/shard_map/ppermute | solution.py:868
  109.2 4.1 %shard_map.122 = (f32[8,256,128]{2,1,0:T(8,128)}, f32[1,128]{1,0:T(1,128)}) custom-call(s32[4]{0:T(128)} %copy-done.11, f32[4,8,128,128]{3,2,1,0:T(8,128)} %bitcast.12, f32[4,8,64,128]{3,2,1,0:T(8,128)} %copy-done.2, f32[32,72,128]{2,1,0:T(8,128)} %all-to-all-done.2.xback_far), custom_call_target="tpu_custom_call" | custom-call | tf_op jit(solution)/shard_map/pallas_call | solution.py:869
  113.4 0.6 collective-permute-done.9.from_w_far
  114.0 14.9 %shard_map.123 = (f32[4,8,128,128]{3,2,1,0:T(8,128)}, f32[4,8,64,128]{3,2,1,0:T(8,128)}) custom-call(s32[4]{0:T(128)} %copy-done.11, f32[64,8,256]{2,1,0:T(8,128)} %copy-done.9, f32[4,64,8,128]{3,2,1,0:T(8,128)} %copy-done.5, f32[2,8,256]{2,1,0:T(8,128)} %copy-done.14, f32[49,8,256]{2,1,0:T(8,128)} %collective-permute-done.9.from_w_far, ...), custom_call_target="tpu_custom_call" | custom-call | tf_op jit(solution)/shard_map/pallas_call | solution.py:876
  128.9 1.7 %all-to-all-done.3.yback_far = f32[8,256,128]{2,1,0:T(8,128)} async-done(((f32[8,256,128]{2,1,0:T(8,128)}), f32[8,256,128]{2,1,0:T(8,128)}, u32[]{:S(2)}, u32[]{:S(2)}) %all-to-all-start.3) | async-done | bytes 1048608 | tf_op jit(solution)/shard_map/all_to_all | solution.py:865
  130.6 3.2 %shard_map.124 = (f32[4,8,128,128]{3,2,1,0:T(8,128)}, f32[4,8,64,128]{3,2,1,0:T(8,128)}) custom-call(s32[4]{0:T(128)} %copy-done.11, f32[8,256,128]{2,1,0:T(8,128)} %get-tuple-element.105.base_far, f32[8,256,128]{2,1,0:T(8,128)} %all-to-all-done.3.yback_far, ...), custom_call_target="tpu_custom_call", output_to_operand_aliasing={{0}: (3, {}), {1}: (4, {})} | custom-call | tf_op jit(solution)/shard_map/pallas_call | solution.py:887
  133.8 2.7 %collective-permute-start.10 = (f32[4,8,64,128]{3,2,1,0:T(8,128)}, f32[4,8,64,128]{3,2,1,0:T(8,128)S(1)}, u32[]{:S(2)}, u32[]{:S(2)}) collective-permute-start(f32[4,8,64,128]{3,2,1,0:T(8,128)} %get-tuple-element.109), channel_id=1, source_target_pairs={{0,128},{128,0},{1,129},{129,1},{2,130},{130,2},{3,131},{131,3},{4... | collective-permute-start | bytes 3145736 | tf_op jit(solution)/shard_map/ppermute | solution.py:894
  136.5 2.5 %collective-permute-done.10.theirs = f32[4,8,64,128]{3,2,1,0:T(8,128)S(1)} collective-permute-done((f32[4,8,64,128]{3,2,1,0:T(8,128)}, f32[4,8,64,128]{3,2,1,0:T(8,128)S(1)}, u32[]{:S(2)}, u32[]{:S(2)}) %collective-permute-start.10) | collective-permute-done | bytes 1048608 | tf_op jit(solution)/shard_map/ppermute | solution.py:894
  139.0 1.5 %shard_map.125 = f32[4,8,128,128]{3,2,1,0:T(8,128)} custom-call(s32[4]{0:T(128)S(1)} %copy-done.13, f32[4,8,64,128]{3,2,1,0:T(8,128)S(1)} %collective-permute-done.10.theirs, f32[4,8,128,128]{3,2,1,0:T(8,128)} %get-tuple-element.110.joined_in), custom_call_target="tpu_custom_call", output_to_operand_aliasing={{}: (2, {})} | custom-call | tf_op jit(solution)/shard_map/pallas_call | solution.py:895
  (36 shorter events, 0.1 us)
Async XLA Ops:
  0.7 17.1 %copy-start.11 = (s32[4]{0:T(128)}, s32[4]{0:T(128)S(1)}, u32[]{:S(2)}) copy-start(s32[4]{0:T(128)S(1)} %pad_add_fusion.place) | copy-start | bytes 52
  0.7 1.6 %copy-start = (f32[1,4,8,128,128]{4,3,2,1,0:T(8,128)S(1)}, f32[1,4,8,128,128]{4,3,2,1,0:T(8,128)}, u32[]{:S(2)}) copy-start(f32[1,4,8,128,128]{4,3,2,1,0:T(8,128)} %param.10) | copy-start | bytes 6291460
  2.3 6.3 %copy-start.1 = (f32[1,4,8,128,128]{4,3,2,1,0:T(8,128)S(1)}, f32[1,4,8,128,128]{4,3,2,1,0:T(8,128)}, u32[]{:S(2)}) copy-start(f32[1,4,8,128,128]{4,3,2,1,0:T(8,128)} %param.10) | copy-start | bytes 6291460
  3.0 5.6 %collective-permute-start = (f32[4,8,64,128]{3,2,1,0:T(8,128)S(1)}, f32[4,8,64,128]{3,2,1,0:T(8,128)S(1)}, u32[]{:S(2)}, u32[]{:S(2)}) collective-permute-start(f32[4,8,64,128]{3,2,1,0:T(8,128)S(1)} %get-tuple-element.57), channel_id=1, source_target_pairs={{0,128},{128,0},{1,129},{129,1},{2,130},{130,2},{3,131},{131,3},{4... | collective-permute-start | bytes 3145736 | tf_op jit(solution)/shard_map/ppermute | solution.py:801
  6.3 6.0 %collective-permute-start.1 = (f32[4,8,128]{2,1,0:T(8,128)S(1)}, f32[4,8,128]{2,1,0:T(8,128)S(1)}, u32[]{:S(2)}, u32[]{:S(2)}) collective-permute-start(f32[4,8,128]{2,1,0:T(8,128)S(1)} %get-tuple-element.58), channel_id=1, source_target_pairs={{64,0},{65,1},{66,2},{67,3},{68,4},{69,5},{70,6},{71,7},{192,128},... | collective-permute-start | bytes 49160 | tf_op jit(solution)/shard_map/ppermute | solution.py:800
  8.6 9.2 %copy-start.2 = (f32[4,8,64,128]{3,2,1,0:T(8,128)}, f32[4,8,64,128]{3,2,1,0:T(8,128)S(1)}, u32[]{:S(2)}) copy-start(f32[4,8,64,128]{3,2,1,0:T(8,128)S(1)} %collective-permute-done.got) | copy-start | bytes 3145732
  10.0 1.0 copy-start.4
  12.3 22.2 %all-to-all-start.1 = ((f32[32,64,128]{2,1,0:T(8,128)}), f32[32,64,128]{2,1,0:T(8,128)}, u32[]{:S(2)}, u32[]{:S(2)}) async-start(f32[32,64,128]{2,1,0:T(8,128)} %copy-done.4), calls=%async_computation.1 | async-start | bytes 2097152 | tf_op jit(solution)/shard_map/all_to_all | solution.py:804
  18.5 1.0 copy-start.3
  24.3 17.4 %copy-start.19 = (f32[4,8,128]{2,1,0:T(8,128)S(1)}, f32[4,8,128]{2,1,0:T(8,128)}, u32[]{:S(2)}) copy-start(f32[4,8,128]{2,1,0:T(8,128)} %get-tuple-element.68) | copy-start | bytes 49156
  24.3 20.7 %copy-start.18 = (f32[4,8,128]{2,1,0:T(8,128)S(1)}, f32[4,8,128]{2,1,0:T(8,128)}, u32[]{:S(2)}) copy-start(f32[4,8,128]{2,1,0:T(8,128)} %get-tuple-element.69) | copy-start | bytes 49156
  24.3 22.9 %copy-start.17 = (f32[4,8,128]{2,1,0:T(8,128)S(1)}, f32[4,8,128]{2,1,0:T(8,128)}, u32[]{:S(2)}) copy-start(f32[4,8,128]{2,1,0:T(8,128)} %get-tuple-element.70) | copy-start | bytes 49156
  24.3 25.7 %copy-start.16 = (f32[4,8,128]{2,1,0:T(8,128)S(1)}, f32[4,8,128]{2,1,0:T(8,128)}, u32[]{:S(2)}) copy-start(f32[4,8,128]{2,1,0:T(8,128)} %get-tuple-element.71) | copy-start | bytes 49156
  34.5 39.1 %all-to-all-start = ((f32[8,288,128]{2,1,0:T(8,128)}), f32[8,288,128]{2,1,0:T(8,128)}, u32[]{:S(2)}, u32[]{:S(2)}) async-start(f32[8,288,128]{2,1,0:T(8,128)} %copy-done.3), calls=%async_computation | async-start | bytes 2359296 | tf_op jit(solution)/shard_map/all_to_all | solution.py:821
  41.6 17.1 %collective-permute-start.2 = (f32[4,8,128]{2,1,0:T(8,128)S(1)}, f32[4,8,128]{2,1,0:T(8,128)S(1)}, u32[]{:S(2)}, u32[]{:S(2)}) collective-permute-start(f32[4,8,128]{2,1,0:T(8,128)S(1)} %copy-done.19), channel_id=1, source_target_pairs={{128,0},{8,128},{136,8},{16,136},{144,16},{24,144},{152,24},{32,15... | collective-permute-start | bytes 49160 | tf_op jit(solution)/shard_map/ppermute | solution.py:822
  45.0 13.8 %collective-permute-start.3 = (f32[4,8,128]{2,1,0:T(8,128)S(1)}, f32[4,8,128]{2,1,0:T(8,128)S(1)}, u32[]{:S(2)}, u32[]{:S(2)}) collective-permute-start(f32[4,8,128]{2,1,0:T(8,128)S(1)} %copy-done.18), channel_id=1, source_target_pairs={{0,128},{128,8},{8,136},{136,16},{16,144},{144,24},{24,152},{152,3... | collective-permute-start | bytes 49160 | tf_op jit(solution)/shard_map/ppermute | solution.py:823
  47.2 19.3 %collective-permute-start.4 = (f32[4,8,128]{2,1,0:T(8,128)S(1)}, f32[4,8,128]{2,1,0:T(8,128)S(1)}, u32[]{:S(2)}, u32[]{:S(2)}) collective-permute-start(f32[4,8,128]{2,1,0:T(8,128)S(1)} %copy-done.17), channel_id=1, source_target_pairs={{0,7},{1,0},{2,1},{3,2},{4,3},{5,4},{6,5},{7,6},{8,15},{9,8},{10,9... | collective-permute-start | bytes 49160 | tf_op jit(solution)/shard_map/ppermute | solution.py:824
  50.0 16.5 %collective-permute-start.5 = (f32[4,8,128]{2,1,0:T(8,128)S(1)}, f32[4,8,128]{2,1,0:T(8,128)S(1)}, u32[]{:S(2)}, u32[]{:S(2)}) collective-permute-start(f32[4,8,128]{2,1,0:T(8,128)S(1)} %copy-done.16), channel_id=1, source_target_pairs={{0,1},{1,2},{2,3},{3,4},{4,5},{5,6},{6,7},{7,0},{8,9},{9,10},{10,1... | collective-permute-start | bytes 49160 | tf_op jit(solution)/shard_map/ppermute | solution.py:825
  76.1 5.3 %copy-start.8 = (f32[4,512,128]{2,1,0:T(8,128)S(1)}, f32[4,512,128]{2,1,0:T(8,128)}, u32[]{:S(2)}) copy-start(f32[4,512,128]{2,1,0:T(8,128)} %get-tuple-element.60) | copy-start | bytes 3145732
  76.1 5.3 %copy-start.10 = (f32[512,128]{1,0:T(8,128)S(1)}, f32[512,128]{1,0:T(8,128)}, u32[]{:S(2)}) copy-start(f32[512,128]{1,0:T(8,128)} %get-tuple-element.61) | copy-start | bytes 786436
  76.1 5.3 %copy-start.12 = (s32[4]{0:T(128)S(1)}, s32[4]{0:T(128)}, u32[]{:S(2)}) copy-start(s32[4]{0:T(128)} %copy-done.11) | copy-start | bytes 52
  76.2 11.5 %copy-start.7 = (bf16[1024,512]{1,0:T(8,128)(2,1)S(1)}, bf16[1024,512]{1,0:T(8,128)(2,1)}, u32[]{:S(2)}) copy-start(bf16[1024,512]{1,0:T(8,128)(2,1)} %constant.30.clone.table_high) | copy-start | bytes 3145732
  76.2 23.2 %all-to-all-start.2 = ((f32[32,72,128]{2,1,0:T(8,128)}), f32[32,72,128]{2,1,0:T(8,128)}, u32[]{:S(2)}, u32[]{:S(2)}) async-start(f32[32,72,128]{2,1,0:T(8,128)} %get-tuple-element.74), calls=%async_computation.2 | async-start | bytes 2359296 | tf_op jit(solution)/shard_map/all_to_all | solution.py:847
  81.4 6.3 %copy-start.6 = (bf16[1024,512]{1,0:T(8,128)(2,1)S(1)}, bf16[1024,512]{1,0:T(8,128)(2,1)}, u32[]{:S(2)}) copy-start(bf16[1024,512]{1,0:T(8,128)(2,1)} %constant.31.clone.table_low) | copy-start | bytes 3145732
  81.4 0.8 copy-start.15
  86.1 7.3 %copy-start.5 = (f32[4,64,8,128]{3,2,1,0:T(8,128)}, f32[4,64,8,128]{3,2,1,0:T(8,128)S(1)}, u32[]{:S(2)}) copy-start(f32[4,64,8,128]{3,2,1,0:T(8,128)S(1)} %get-tuple-element.86.star.star_far) | copy-start | bytes 3145732
  86.1 7.3 %collective-permute-start.6 = (f32[33,8,128]{2,1,0:T(8,128)S(1)}, f32[33,8,128]{2,1,0:T(8,128)S(1)}, u32[]{:S(2)}, u32[]{:S(2)}) collective-permute-start(f32[33,8,128]{2,1,0:T(8,128)S(1)} %get-tuple-element.82), channel_id=1, source_target_pairs={{0,7},{1,0},{2,1},{3,2},{4,3},{5,4},{6,5},{7,6},{8,15},{9,8},{10,9... | collective-permute-start | bytes 405512 | tf_op jit(solution)/shard_map/ppermute | solution.py:853
  86.2 7.2 %collective-permute-start.7 = (f32[33,8,128]{2,1,0:T(8,128)S(1)}, f32[33,8,128]{2,1,0:T(8,128)S(1)}, u32[]{:S(2)}, u32[]{:S(2)}) collective-permute-start(f32[33,8,128]{2,1,0:T(8,128)S(1)} %get-tuple-element.83), channel_id=1, source_target_pairs={{0,1},{1,2},{2,3},{3,4},{4,5},{5,6},{6,7},{7,0},{8,9},{9,10},{10,1... | collective-permute-start | bytes 405512 | tf_op jit(solution)/shard_map/ppermute | solution.py:854
  95.7 0.8 copy-start.9
  96.5 0.6 copy-start.14
  99.4 31.3 %all-to-all-start.3 = ((f32[8,256,128]{2,1,0:T(8,128)}), f32[8,256,128]{2,1,0:T(8,128)}, u32[]{:S(2)}, u32[]{:S(2)}) async-start(f32[8,256,128]{2,1,0:T(8,128)} %shard_map.119), calls=%async_computation.3 | async-start | bytes 2097152 | tf_op jit(solution)/shard_map/all_to_all | solution.py:865
  103.6 9.7 %collective-permute-start.8 = (f32[49,8,256]{2,1,0:T(8,128)S(1)}, f32[49,8,256]{2,1,0:T(8,128)}, u32[]{:S(2)}, u32[]{:S(2)}) collective-permute-start(f32[49,8,256]{2,1,0:T(8,128)S(1)} %get-tuple-element.96), channel_id=1, source_target_pairs={{128,0},{8,128},{136,8},{16,136},{144,16},{24,144},{152,24},{32,15... | collective-permute-start | bytes 1204232 | tf_op jit(solution)/shard_map/ppermute | solution.py:867
  106.7 7.2 %collective-permute-start.9 = (f32[49,8,256]{2,1,0:T(8,128)S(1)}, f32[49,8,256]{2,1,0:T(8,128)}, u32[]{:S(2)}, u32[]{:S(2)}) collective-permute-start(f32[49,8,256]{2,1,0:T(8,128)S(1)} %get-tuple-element.97), channel_id=1, source_target_pairs={{0,128},{128,8},{8,136},{136,16},{16,144},{144,24},{24,152},{152,3... | collective-permute-start | bytes 1204232 | tf_op jit(solution)/shard_map/ppermute | solution.py:868
  130.6 8.4 %copy-start.13 = (s32[4]{0:T(128)S(1)}, s32[4]{0:T(128)}, u32[]{:S(2)}) copy-start(s32[4]{0:T(128)} %copy-done.11) | copy-start | bytes 52
  133.8 5.2 %collective-permute-start.10 = (f32[4,8,64,128]{3,2,1,0:T(8,128)}, f32[4,8,64,128]{3,2,1,0:T(8,128)S(1)}, u32[]{:S(2)}, u32[]{:S(2)}) collective-permute-start(f32[4,8,64,128]{3,2,1,0:T(8,128)} %get-tuple-element.109), channel_id=1, source_target_pairs={{0,128},{128,0},{1,129},{129,1},{2,130},{130,2},{3,131},{131,3},{4... | collective-permute-start | bytes 3145736 | tf_op jit(solution)/shard_map/ppermute | solution.py:894
